TPU v7x, 32 devices: a whole 2x2x4 slice. The times are simulated.
32 devices in a mesh: section: 4 (over y, x), dp: 8 (over z, core).
Axes of the slice: x: 2, y: 2, z: 4, core: 2. Of those that a mesh axis runs over, the one named last changes fastest.
Arguments:
- stream_in: bfloat16 [3, 2048, 1024], P(None, 'dp'), may hold values from -6 to 6
- segment_ids: int32 [3, 2048], replicated, may hold values from 0 to 7, as said below
- chosen_rows: int32 [3, 256], replicated, may hold values from 0 to 2047, as said below
- cotangent: bfloat16 [3, 2048, 1024], P(None, 'dp'), may hold values from -6 to 6
- dense_prenorm: bfloat16 [1024], P('dp'), may hold values from 0.5 to 1.5
- dense_query: bfloat16 [1024, 1024], P('dp'), may hold values from -0.1875 to 0.1875
- dense_keys: bfloat16 [1024, 1024], P('dp'), may hold values from -0.1875 to 0.1875
- dense_values: bfloat16 [1024, 1024], P('dp'), may hold values from -0.1875 to 0.1875
- dense_output: bfloat16 [1024, 1024], P('dp'), may hold values from -1 to 1
- dense_midnorm: bfloat16 [1024], P('dp'), may hold values from 0.5 to 1.5
- dense_expand: bfloat16 [1024, 4096], P('dp'), may hold values from -0.1875 to 0.1875
- dense_shrink: bfloat16 [4096, 1024], P('dp'), may hold values from -0.09375 to 0.09375
- routed_prenorm: bfloat16 [1024], P('dp'), may hold values from 0.5 to 1.5
- routed_query: bfloat16 [1024, 1024], P('dp'), may hold values from -0.1875 to 0.1875
- routed_keys: bfloat16 [1024, 1024], P('dp'), may hold values from -0.1875 to 0.1875
- routed_values: bfloat16 [1024, 1024], P('dp'), may hold values from -0.1875 to 0.1875
- routed_output: bfloat16 [1024, 1024], P('dp'), may hold values from -0.75 to 0.75
- routed_midnorm: bfloat16 [1024], P('dp'), may hold values from 0.5 to 1.5
- routed_expand: bfloat16 [1024, 4096], P('dp'), may hold values from -0.1875 to 0.1875
- routed_shrink: bfloat16 [4096, 1024], P('dp'), may hold values from -0.1875 to 0.1875
- router_weight: bfloat16 [1024], P('dp'), may hold values from -0.1875 to 0.1875
Outputs:
- stream_out: bfloat16 [3, 2048, 1024], P(None, 'dp', 'section')
- stream_grad: bfloat16 [3, 2048, 1024], P(None, 'dp', 'section')
- grad_dense_prenorm: float32 [1024], P('dp')
- grad_dense_query: float32 [1024, 1024], P('dp')
- grad_dense_keys: float32 [1024, 1024], P('dp')
- grad_dense_values: float32 [1024, 1024], P('dp')
- grad_dense_output: float32 [1024, 1024], P('dp')
- grad_dense_midnorm: float32 [1024], P('dp')
- grad_dense_expand: float32 [1024, 4096], P('dp')
- grad_dense_shrink: float32 [4096, 1024], P('dp')
- grad_routed_prenorm: float32 [1024], P('dp')
- grad_routed_query: float32 [1024, 1024], P('dp')
- grad_routed_keys: float32 [1024, 1024], P('dp')
- grad_routed_values: float32 [1024, 1024], P('dp')
- grad_routed_output: float32 [1024, 1024], P('dp')
- grad_routed_midnorm: float32 [1024], P('dp')
- grad_routed_expand: float32 [1024, 4096], P('dp')
- grad_routed_shrink: float32 [4096, 1024], P('dp')
- grad_router_weight: float32 [1024], P('dp')
Inputs may be any that keep to these rules, and one draw needn't show every extreme that they name: `segment_ids`: within each sequence the ids start at 0 and never fall; one sequence, drawn from the seed, is a single document, each other one holds exactly 8 documents. `chosen_rows`: each sequence's 256 positions are distinct and ascending and include 0 and 2047.
All inputs are finite; a program needn't handle non-finite values.
Results may differ from a plain program's by a relative error of at most 0.035.
Values may be sent and summed in bfloat16 or wider, within the bound.
A program may use at most 320 MiB of HBM per device.

v0:
```python
import math

import jax
import jax.numpy as jnp
from jax import lax
from jax.sharding import PartitionSpec as P

HEADS = 16
HDIM = 64


EPS = 1e-06
NEG = -1e30
HIGH = lax.Precision.HIGHEST


def broadcast(value, axis, source):
    kept = jnp.where(lax.axis_index(axis) == source, value, 0).astype(value.dtype)
    return lax.psum(kept, axis)


def norm_rows(value, gain):
    return value * lax.rsqrt(jnp.mean(value * value, axis=-1, keepdims=True) + EPS) * gain


def split_heads(value):
    return value.reshape(value.shape[0], HEADS, HDIM)


def matmul(left, right):
    return jnp.dot(left, right, preferred_element_type=jnp.float32)


def left_outer(left, right):
    return lax.dot_general(
        left, right, (((0,), (0,)), ((), ())), preferred_element_type=jnp.float32
    )


def right_outer(left, right):
    return lax.dot_general(
        left, right, (((1,), (1,)), ((), ())), preferred_element_type=jnp.float32
    )


def scan_blocks(arrays, step, carry):
    count = arrays[0].shape[0]
    size = math.gcd(count, 1024)
    stacked = tuple((item.reshape((count // size, size) + item.shape[1:]) for item in arrays))
    return lax.scan(step, carry, stacked)


def allowed_mask(qpos, qseg, kpos, kseg):
    return (kpos[None, :] <= qpos[:, None]) & (kseg[None, :] == qseg[:, None])


def project_in(value, weights):
    normed = norm_rows(value, weights[0].astype(jnp.float32)).astype(jnp.bfloat16)
    query = matmul(normed, weights[1]).astype(jnp.bfloat16)
    keys = matmul(normed, weights[2]).astype(jnp.bfloat16)
    values = matmul(normed, weights[3]).astype(jnp.bfloat16)
    return (normed, query, keys, values)


def project_out(value, mixed, weights):
    mixed_low = mixed.astype(jnp.bfloat16)
    attended = matmul(mixed_low, weights[4])
    middle = value + attended
    normed_mid = norm_rows(middle, weights[5].astype(jnp.float32)).astype(jnp.bfloat16)
    hidden_pre = matmul(normed_mid, weights[6])
    hidden = jax.nn.gelu(hidden_pre).astype(jnp.bfloat16)
    fed = matmul(hidden, weights[7])
    return (mixed_low, attended, middle, normed_mid, hidden_pre, hidden, fed)


def back_out(kept, weights, grad_fed, extra_middle, extra_attended):
    mixed_low, attended, middle, normed_mid, hidden_pre, hidden, fed = kept
    fed_low = grad_fed.astype(jnp.bfloat16)
    grad_shrink = left_outer(hidden, fed_low)
    grad_hidden = right_outer(fed_low, weights[7])
    _, gelu_pull = jax.vjp(jax.nn.gelu, hidden_pre)
    grad_pre = gelu_pull(grad_hidden)[0].astype(jnp.bfloat16)
    grad_expand = left_outer(normed_mid, grad_pre)
    grad_normed = right_outer(grad_pre, weights[6])
    _, norm_pull = jax.vjp(norm_rows, middle, weights[5].astype(jnp.float32))
    grad_middle, grad_mid = norm_pull(grad_normed)
    grad_middle = grad_middle + extra_middle
    grad_attended = (grad_middle + extra_attended).astype(jnp.bfloat16)
    grad_output = left_outer(mixed_low, grad_attended)
    grad_mixed = right_outer(grad_attended, weights[4]).astype(jnp.bfloat16)
    return (grad_middle, grad_mixed, (grad_output, grad_mid, grad_expand, grad_shrink))


def back_in(value, weights, normed, grad_query, grad_keys, grad_values):
    query_low = grad_query.astype(jnp.bfloat16)
    keys_low = grad_keys.astype(jnp.bfloat16)
    values_low = grad_values.astype(jnp.bfloat16)
    grads = (
        left_outer(normed, query_low),
        left_outer(normed, keys_low),
        left_outer(normed, values_low),
    )
    grad_normed = (
        right_outer(query_low, weights[1])
        + right_outer(keys_low, weights[2])
        + right_outer(values_low, weights[3])
    )
    _, norm_pull = jax.vjp(norm_rows, value, weights[0].astype(jnp.float32))
    grad_value, grad_pre = norm_pull(grad_normed)
    return (grad_value, (grad_pre,) + grads)


def online_step(carry, queries, qpos, qseg, keys, values, kpos, kseg):
    peak, total, accum = carry
    scale = HDIM ** (-0.5)
    scores = (
        jnp.einsum("rhd,khd->rhk", queries, split_heads(keys), preferred_element_type=jnp.float32)
        * scale
    )
    allowed = allowed_mask(qpos, qseg, kpos, kseg)[:, None, :]
    scores = jnp.where(allowed, scores, NEG)
    fresh = jnp.maximum(peak, jnp.max(scores, axis=-1))
    weight = jnp.where(allowed, jnp.exp(scores - fresh[..., None]), 0.0)
    factor = jnp.exp(peak - fresh)
    total = total * factor + jnp.sum(weight, axis=-1)
    accum = accum * factor[..., None] + jnp.einsum(
        "rhk,khd->rhd",
        weight.astype(jnp.bfloat16),
        split_heads(values),
        preferred_element_type=jnp.float32,
    )
    return (fresh, total, accum)


def pair_terms(queries, qpos, qseg, lse, row_sums, grads, keys, values, kpos, kseg):
    scale = HDIM ** (-0.5)
    scores = jnp.einsum("rhd,khd->rhk", queries, keys, preferred_element_type=jnp.float32) * scale
    allowed = allowed_mask(qpos, qseg, kpos, kseg)[:, None, :]
    probs = jnp.where(allowed, jnp.exp(scores - lse[..., None]), 0.0)
    probs_low = probs.astype(jnp.bfloat16)
    grad_probs = jnp.einsum("rhd,khd->rhk", grads, values, preferred_element_type=jnp.float32)
    grad_scores = (probs * (grad_probs - row_sums[..., None])).astype(jnp.bfloat16)
    grad_query = (
        jnp.einsum("rhk,khd->rhd", grad_scores, keys, preferred_element_type=jnp.float32) * scale
    )
    grad_keys = (
        jnp.einsum("rhk,rhd->khd", grad_scores, queries, preferred_element_type=jnp.float32) * scale
    )
    grad_values = jnp.einsum("rhk,rhd->khd", probs_low, grads, preferred_element_type=jnp.float32)
    return (grad_query, grad_keys, grad_values)


def on_device(
    stream_in,
    segment_ids,
    chosen_rows,
    cotangent,
    dense_prenorm,
    dense_query,
    dense_keys,
    dense_values,
    dense_output,
    dense_midnorm,
    dense_expand,
    dense_shrink,
    routed_prenorm,
    routed_query,
    routed_keys,
    routed_values,
    routed_output,
    routed_midnorm,
    routed_expand,
    routed_shrink,
    router_weight,
):
    sections = lax.axis_size("section")
    seqs = segment_ids.shape[0]
    section_place = lax.axis_index("section")
    own = jnp.minimum(section_place, seqs - 1)
    valid = (section_place < seqs).astype(jnp.float32)
    last = (section_place == sections - 1).astype(jnp.float32)
    value = lax.dynamic_index_in_dim(stream_in, own, 0, keepdims=False).astype(jnp.float32) * valid
    grad_top = (
        lax.dynamic_index_in_dim(cotangent, own, 0, keepdims=False).astype(jnp.float32) * valid
    )
    rows = value.shape[0]
    width = value.shape[1]
    gathered = (
        lax.all_gather(dense_prenorm, "dp", axis=0, tiled=True),
        lax.all_gather(dense_query, "dp", axis=0, tiled=True),
        lax.all_gather(dense_keys, "dp", axis=0, tiled=True),
        lax.all_gather(dense_values, "dp", axis=0, tiled=True),
        lax.all_gather(dense_output, "dp", axis=0, tiled=True),
        lax.all_gather(dense_midnorm, "dp", axis=0, tiled=True),
        lax.all_gather(dense_expand, "dp", axis=0, tiled=True),
        lax.all_gather(dense_shrink, "dp", axis=0, tiled=True),
        lax.all_gather(routed_prenorm, "dp", axis=0, tiled=True),
        lax.all_gather(routed_query, "dp", axis=0, tiled=True),
        lax.all_gather(routed_keys, "dp", axis=0, tiled=True),
        lax.all_gather(routed_values, "dp", axis=0, tiled=True),
        lax.all_gather(routed_output, "dp", axis=0, tiled=True),
        lax.all_gather(routed_midnorm, "dp", axis=0, tiled=True),
        lax.all_gather(routed_expand, "dp", axis=0, tiled=True),
        lax.all_gather(routed_shrink, "dp", axis=0, tiled=True),
        lax.all_gather(router_weight, "dp", axis=0, tiled=True),
    )
    dense_full = gathered[:8]
    routed_full = gathered[8:16]
    router_full = gathered[16].astype(jnp.float32)
    seg_all = lax.dynamic_index_in_dim(segment_ids, own, 0, keepdims=False)
    picks = lax.dynamic_index_in_dim(chosen_rows, own, 0, keepdims=False)
    first_row = lax.axis_index("dp") * rows
    qpos = first_row + jnp.arange(rows, dtype=jnp.int32)
    qseg = lax.dynamic_slice_in_dim(seg_all, first_row, rows)
    scale = HDIM ** (-0.5)
    normed, query, keys, values = project_in(value, dense_full)
    query_heads = split_heads(query)
    start_state = (
        jnp.full((rows, HEADS), NEG, jnp.float32),
        jnp.zeros((rows, HEADS), jnp.float32),
        jnp.zeros((rows, HEADS, HDIM), jnp.float32),
    )
    piece_keys = lax.all_gather(keys, "dp", axis=0, tiled=True)
    piece_values = lax.all_gather(values, "dp", axis=0, tiled=True)
    count = piece_keys.shape[0]
    kpos = jnp.arange(count, dtype=jnp.int32)

    def step(inner, block):
        return (
            online_step(inner, query_heads, qpos, qseg, block[0], block[1], block[2], block[3]),
            None,
        )

    result, _ = scan_blocks((piece_keys, piece_values, kpos, seg_all), step, start_state)
    peak, total, accum = result
    mixed = (accum / total[..., None]).reshape(rows, width)
    lse = peak + jnp.log(total)
    kept = project_out(value, mixed, dense_full)
    after_dense = kept[2] + kept[6]
    paired = jnp.concatenate([after_dense, grad_top], axis=1)
    sel_dev = chosen_rows.shape[1] // lax.axis_size("dp")
    total_sel = chosen_rows.shape[1]
    wanted = picks
    table = (wanted[:, None] == qpos[None, :]).astype(jnp.float32)
    own_rows = lax.psum_scatter(
        jnp.dot(table, paired, precision=HIGH).astype(jnp.bfloat16),
        "dp",
        scatter_dimension=0,
        tiled=True,
    ).astype(jnp.float32)
    arrived = (
        lax.all_gather(own_rows[None].astype(jnp.bfloat16), "section", axis=0, tiled=True).astype(
            jnp.float32
        )[:seqs]
        * last
    )
    picked = jnp.transpose(arrived, (1, 0, 2))
    flat_value = picked[:, :, :width].reshape(sel_dev * seqs, width)
    grad_sent = picked[:, :, width:].reshape(sel_dev * seqs, width)
    slot_start = lax.axis_index("dp") * sel_dev
    spos = lax.dynamic_slice_in_dim(chosen_rows, slot_start, sel_dev, 1)
    sseg = jnp.take_along_axis(segment_ids, spos, axis=1)
    key_seg = jnp.take_along_axis(segment_ids, chosen_rows, axis=1)
    routed_normed, routed_q, routed_k, routed_v = project_in(flat_value, routed_full)
    keys_sel, values_sel = (
        lax.all_gather(routed_k.reshape(sel_dev, seqs, width), "dp", axis=0, tiled=True),
        lax.all_gather(routed_v.reshape(sel_dev, seqs, width), "dp", axis=0, tiled=True),
    )
    keys_heads = keys_sel.reshape(total_sel, seqs, HEADS, HDIM)
    values_heads = values_sel.reshape(total_sel, seqs, HEADS, HDIM)
    routed_qh = routed_q.reshape(sel_dev, seqs, HEADS, HDIM)
    scores = (
        jnp.einsum("rshd,kshd->shrk", routed_qh, keys_heads, preferred_element_type=jnp.float32)
        * scale
    )
    allowed = (
        (chosen_rows[:, None, :] <= spos[:, :, None]) & (key_seg[:, None, :] == sseg[:, :, None])
    )[:, None]
    probs = jax.nn.softmax(jnp.where(allowed, scores, NEG), axis=-1)
    probs_low = probs.astype(jnp.bfloat16)
    routed_mixed = jnp.einsum(
        "shrk,kshd->rshd", probs_low, values_heads, preferred_element_type=jnp.float32
    ).reshape(sel_dev * seqs, width)
    routed_kept = project_out(flat_value, routed_mixed, routed_full)
    delta = routed_kept[1] + routed_kept[6]
    gate = jax.nn.sigmoid(jnp.dot(flat_value, router_full, precision=HIGH))
    sent = (gate[:, None] * delta).astype(jnp.bfloat16)
    grad_gate = jnp.sum(grad_sent * delta, axis=1)
    grad_delta = gate[:, None] * grad_sent
    grad_logit = grad_gate * gate * (1.0 - gate)
    grad_router = jnp.dot(grad_logit, flat_value, precision=HIGH) * last
    routed_middle_grad, routed_grad_mixed, routed_outer = back_out(
        routed_kept, routed_full, grad_delta, 0.0, grad_delta
    )
    grad_mixed_heads = routed_grad_mixed.reshape(sel_dev, seqs, HEADS, HDIM)
    grad_probs = jnp.einsum(
        "rshd,kshd->shrk", grad_mixed_heads, values_heads, preferred_element_type=jnp.float32
    )
    grad_scores = (
        probs * (grad_probs - jnp.sum(grad_probs * probs, axis=-1, keepdims=True))
    ).astype(jnp.bfloat16)
    routed_dq = (
        jnp.einsum("shrk,kshd->rshd", grad_scores, keys_heads, preferred_element_type=jnp.float32)
        * scale
    )
    routed_dk = (
        jnp.einsum("shrk,rshd->kshd", grad_scores, routed_qh, preferred_element_type=jnp.float32)
        * scale
    )
    routed_dv = jnp.einsum(
        "shrk,rshd->kshd", probs_low, grad_mixed_heads, preferred_element_type=jnp.float32
    )
    mine_rk, mine_rv = (
        lax.psum_scatter(
            routed_dk.reshape(total_sel, seqs, width).astype(jnp.bfloat16),
            "dp",
            scatter_dimension=0,
            tiled=True,
        ).astype(jnp.float32),
        lax.psum_scatter(
            routed_dv.reshape(total_sel, seqs, width).astype(jnp.bfloat16),
            "dp",
            scatter_dimension=0,
            tiled=True,
        ).astype(jnp.float32),
    )
    routed_grad_in, routed_inner = back_in(
        flat_value,
        routed_full,
        routed_normed,
        routed_dq.reshape(sel_dev * seqs, width),
        mine_rk.reshape(sel_dev * seqs, width),
        mine_rv.reshape(sel_dev * seqs, width),
    )
    grad_chosen = (routed_middle_grad + routed_grad_in + grad_logit[:, None] * router_full).astype(
        jnp.bfloat16
    )
    routed_inner = tuple((item * last for item in routed_inner))
    routed_outer = tuple((item * last for item in routed_outer))
    back_sent, back_grad = (
        broadcast(sent.reshape(sel_dev, seqs, width), "section", sections - 1),
        broadcast(grad_chosen.reshape(sel_dev, seqs, width), "section", sections - 1),
    )
    own_sent = lax.dynamic_index_in_dim(back_sent, own, 1, keepdims=False)
    own_grad = lax.dynamic_index_in_dim(back_grad, own, 1, keepdims=False)
    wanted = picks
    table = (qpos[:, None] == wanted[None, :]).astype(jnp.bfloat16)
    added = matmul(table, lax.all_gather(own_sent, "dp", axis=0, tiled=True))
    returned = matmul(table, lax.all_gather(own_grad, "dp", axis=0, tiled=True))
    out_rows = (after_dense + added).astype(jnp.bfloat16)
    grad_after = (grad_top + returned) * valid
    dense_middle_grad, dense_grad_mixed, dense_outer = back_out(
        kept, dense_full, grad_after, grad_after, 0.0
    )
    grad_heads = split_heads(dense_grad_mixed)
    row_sums = jnp.sum(
        split_heads(kept[0]).astype(jnp.float32) * grad_heads.astype(jnp.float32), axis=-1
    )
    zero_heads = jnp.zeros((rows, HEADS, HDIM), jnp.float32)
    keys_all, values_all = (
        lax.all_gather(keys, "dp", axis=0, tiled=True),
        lax.all_gather(values, "dp", axis=0, tiled=True),
    )
    length = keys_all.shape[0]

    def key_step(grad_acc, block):
        block_keys, block_values, block_pos, block_seg = block
        part_q, part_k, part_v = pair_terms(
            query_heads,
            qpos,
            qseg,
            lse,
            row_sums,
            grad_heads,
            split_heads(block_keys),
            split_heads(block_values),
            block_pos,
            block_seg,
        )
        return (grad_acc + part_q, (part_k, part_v))

    grad_query_heads, (key_terms, value_terms) = scan_blocks(
        (keys_all, values_all, jnp.arange(length, dtype=jnp.int32), seg_all), key_step, zero_heads
    )
    mine_keys, mine_values = (
        lax.psum_scatter(
            key_terms.reshape(length, width).astype(jnp.bfloat16),
            "dp",
            scatter_dimension=0,
            tiled=True,
        ).astype(jnp.float32),
        lax.psum_scatter(
            value_terms.reshape(length, width).astype(jnp.bfloat16),
            "dp",
            scatter_dimension=0,
            tiled=True,
        ).astype(jnp.float32),
    )
    dense_grad_in, dense_inner = back_in(
        value, dense_full, normed, grad_query_heads.reshape(rows, width), mine_keys, mine_values
    )
    grad_rows = (dense_middle_grad + dense_grad_in).astype(jnp.bfloat16)
    out_parts, grad_parts = (
        lax.all_to_all(out_rows[None], "section", split_axis=2, concat_axis=0, tiled=True),
        lax.all_to_all(grad_rows[None], "section", split_axis=2, concat_axis=0, tiled=True),
    )
    stream_out = out_parts[:seqs]
    stream_grad = grad_parts[:seqs]
    shards = (
        lax.psum_scatter(
            dense_inner[0].astype(jnp.bfloat16), "dp", scatter_dimension=0, tiled=True
        ).astype(jnp.float32),
        lax.psum_scatter(
            dense_inner[1].astype(jnp.bfloat16), "dp", scatter_dimension=0, tiled=True
        ).astype(jnp.float32),
        lax.psum_scatter(
            dense_inner[2].astype(jnp.bfloat16), "dp", scatter_dimension=0, tiled=True
        ).astype(jnp.float32),
        lax.psum_scatter(
            dense_inner[3].astype(jnp.bfloat16), "dp", scatter_dimension=0, tiled=True
        ).astype(jnp.float32),
        lax.psum_scatter(
            dense_outer[0].astype(jnp.bfloat16), "dp", scatter_dimension=0, tiled=True
        ).astype(jnp.float32),
        lax.psum_scatter(
            dense_outer[1].astype(jnp.bfloat16), "dp", scatter_dimension=0, tiled=True
        ).astype(jnp.float32),
        lax.psum_scatter(
            dense_outer[2].astype(jnp.bfloat16), "dp", scatter_dimension=0, tiled=True
        ).astype(jnp.float32),
        lax.psum_scatter(
            dense_outer[3].astype(jnp.bfloat16), "dp", scatter_dimension=0, tiled=True
        ).astype(jnp.float32),
        lax.psum_scatter(
            routed_inner[0].astype(jnp.bfloat16), "dp", scatter_dimension=0, tiled=True
        ).astype(jnp.float32),
        lax.psum_scatter(
            routed_inner[1].astype(jnp.bfloat16), "dp", scatter_dimension=0, tiled=True
        ).astype(jnp.float32),
        lax.psum_scatter(
            routed_inner[2].astype(jnp.bfloat16), "dp", scatter_dimension=0, tiled=True
        ).astype(jnp.float32),
        lax.psum_scatter(
            routed_inner[3].astype(jnp.bfloat16), "dp", scatter_dimension=0, tiled=True
        ).astype(jnp.float32),
        lax.psum_scatter(
            routed_outer[0].astype(jnp.bfloat16), "dp", scatter_dimension=0, tiled=True
        ).astype(jnp.float32),
        lax.psum_scatter(
            routed_outer[1].astype(jnp.bfloat16), "dp", scatter_dimension=0, tiled=True
        ).astype(jnp.float32),
        lax.psum_scatter(
            routed_outer[2].astype(jnp.bfloat16), "dp", scatter_dimension=0, tiled=True
        ).astype(jnp.float32),
        lax.psum_scatter(
            routed_outer[3].astype(jnp.bfloat16), "dp", scatter_dimension=0, tiled=True
        ).astype(jnp.float32),
        lax.psum_scatter(
            grad_router.astype(jnp.bfloat16), "dp", scatter_dimension=0, tiled=True
        ).astype(jnp.float32),
    )
    totals = (
        lax.psum(shards[0].astype(jnp.bfloat16), "section").astype(jnp.float32),
        lax.psum(shards[1].astype(jnp.bfloat16), "section").astype(jnp.float32),
        lax.psum(shards[2].astype(jnp.bfloat16), "section").astype(jnp.float32),
        lax.psum(shards[3].astype(jnp.bfloat16), "section").astype(jnp.float32),
        lax.psum(shards[4].astype(jnp.bfloat16), "section").astype(jnp.float32),
        lax.psum(shards[5].astype(jnp.bfloat16), "section").astype(jnp.float32),
        lax.psum(shards[6].astype(jnp.bfloat16), "section").astype(jnp.float32),
        lax.psum(shards[7].astype(jnp.bfloat16), "section").astype(jnp.float32),
        lax.psum(shards[8].astype(jnp.bfloat16), "section").astype(jnp.float32),
        lax.psum(shards[9].astype(jnp.bfloat16), "section").astype(jnp.float32),
        lax.psum(shards[10].astype(jnp.bfloat16), "section").astype(jnp.float32),
        lax.psum(shards[11].astype(jnp.bfloat16), "section").astype(jnp.float32),
        lax.psum(shards[12].astype(jnp.bfloat16), "section").astype(jnp.float32),
        lax.psum(shards[13].astype(jnp.bfloat16), "section").astype(jnp.float32),
        lax.psum(shards[14].astype(jnp.bfloat16), "section").astype(jnp.float32),
        lax.psum(shards[15].astype(jnp.bfloat16), "section").astype(jnp.float32),
        lax.psum(shards[16].astype(jnp.bfloat16), "section").astype(jnp.float32),
    )
    return (
        stream_out,
        stream_grad,
        totals[0],
        totals[1],
        totals[2],
        totals[3],
        totals[4],
        totals[5],
        totals[6],
        totals[7],
        totals[8],
        totals[9],
        totals[10],
        totals[11],
        totals[12],
        totals[13],
        totals[14],
        totals[15],
        totals[16],
    )


def solution(mesh):
    placed = (
        P(None, "dp", None),
        P(),
        P(),
        P(None, "dp", None),
        P("dp"),
        P("dp", None),
        P("dp", None),
        P("dp", None),
        P("dp", None),
        P("dp"),
        P("dp", None),
        P("dp", None),
        P("dp"),
        P("dp", None),
        P("dp", None),
        P("dp", None),
        P("dp", None),
        P("dp"),
        P("dp", None),
        P("dp", None),
        P("dp"),
    )
    return jax.shard_map(
        on_device,
        mesh=mesh,
        in_specs=placed,
        out_specs=(
            P(None, "dp", "section"),
            P(None, "dp", "section"),
            P("dp"),
            P("dp", None),
            P("dp", None),
            P("dp", None),
            P("dp", None),
            P("dp"),
            P("dp", None),
            P("dp", None),
            P("dp"),
            P("dp", None),
            P("dp", None),
            P("dp", None),
            P("dp", None),
            P("dp"),
            P("dp", None),
            P("dp", None),
            P("dp"),
        ),
        check_vma=False,
    )
```

profile of v0, /device:TPU:0, one launch (start us, length us, event | category | flops | bytes accessed | tf_op | source)
XLA Modules:
  0.0 2099.1 jit_solution(1570273394109145869)
XLA Ops:
  9.5 13.5 all-gather.3
  24.3 17.1 all-gather.25.cloned.1.call-done
  45.0 26.7 %all-gather.31.cloned.1.call-done = bf16[1024,1024]{1,0:T(8,128)(2,1)} async-done(((bf16[128,1024]{1,0:T(8,128)(2,1)}), bf16[1024,1024]{1,0:T(8,128)(2,1)}) %all-gather.31.cloned.1.call-update) | async-done | bytes 2097168 | tf_op jit(solution)/shard_map/all_gather | solution.py:192
  77.1 10.3 all-gather.4
  89.7 12.3 all-gather.29.cloned.1.call-done
  104.5 46.1 %all-gather.27.cloned.1.call-done = bf16[2048,1024]{1,0:T(8,128)(2,1)} async-done(((bf16[256,1024]{1,0:T(8,128)(2,1)}), bf16[2048,1024]{1,0:T(8,128)(2,1)}) %all-gather.27.cloned.1.call-update) | async-done | bytes 4194320 | tf_op jit(solution)/shard_map/all_gather | solution.py:223
  156.9 41.7 %all-gather.33.cloned.1.call-done = bf16[2048,1024]{1,0:T(8,128)(2,1)} async-done(((bf16[256,1024]{1,0:T(8,128)(2,1)}), bf16[2048,1024]{1,0:T(8,128)(2,1)}) %all-gather.33.cloned.1.call-update) | async-done | bytes 4194320 | tf_op jit(solution)/shard_map/all_gather | solution.py:224
  204.9 57.7 %while.30 = (s32[]{:T(128)}, f32[256,16]{0,1:T(8,128)S(1)}, f32[256,16]{0,1:T(8,128)S(1)}, f32[256,16,64]{0,2,1:T(8,128)S(1)}, s32[2,1024]{1,0:T(2,128)S(1)}, /*...) while((s32[]{:T(128)}, f32[256,16]{0,1:T(8,128)S(1)}, ...), condition=%wide.region_4.5_spmd.clone, body=%wide.region_1.4_spmd.clone.sunk | while | flops 1129861376 | bytes 133983400 | solution.py:50
  209.5 7.5 fusion.224
  217.0 8.3 fusion.225
  238.2 7.4 fusion.224
  245.7 8.3 fusion.225
  267.7 43.3 %all-gather.37.cloned.1.call-done = bf16[1024,4096]{1,0:T(8,128)(2,1)} async-done(((bf16[128,4096]{1,0:T(8,128)(2,1)}), bf16[1024,4096]{1,0:T(8,128)(2,1)}) %all-gather.37.cloned.1.call-update) | async-done | bytes 8388624 | tf_op jit(solution)/shard_map/all_gather | solution.py:195
  311.0 7.7 fusion.123
  318.8 74.5 %all-gather.39.cloned.1.call-done = bf16[4096,1024]{1,0:T(8,128)(2,1)} async-done(((bf16[512,1024]{1,0:T(8,128)(2,1)}), bf16[4096,1024]{1,0:T(8,128)(2,1)}) %all-gather.39.cloned.1.call-update) | async-done | bytes 8388624 | tf_op jit(solution)/shard_map/all_gather | solution.py:196
  393.3 7.5 convolution_add_fusion.5
  405.9 9.0 all-gather.6
  414.9 20.0 reduce-scatter.16.cloned.1.call-done
  434.9 10.6 all-gather
  449.0 14.9 all-gather.47.cloned.1.call-done
  467.0 27.2 %all-gather.41.cloned.1.call-done = bf16[1024,1024]{1,0:T(8,128)(2,1)} async-done(((bf16[128,1024]{1,0:T(8,128)(2,1)}), bf16[1024,1024]{1,0:T(8,128)(2,1)}) %all-gather.41.cloned.1.call-update) | async-done | bytes 2097168 | tf_op jit(solution)/shard_map/all_gather | solution.py:200
  500.8 6.7 gather_fusion
  507.5 10.3 all-gather.7
  517.8 8.8 all-gather.5
  529.6 21.4 %all-gather.49.cloned.1.call-done = bf16[256,3,1024]{2,0,1:T(8,128)(2,1)} async-done(((bf16[32,3,1024]{2,0,1:T(8,128)(2,1)}), bf16[256,3,1024]{2,0,1:T(8,128)(2,1)}) %all-gather.49.cloned.1.call-update) | async-done | bytes 1572880 | tf_op jit(solution)/shard_map/all_gather | solution.py:266
  553.6 24.1 %all-gather.43.cloned.1.call-done = bf16[256,3,1024]{2,0,1:T(8,128)(2,1)} async-done(((bf16[32,3,1024]{2,0,1:T(8,128)(2,1)}), bf16[256,3,1024]{2,0,1:T(8,128)(2,1)}) %all-gather.43.cloned.1.call-update) | async-done | bytes 1572880 | tf_op jit(solution)/shard_map/all_gather | solution.py:267
  590.9 16.9 all-gather.51.cloned.1.call-done
  610.8 80.1 %all-gather.53.cloned.1.call-done = bf16[1024,4096]{1,0:T(8,128)(2,1)} async-done(((bf16[128,4096]{1,0:T(8,128)(2,1)}), bf16[1024,4096]{1,0:T(8,128)(2,1)}) %all-gather.53.cloned.1.call-update) | async-done | bytes 8388624 | tf_op jit(solution)/shard_map/all_gather | solution.py:203
  696.9 76.0 %all-gather.55.cloned.1.call-done = bf16[4096,1024]{1,0:T(8,128)(2,1)} async-done(((bf16[512,1024]{1,0:T(8,128)(2,1)}), bf16[4096,1024]{1,0:T(8,128)(2,1)}) %all-gather.55.cloned.1.call-update) | async-done | bytes 8388624 | tf_op jit(solution)/shard_map/all_gather | solution.py:204
  772.9 7.1 fusion.54
  787.5 6.4 convolution_convert_fusion.7
  814.9 88.8 %all-reduce.17.cloned.1.call-done = (bf16[256,3,1024]{2,1,0:T(4,128)(2,1)}, bf16[256,3,1024]{2,1,0:T(4,128)(2,1)}) async-done(((bf16[256,3,1024]{2,1,0:T(4,128)(2,1)}, bf16[256,3,1024]{2,1,0:T(4,128)(2,1)}), (bf16[256,3,1024]{2,1,0:T(4,128)(2,1)}, bf16[256,3,1024]{2,1,0:T(4,128)(2,1)})) %all-reduce.17.cloned.1.call-update) | async-done | bytes 3145744
  912.3 43.1 %all-reduce.15.cloned.1.call-done = bf16[32,3,1024]{2,1,0:T(4,128)(2,1)} async-done(((bf16[32,3,1024]{2,1,0:T(4,128)(2,1)}), bf16[32,3,1024]{2,1,0:T(4,128)(2,1)}) %all-reduce.15.cloned.1.call-update) | async-done | bytes 196624 | tf_op jit(solution)/shard_map/psum | solution.py:19
  956.5 14.9 all-gather.2
  972.8 11.6 fusion.41
  991.1 88.0 %while.31 = (s32[]{:T(128)}, f32[256,16,64]{0,2,1:T(8,128)}, bf16[2,1024,16,64]{1,3,2,0:T(8,128)(2,1)}, bf16[2,1024,16,64]{1,3,2,0:T(8,128)(2,1)}, bf16[2,1024,1...) while((s32[]{:T(128)}, f32[256,16,64]{0,2,1:T(8,128)}, ...), condition=%wide.region_22.23_spmd.clone, body=%wide.region_21.22_spmd.clone.sunk | while | flops 2728919296 | bytes 137179344 | solution.py:50
  994.5 8.2 fusion.238
  1002.8 8.7 fusion.239
  1024.7 10.5 bitcast_dynamic-update-slice_fusion.5
  1038.2 8.2 fusion.238
  1046.4 8.7 fusion.239
  1068.6 10.4 bitcast_dynamic-update-slice_fusion.5
  1079.1 6.5 copy.155
  1089.1 6.5 copy.156
  1114.9 24.5 %reduce-scatter.18.cloned.1.call-done = bf16[256,1024]{0,1:T(8,128)(2,1)} async-done(((bf16[2048,1024]{0,1:T(8,128)(2,1)}), bf16[256,1024]{0,1:T(8,128)(2,1)}) %reduce-scatter.18.cloned.1.call-update) | async-done | bytes 524304 | tf_op jit(solution)/shard_map/reduce_scatter | solution.py:386
  1143.2 46.7 %reduce-scatter.20.cloned.1.call-done = bf16[256,1024]{0,1:T(8,128)(2,1)} async-done(((bf16[2048,1024]{0,1:T(8,128)(2,1)}), bf16[256,1024]{0,1:T(8,128)(2,1)}) %reduce-scatter.20.cloned.1.call-update) | async-done | bytes 524304 | tf_op jit(solution)/shard_map/reduce_scatter | solution.py:392
  1200.2 7.1 multiply_convert_fusion
  1208.6 7.4 convolution_convert_fusion.1
  1217.2 8.5 convolution_convert_fusion
  1227.5 35.8 %reduce-scatter.34.cloned.1.call-done = bf16[128,1024]{1,0:T(8,128)(2,1)} async-done(((bf16[1024,1024]{1,0:T(8,128)(2,1)}), bf16[128,1024]{1,0:T(8,128)(2,1)}) %reduce-scatter.34.cloned.1.call-update) | async-done | bytes 262160 | tf_op jit(solution)/shard_map/reduce_scatter | solution.py:437
  1263.3 36.9 %reduce-scatter.36.cloned.1.call-done = bf16[128,1024]{1,0:T(8,128)(2,1)} async-done(((bf16[1024,1024]{1,0:T(8,128)(2,1)}), bf16[128,1024]{1,0:T(8,128)(2,1)}) %reduce-scatter.36.cloned.1.call-update) | async-done | bytes 262160 | tf_op jit(solution)/shard_map/reduce_scatter | solution.py:440
  1300.2 36.7 %reduce-scatter.38.cloned.1.call-done = bf16[128,1024]{1,0:T(8,128)(2,1)} async-done(((bf16[1024,1024]{1,0:T(8,128)(2,1)}), bf16[128,1024]{1,0:T(8,128)(2,1)}) %reduce-scatter.38.cloned.1.call-update) | async-done | bytes 262160 | tf_op jit(solution)/shard_map/reduce_scatter | solution.py:443
  1336.8 37.4 %reduce-scatter.28.cloned.1.call-done = bf16[128,1024]{1,0:T(8,128)(2,1)} async-done(((bf16[1024,1024]{1,0:T(8,128)(2,1)}), bf16[128,1024]{1,0:T(8,128)(2,1)}) %reduce-scatter.28.cloned.1.call-update) | async-done | bytes 262160 | tf_op jit(solution)/shard_map/reduce_scatter | solution.py:422
  1374.2 37.3 %reduce-scatter.22.cloned.1.call-done = bf16[128,1024]{1,0:T(8,128)(2,1)} async-done(((bf16[1024,1024]{1,0:T(8,128)(2,1)}), bf16[128,1024]{1,0:T(8,128)(2,1)}) %reduce-scatter.22.cloned.1.call-update) | async-done | bytes 262160 | tf_op jit(solution)/shard_map/reduce_scatter | solution.py:413
  1411.5 37.5 %reduce-scatter.24.cloned.1.call-done = bf16[128,1024]{1,0:T(8,128)(2,1)} async-done(((bf16[1024,1024]{1,0:T(8,128)(2,1)}), bf16[128,1024]{1,0:T(8,128)(2,1)}) %reduce-scatter.24.cloned.1.call-update) | async-done | bytes 262160 | tf_op jit(solution)/shard_map/reduce_scatter | solution.py:416
  1448.9 37.5 %reduce-scatter.26.cloned.1.call-done = bf16[128,1024]{1,0:T(8,128)(2,1)} async-done(((bf16[1024,1024]{1,0:T(8,128)(2,1)}), bf16[128,1024]{1,0:T(8,128)(2,1)}) %reduce-scatter.26.cloned.1.call-update) | async-done | bytes 262160 | tf_op jit(solution)/shard_map/reduce_scatter | solution.py:419
  1486.5 90.6 %reduce-scatter.42.cloned.1.call-done = bf16[128,4096]{1,0:T(8,128)(2,1)} async-done(((bf16[1024,4096]{1,0:T(8,128)(2,1)}), bf16[128,4096]{1,0:T(8,128)(2,1)}) %reduce-scatter.42.cloned.1.call-update) | async-done | bytes 1048592 | tf_op jit(solution)/shard_map/reduce_scatter | solution.py:452
  1577.0 90.4 %reduce-scatter.44.cloned.1.call-done = bf16[512,1024]{1,0:T(8,128)(2,1)} async-done(((bf16[4096,1024]{1,0:T(8,128)(2,1)}), bf16[512,1024]{1,0:T(8,128)(2,1)}) %reduce-scatter.44.cloned.1.call-update) | async-done | bytes 1048592 | tf_op jit(solution)/shard_map/reduce_scatter | solution.py:455
  1667.4 90.4 %reduce-scatter.30.cloned.1.call-done = bf16[128,4096]{1,0:T(8,128)(2,1)} async-done(((bf16[1024,4096]{1,0:T(8,128)(2,1)}), bf16[128,4096]{1,0:T(8,128)(2,1)}) %reduce-scatter.30.cloned.1.call-update) | async-done | bytes 1048592 | tf_op jit(solution)/shard_map/reduce_scatter | solution.py:428
  1757.8 90.2 %reduce-scatter.32.cloned.1.call-done = bf16[512,1024]{1,0:T(8,128)(2,1)} async-done(((bf16[4096,1024]{1,0:T(8,128)(2,1)}), bf16[512,1024]{1,0:T(8,128)(2,1)}) %reduce-scatter.32.cloned.1.call-update) | async-done | bytes 1048592 | tf_op jit(solution)/shard_map/reduce_scatter | solution.py:431
  1865.2 141.9 %all-reduce.19.cloned.1.call-done = (bf16[32,3,1024]{2,1,0:T(4,128)(2,1)}, bf16[128,1024]{1,0:T(8,128)(2,1)}, bf16[128,1024]{1,0:T(8,128)(2,1)}, bf16[128,1024]{...) async-done(((bf16[32,3,1024]{2,1,0:T(4,128)(2,1)}, ...) | async-done | bytes 6488080 | tf_op jit(solution)/shard_map/psum | solution.py:19
  2008.2 14.7 all-gather.1
  2032.5 29.3 %all-reduce.7 = (bf16[1024]{0:T(1024)(128)(2,1)S(1)}, bf16[1024]{0:T(1024)(128)(2,1)S(1)}, bf16[1024]{0:T(1024)(128)(2,1)S(1)}, bf16[1024]{0:T(1024)(128)(2,1)S(1)}, bf16[1024]{0:T(1024)(128)(2,1)S(1)}) all-reduce(bf16[1024]{0:T(1024)(128)(2,1)S(1)} %get-tuple-element.364, ...), channel_id=10, replica_groups=mesh['section'=4,'dp'=8] {'dp'}, use_global_device_ids=true, to_apply=%region_27.28.clone | all-reduce | flops 5120 | bytes 20480
  2062.1 10.0 all-reduce.9
  (518 shorter events, 271.9 us)
Async XLA Ops:
  7.2 34.3 %all-gather.25.cloned.1.call-start = ((), (), s32[]{:S(2)}) async-start(), calls=%async_computation.17 | async-start | bytes 2359296 | tf_op jit(solution)/shard_map/all_gather | solution.py:191
  7.9 63.8 %all-gather.31.cloned.1.call-start = ((), (), s32[]{:S(2)}) async-start(), calls=%async_computation.20 | async-start | bytes 2359296 | tf_op jit(solution)/shard_map/all_gather | solution.py:192
  8.7 93.3 %all-gather.29.cloned.1.call-start = ((), (), s32[]{:S(2)}) async-start(), calls=%async_computation.19 | async-start | bytes 2359296 | tf_op jit(solution)/shard_map/all_gather | solution.py:190
  9.4 141.2 %all-gather.27.cloned.1.call-start = ((), (), s32[]{:S(2)}) async-start(), calls=%async_computation.18 | async-start | bytes 4718592 | tf_op jit(solution)/shard_map/all_gather | solution.py:223
  23.0 78.9 %copy-start.77 = (f32[8,1,128]{2,1,0:T(1,128)}, f32[8,1,128]{2,1,0:T(1,128)S(1)}, u32[]{:S(2)}) copy-start(f32[8,1,128]{2,1,0:T(1,128)S(1)} %convert_element_type.468) | copy-start | bytes 12292
  24.3 77.6 %copy-start.83 = (f32[256]{0:T(256)}, f32[256]{0:T(256)S(1)}, u32[]{:S(2)}) copy-start(f32[256]{0:T(256)S(1)} %fusion.114) | copy-start | bytes 3076
  41.5 30.2 %copy-start.18 = (bf16[3,256,1024]{2,1,0:T(8,128)(2,1)S(1)}, bf16[3,256,1024]{2,1,0:T(8,128)(2,1)}, u32[]{:S(2)}) copy-start(bf16[3,256,1024]{2,1,0:T(8,128)(2,1)} %param.25) | copy-start | bytes 4718596
  44.9 153.6 %all-gather.33.cloned.1.call-start = ((), (), s32[]{:S(2)}) async-start(), calls=%async_computation.21 | async-start | bytes 4718592 | tf_op jit(solution)/shard_map/all_gather | solution.py:224
  74.9 190.1 %all-gather.35.cloned.1.call-start = ((), (), s32[]{:S(2)}) async-start(), calls=%async_computation.22 | async-start | bytes 2359296 | tf_op jit(solution)/shard_map/all_gather | solution.py:193
  75.4 235.6 %all-gather.37.cloned.1.call-start = ((), (), s32[]{:S(2)}) async-start(), calls=%async_computation.23 | async-start | bytes 9437184 | tf_op jit(solution)/shard_map/all_gather | solution.py:195
  76.2 317.1 %all-gather.39.cloned.1.call-start = ((), (), s32[]{:S(2)}) async-start(), calls=%async_computation.24 | async-start | bytes 9437184 | tf_op jit(solution)/shard_map/all_gather | solution.py:196
  76.9 357.9 %reduce-scatter.16.cloned.1.call-start = ((), (), s32[]{:S(2)}) async-start(), calls=%async_computation.25 | async-start | bytes 1179648 | tf_op jit(solution)/shard_map/reduce_scatter | solution.py:245
  87.4 900.2 %copy-start.59 = (f32[8,1,128]{2,1,0:T(1,128)}, f32[8,1,128]{2,1,0:T(1,128)S(1)}, u32[]{:S(2)}) copy-start(f32[8,1,128]{2,1,0:T(1,128)S(1)} %convert_element_type.469) | copy-start | bytes 12292
  87.5 313.3 %copy-start.92 = (s32[256]{0:T(256)}, s32[256]{0:T(256)S(1)}, u32[]{:S(2)}) copy-start(s32[256]{0:T(256)S(1)} %iota_add_fusion.2) | copy-start | bytes 3076
  87.5 313.3 %copy-start.87 = (s32[1,256]{1,0:T(1,128)}, s32[1,256]{1,0:T(1,128)S(1)}, u32[]{:S(2)}) copy-start(s32[1,256]{1,0:T(1,128)S(1)} %constant_dynamic-slice_fusion.11) | copy-start | bytes 3076
  267.7 51.1 %copy-start.97 = (f32[256]{0:T(256)}, f32[256]{0:T(256)S(1)}, u32[]{:S(2)}) copy-start(f32[256]{0:T(256)S(1)} %get-tuple-element.470) | copy-start | bytes 3076
  267.7 719.9 %copy-start.5 = (f32[256,1024]{1,0:T(8,128)}, f32[256,1024]{1,0:T(8,128)S(1)}, u32[]{:S(2)}) copy-start(f32[256,1024]{1,0:T(8,128)S(1)} %get-tuple-element.471) | copy-start | bytes 3145732
  267.7 51.1 %copy-start.80 = (f32[256]{0:T(256)}, f32[256]{0:T(256)S(1)}, u32[]{:S(2)}) copy-start(f32[256]{0:T(256)S(1)} %fusion.115) | copy-start | bytes 3076
  404.0 59.9 %all-gather.47.cloned.1.call-start = ((), (), s32[]{:S(2)}) async-start(), calls=%async_computation.29 | async-start | bytes 2359296 | tf_op jit(solution)/shard_map/all_gather | solution.py:199
  404.6 89.6 %all-gather.41.cloned.1.call-start = ((), (), s32[]{:S(2)}) async-start(), calls=%async_computation.26 | async-start | bytes 2359296 | tf_op jit(solution)/shard_map/all_gather | solution.py:200
  405.3 121.4 %all-gather.45.cloned.1.call-start = ((), (), s32[]{:S(2)}) async-start(), calls=%async_computation.28 | async-start | bytes 2359296 | tf_op jit(solution)/shard_map/all_gather | solution.py:198
  405.9 145.2 %all-gather.49.cloned.1.call-start = ((), (), s32[]{:S(2)}) async-start(), calls=%async_computation.30 | async-start | bytes 1769472 | tf_op jit(solution)/shard_map/all_gather | solution.py:266
  448.7 462.3 %copy-start.9 = (f32[96,1024]{1,0:T(8,128)}, f32[96,1024]{1,0:T(8,128)S(1)}, u32[]{:S(2)}) copy-start(f32[96,1024]{1,0:T(8,128)S(1)} %reshape.438) | copy-start | bytes 1179652
  466.9 110.8 %all-gather.43.cloned.1.call-start = ((), (), s32[]{:S(2)}) async-start(), calls=%async_computation.27 | async-start | bytes 1769472 | tf_op jit(solution)/shard_map/all_gather | solution.py:267
  497.1 110.7 %all-gather.51.cloned.1.call-start = ((), (), s32[]{:S(2)}) async-start(), calls=%async_computation.31 | async-start | bytes 2359296 | tf_op jit(solution)/shard_map/all_gather | solution.py:201
  497.7 193.1 %all-gather.53.cloned.1.call-start = ((), (), s32[]{:S(2)}) async-start(), calls=%async_computation.32 | async-start | bytes 9437184 | tf_op jit(solution)/shard_map/all_gather | solution.py:203
  498.3 274.6 %all-gather.55.cloned.1.call-start = ((), (), s32[]{:S(2)}) async-start(), calls=%async_computation.33 | async-start | bytes 9437184 | tf_op jit(solution)/shard_map/all_gather | solution.py:204
  498.9 404.9 %all-reduce.17.cloned.1.call-start = ((), (), s32[]{:S(2)}) async-start(), calls=%async_computation.49 | async-start | bytes 8388608
  517.8 393.3 %copy-start.56 = (f32[8,1,128]{2,1,0:T(1,128)}, f32[8,1,128]{2,1,0:T(1,128)S(1)}, u32[]{:S(2)}) copy-start(f32[8,1,128]{2,1,0:T(1,128)S(1)} %convert_element_type.471) | copy-start | bytes 12292
  529.1 51.5 %copy-start.32 = (bf16[32,3,16,64]{3,2,1,0:T(8,128)(2,1)}, bf16[32,3,16,64]{3,2,1,0:T(8,128)(2,1)S(1)}, u32[]{:S(2)}) copy-start(bf16[32,3,16,64]{3,2,1,0:T(8,128)(2,1)S(1)} %reshape.443) | copy-start | bytes 589828
  529.3 256.5 %copy-start.46 = (f32[96,1024]{1,0:T(8,128)}, f32[96,1024]{1,0:T(8,128)S(1)}, u32[]{:S(2)}) copy-start(f32[96,1024]{1,0:T(8,128)S(1)} %reshape.446) | copy-start | bytes 1179652
  529.6 256.2 %copy-start.102 = (f32[96]{0:T(128)}, f32[96]{0:T(128)S(1)}, u32[]{:S(2)}) copy-start(f32[96]{0:T(128)S(1)} %fusion.65) | copy-start | bytes 1156
  590.8 106.1 %copy-start.39 = (bf16[96,1024]{1,0:T(8,128)(2,1)}, bf16[96,1024]{1,0:T(8,128)(2,1)S(1)}, u32[]{:S(2)}) copy-start(bf16[96,1024]{1,0:T(8,128)(2,1)S(1)} %convert_element_type.393) | copy-start | bytes 589828
  610.7 300.3 %copy-start.7 = (f32[96,1024]{1,0:T(8,128)}, f32[96,1024]{1,0:T(8,128)S(1)}, u32[]{:S(2)}) copy-start(f32[96,1024]{1,0:T(8,128)S(1)} %get-tuple-element.450) | copy-start | bytes 1179652
  610.8 300.3 %copy-start.85 = (f32[96]{0:T(128)}, f32[96]{0:T(128)S(1)}, u32[]{:S(2)}) copy-start(f32[96]{0:T(128)S(1)} %fusion.119) | copy-start | bytes 1156
  808.2 147.2 %all-reduce.15.cloned.1.call-start = ((), (), s32[]{:S(2)}) async-start(), calls=%async_computation.34 | async-start | bytes 524288 | tf_op jit(solution)/shard_map/psum | solution.py:19
  812.4 94.3 %copy-start.43 = (bf16[96,1024]{1,0:T(8,128)(2,1)}, bf16[96,1024]{1,0:T(8,128)(2,1)S(1)}, u32[]{:S(2)}) copy-start(bf16[96,1024]{1,0:T(8,128)(2,1)S(1)} %convert_element_type.406) | copy-start | bytes 589828
  812.5 98.6 %copy-start.105 = (f32[96]{0:T(128)}, f32[96]{0:T(128)S(1)}, u32[]{:S(2)}) copy-start(f32[96]{0:T(128)S(1)} %subtract_multiply_fusion) | copy-start | bytes 1156
  911.0 60.4 %copy-start.88 = (s32[1,256]{1,0:T(1,128)S(1)}, s32[1,256]{1,0:T(1,128)}, u32[]{:S(2)}) copy-start(s32[1,256]{1,0:T(1,128)} %copy-done.87) | copy-start | bytes 3076
  911.0 60.4 %copy-start.93 = (s32[256]{0:T(256)S(1)}, s32[256]{0:T(256)}, u32[]{:S(2)}) copy-start(s32[256]{0:T(256)} %copy-done.92) | copy-start | bytes 3076
  912.2 227.1 %reduce-scatter.18.cloned.1.call-start = ((), (), s32[]{:S(2)}) async-start(), calls=%async_computation.35 | async-start | bytes 4718592 | tf_op jit(solution)/shard_map/reduce_scatter | solution.py:386
  1089.0 100.9 %reduce-scatter.20.cloned.1.call-start = ((), (), s32[]{:S(2)}) async-start(), calls=%async_computation.36 | async-start | bytes 4718592 | tf_op jit(solution)/shard_map/reduce_scatter | solution.py:392
  1099.1 128.4 %reduce-scatter.40.cloned.1.call-start = ((), (), s32[]{:S(2)}) async-start(), calls=%async_computation.46 | async-start | bytes 2359296 | tf_op jit(solution)/shard_map/reduce_scatter | solution.py:446
  1102.1 161.1 %reduce-scatter.34.cloned.1.call-start = ((), (), s32[]{:S(2)}) async-start(), calls=%async_computation.43 | async-start | bytes 2359296 | tf_op jit(solution)/shard_map/reduce_scatter | solution.py:437
  1104.5 195.7 %reduce-scatter.36.cloned.1.call-start = ((), (), s32[]{:S(2)}) async-start(), calls=%async_computation.44 | async-start | bytes 2359296 | tf_op jit(solution)/shard_map/reduce_scatter | solution.py:440
  1106.7 230.2 %reduce-scatter.38.cloned.1.call-start = ((), (), s32[]{:S(2)}) async-start(), calls=%async_computation.45 | async-start | bytes 2359296 | tf_op jit(solution)/shard_map/reduce_scatter | solution.py:443
  1108.8 265.4 %reduce-scatter.28.cloned.1.call-start = ((), (), s32[]{:S(2)}) async-start(), calls=%async_computation.40 | async-start | bytes 2359296 | tf_op jit(solution)/shard_map/reduce_scatter | solution.py:422
  1110.9 300.5 %reduce-scatter.22.cloned.1.call-start = ((), (), s32[]{:S(2)}) async-start(), calls=%async_computation.37 | async-start | bytes 2359296 | tf_op jit(solution)/shard_map/reduce_scatter | solution.py:413
  1114.8 334.1 %reduce-scatter.24.cloned.1.call-start = ((), (), s32[]{:S(2)}) async-start(), calls=%async_computation.38 | async-start | bytes 2359296 | tf_op jit(solution)/shard_map/reduce_scatter | solution.py:416
  1142.7 50.6 %copy-start.8 = (f32[96,1024]{1,0:T(8,128)S(1)}, f32[96,1024]{1,0:T(8,128)}, u32[]{:S(2)}) copy-start(f32[96,1024]{1,0:T(8,128)} %copy-done.7) | copy-start | bytes 1179652
  1142.8 50.6 %copy-start.35 = (bf16[96,4096]{1,0:T(8,128)(2,1)S(1)}, bf16[96,4096]{1,0:T(8,128)(2,1)}, u32[]{:S(2)}) copy-start(bf16[96,4096]{1,0:T(8,128)(2,1)} %copy-done.34) | copy-start | bytes 2359300
  1142.8 50.6 %copy-start.57 = (f32[8,1,128]{2,1,0:T(1,128)S(1)}, f32[8,1,128]{2,1,0:T(1,128)}, u32[]{:S(2)}) copy-start(f32[8,1,128]{2,1,0:T(1,128)} %copy-done.56) | copy-start | bytes 12292
  1142.8 50.6 %copy-start.86 = (f32[96]{0:T(128)S(1)}, f32[96]{0:T(128)}, u32[]{:S(2)}) copy-start(f32[96]{0:T(128)} %copy-done.85) | copy-start | bytes 1156
  1142.8 343.7 %reduce-scatter.26.cloned.1.call-start = ((), (), s32[]{:S(2)}) async-start(), calls=%async_computation.39 | async-start | bytes 2359296 | tf_op jit(solution)/shard_map/reduce_scatter | solution.py:419
  1193.3 383.7 %reduce-scatter.42.cloned.1.call-start = ((), (), s32[]{:S(2)}) async-start(), calls=%async_computation.47 | async-start | bytes 9437184 | tf_op jit(solution)/shard_map/reduce_scatter | solution.py:452
  1199.2 468.2 %reduce-scatter.44.cloned.1.call-start = ((), (), s32[]{:S(2)}) async-start(), calls=%async_computation.48 | async-start | bytes 9437184 | tf_op jit(solution)/shard_map/reduce_scatter | solution.py:455
  1207.4 550.4 %reduce-scatter.30.cloned.1.call-start = ((), (), s32[]{:S(2)}) async-start(), calls=%async_computation.41 | async-start | bytes 9437184 | tf_op jit(solution)/shard_map/reduce_scatter | solution.py:428
  1216.0 632.0 %reduce-scatter.32.cloned.1.call-start = ((), (), s32[]{:S(2)}) async-start(), calls=%async_computation.42 | async-start | bytes 9437184 | tf_op jit(solution)/shard_map/reduce_scatter | solution.py:431
  1225.7 781.4 %all-reduce.19.cloned.1.call-start = ((), (), s32[]{:S(2)}) async-start(), calls=%async_computation.50 | async-start | bytes 13107200 | tf_op jit(solution)/shard_map/psum | solution.py:19
  1856.7 166.2 %copy-start.28 = (f32[256,1024]{1,0:T(8,128)S(1)}, f32[256,1024]{1,0:T(8,128)}, u32[]{:S(2)}) copy-start(f32[256,1024]{1,0:T(8,128)} %copy-done.27) | copy-start | bytes 3145732
  1856.7 166.2 %copy-start.89 = (s32[1,256]{1,0:T(1,128)S(1)}, s32[1,256]{1,0:T(1,128)}, u32[]{:S(2)}) copy-start(s32[1,256]{1,0:T(1,128)} %copy-done.87) | copy-start | bytes 3076
  1856.7 166.2 %copy-start.94 = (s32[256]{0:T(256)S(1)}, s32[256]{0:T(256)}, u32[]{:S(2)}) copy-start(s32[256]{0:T(256)} %copy-done.92) | copy-start | bytes 3076
  1861.6 167.4 %all-to-all-start.1 = ((bf16[4,2,32768]{2,1,0:T(2,128)(2,1)}), bf16[4,2,32768]{2,1,0:T(2,128)(2,1)S(1)}, u32[]{:S(2)}, u32[]{:S(2)}) async-start(bf16[4,2,32768]{2,1,0:T(2,128)(2,1)} %reshape.523), calls=%async_computation.4 | async-start | bytes 1048576 | tf_op jit(solution)/shard_map/all_to_all | solution.py:405
  2028.9 61.6 %all-to-all-start = ((bf16[4,2,32768]{2,1,0:T(2,128)(2,1)}), bf16[4,2,32768]{2,1,0:T(2,128)(2,1)S(1)}, u32[]{:S(2)}, u32[]{:S(2)}) async-start(bf16[4,2,32768]{2,1,0:T(2,128)(2,1)} %reshape.521), calls=%async_computation.1 | async-start | bytes 1048576 | tf_op jit(solution)/shard_map/all_to_all | solution.py:404
  (95 other events, 412.2 us)
Sparse Core Ops, SparseCore 0:
  9.6 31.7 all-gather.24
  43.1 28.5 all-gather.30
  73.3 28.5 all-gather.28
  104.0 46.6 all-gather.26
  152.7 45.8 all-gather.32
  200.0 27.8 all-gather.34
  229.5 81.5 all-gather.36
  312.6 80.5 all-gather.38
  404.1 30.7 reduce-scatter.15
  436.3 27.5 all-gather.46
  465.5 28.5 all-gather.40
  495.6 28.6 all-gather.44
  526.4 24.5 all-gather.48
  553.1 24.5 all-gather.42
  579.1 28.6 all-gather.50
  609.2 81.5 all-gather.52
  692.3 80.5 all-gather.54
  808.3 95.4 all-reduce.16
  912.3 42.9 all-reduce.14
  1089.2 50.1 reduce-scatter.17
  1141.8 48.1 reduce-scatter.19
  1192.3 33.9 reduce-scatter.39
  1228.8 34.4 reduce-scatter.33
  1265.5 34.6 reduce-scatter.35
  1302.6 34.2 reduce-scatter.37
  1339.7 34.4 reduce-scatter.27
  1377.0 34.4 reduce-scatter.21
  1414.4 34.4 reduce-scatter.23
  1451.9 34.5 reduce-scatter.25
  1488.7 88.2 reduce-scatter.41
  1579.4 87.9 reduce-scatter.43
  1669.8 87.9 reduce-scatter.29
  1760.1 87.9 reduce-scatter.31
  1855.7 151.4 all-reduce.18
where the time goes:
time: 2110 us; the launch traced here: 2100 us
  waiting for transfers between devices  1520 us (72%)
  matrix products  256 us (12%)
  blocking collectives  131 us (6%)
  local copies, waits for them, and re-layouts  115 us (5%)
  other arithmetic  52.9 us (3%)
    psum x2, waiting for transfers between devices, broadcast(): return lax.psum(kept, axis)  185 us
    unnamed x35, waiting for transfers between devices  96.5 us
    reduce_scatter x1, waiting for transfers between devices, on_device(): lax.psum_scatter(routed_outer[2].astype(jnp.bfloat16), 'dp', scatter_dime...  90.6 us
    reduce_scatter x1, waiting for transfers between devices, on_device(): lax.psum_scatter(routed_outer[3].astype(jnp.bfloat16), 'dp', scatter_dime...  90.4 us
    reduce_scatter x1, waiting for transfers between devices, on_device(): lax.psum_scatter(dense_outer[2].astype(jnp.bfloat16), 'dp', scatter_dimen...  90.4 us
    reduce_scatter x1, waiting for transfers between devices, on_device(): lax.psum_scatter(dense_outer[3].astype(jnp.bfloat16), 'dp', scatter_dimen...  90.2 us
    all_gather x1, waiting for transfers between devices, on_device(): lax.all_gather(routed_expand, 'dp', axis=0, tiled=True)  80.1 us
    all_gather x1, waiting for transfers between devices, on_device(): lax.all_gather(routed_shrink, 'dp', axis=0, tiled=True)  76 us
  transfers between devices with their start and end apart: 36, of which 31 were waited for; matrix products, arithmetic and copies ran while one was open for 11% of the time, Pallas kernels for 0%

commit v1 on v0

v1 whole, which is shorter than its diff:
```python
import functools

import jax
import jax.numpy as jnp
from jax import lax
from jax.experimental import pallas as pl
from jax.experimental.pallas import tpu as pltpu
from jax.sharding import PartitionSpec as P

HEADS = 16
HDIM = 64
DOCS = 8
EPS = 1e-06
NEG = -1e30
SCALE = HDIM ** (-0.5)
VMEM = 56 * 2**20
MESH = pl.DeviceIdType.MESH
BF = jnp.bfloat16
F32 = jnp.float32


def matmul(left, right):
    return jnp.dot(left, right, preferred_element_type=F32)


def contract(left, right, ldim, rdim):
    return lax.dot_general(left, right, (((ldim,), (rdim,)), ((), ())), preferred_element_type=F32)


class Line:
    def __init__(self, kind, dp, group):
        self.axis = "section" if kind == "section" else "dp"
        self.kind = kind
        self.stride = dp // group
        self.size = {"section": lax.axis_size("section"), "dp": dp, "z": group, "core": dp // group}[kind]

    def place(self):
        index = lax.axis_index(self.axis)
        if self.kind == "z":
            return index // self.stride
        if self.kind == "core":
            return lax.rem(index, self.stride)
        return index

    def coordinate(self, place):
        index = lax.axis_index(self.axis)
        if self.kind == "z":
            return place * self.stride + lax.rem(index, self.stride)
        if self.kind == "core":
            return (index // self.stride) * self.stride + place
        return place


def exchange_kernel(line, plan, n_in, n_out, *refs):
    ins, outs = refs[:n_in], refs[n_in : n_in + n_out]
    send, recv, local = refs[n_in + n_out :]
    count = line.size
    me = line.place()
    barrier = pltpu.get_barrier_semaphore()
    peers = [lax.rem(me + step, count) for step in range(1, count)]
    for peer in peers:
        pl.semaphore_signal(
            barrier, inc=1, device_id={line.axis: line.coordinate(peer)}, device_id_type=MESH
        )
    pl.semaphore_wait(barrier, count - 1)
    copies = []
    for step, peer in enumerate(peers):
        for item, (i, src, o, dst) in enumerate(plan):
            copy = pltpu.make_async_remote_copy(
                src_ref=src(ins[i], peer),
                dst_ref=dst(outs[o], me),
                send_sem=send.at[step, item],
                recv_sem=recv.at[step, item],
                device_id={line.axis: line.coordinate(peer)},
                device_id_type=MESH,
            )
            copy.start()
            copies.append(copy)
    for item, (i, src, o, dst) in enumerate(plan):
        copy = pltpu.make_async_copy(src(ins[i], me), dst(outs[o], me), local.at[item])
        copy.start()
        copies.append(copy)
    for copy in copies:
        copy.wait()


class Exchanger:
    def __init__(self, dp, group):
        self.dp, self.group, self.next_id = dp, group, 1

    def __call__(self, kind, arrays, shapes, plan, name):
        line = Line(kind, self.dp, self.group)
        ident = self.next_id
        self.next_id += 1
        if line.size == 1:
            return list(arrays)
        items = len(plan)
        return pl.pallas_call(
            functools.partial(exchange_kernel, line, plan, len(arrays), len(shapes)),
            out_shape=[jax.ShapeDtypeStruct(s, d) for s, d in shapes],
            in_specs=[pl.BlockSpec(memory_space=pl.ANY)] * len(arrays),
            out_specs=[pl.BlockSpec(memory_space=pl.ANY)] * len(shapes),
            scratch_shapes=[
                pltpu.SemaphoreType.DMA((line.size - 1, items)),
                pltpu.SemaphoreType.DMA((line.size - 1, items)),
                pltpu.SemaphoreType.DMA((items,)),
            ],
            compiler_params=pltpu.CompilerParams(collective_id=ident, has_side_effects=True),
            name=name,
        )(*arrays)


def whole(ref, place):
    return ref


def slot(ref, place):
    return ref.at[place]


def columns(width):
    def view(ref, place):
        return ref.at[:, pl.ds(pl.multiple_of(place * width, width), width)]

    return view


def middle(width):
    def view(ref, place):
        return ref.at[:, pl.ds(pl.multiple_of(place * width, width), width), :]

    return view


def gather_columns(swap, parts, name):
    size = lax.axis_size("section")
    shapes = [((p.shape[0], size * p.shape[1]), p.dtype) for p in parts]
    plan = [(i, whole, i, columns(p.shape[1])) for i, p in enumerate(parts)]
    return swap("section", parts, shapes, plan, name)


def scatter_columns(swap, part, extra, name):
    size = lax.axis_size("section")
    width = part.shape[1] // size
    arrays = [part] + ([] if extra is None else [extra])
    shapes = [((size, part.shape[0], width), part.dtype)]
    plan = [(0, columns(width), 0, slot)]
    if extra is not None:
        shapes.append(((size,) + extra.shape, extra.dtype))
        plan.append((1, whole, 1, slot))
    got = swap("section", arrays, shapes, plan, name)
    total = jnp.sum(got[0].astype(F32), axis=0)
    if extra is None:
        return total
    return total, jnp.sum(got[1].astype(F32), axis=0)


def unpack_low(packed):
    lane = lax.broadcasted_iota(jnp.int32, packed.shape, 1)
    zero = jnp.zeros_like(packed)
    low = jnp.where(lane < HDIM, packed, zero)
    turned = jnp.concatenate([packed[:, HDIM:], packed[:, :HDIM]], axis=1)
    high = jnp.where(lane < HDIM, turned, zero)
    return jnp.concatenate([low, high], axis=0)


def unpack_high(packed):
    lane = lax.broadcasted_iota(jnp.int32, packed.shape, 1)
    zero = jnp.zeros_like(packed)
    turned = jnp.concatenate([packed[:, HDIM:], packed[:, :HDIM]], axis=1)
    low = jnp.where(lane >= HDIM, turned, zero)
    high = jnp.where(lane >= HDIM, packed, zero)
    return jnp.concatenate([low, high], axis=0)


def pack_turned(turned):
    half = turned.shape[1] // 2
    return jnp.concatenate([turned[:, :half], turned[:, half:]], axis=0).T


def forward_block(query, pieces, qpos, start, causal):
    scores = []
    peak = None
    for index, (pair, _, first) in enumerate(pieces):
        item = contract(pair, query, 1, 1)
        kpos = first + lax.broadcasted_iota(jnp.int32, item.shape, 0)
        allowed = kpos >= start
        if causal[index]:
            allowed = allowed & (kpos <= qpos)
        item = jnp.where(allowed, item, NEG)
        top = jnp.max(item, axis=0, keepdims=True)
        peak = top if peak is None else jnp.maximum(peak, top)
        scores.append(item)
    total = jnp.zeros_like(peak)
    mixed = None
    for item, (_, turned, _) in zip(scores, pieces):
        weight = jnp.exp(item - peak)
        total = total + jnp.sum(weight, axis=0, keepdims=True)
        part = matmul(turned[HDIM:], weight.astype(BF))
        mixed = part if mixed is None else mixed + part
    return mixed / total, peak + jnp.log(total)


def backward_block(query, grad, grad_turned, mixed_turned, lse, pieces, qpos, start, causal):
    row_sum = jnp.sum(grad_turned.astype(F32) * mixed_turned.astype(F32), axis=0, keepdims=True)
    grad_query = None
    grads = []
    for index, (pair, turned, first) in enumerate(pieces):
        scores = contract(pair, query, 1, 1)
        kpos = first + lax.broadcasted_iota(jnp.int32, scores.shape, 0)
        allowed = kpos >= start
        if causal[index]:
            allowed = allowed & (kpos <= qpos)
        probs = jnp.where(allowed, jnp.exp(scores - lse), 0.0)
        grad_probs = contract(pair, grad, 1, 1)
        grad_scores = (probs * (grad_probs - row_sum)).astype(BF)
        grads.append(matmul(grad_scores, query) + matmul(probs.astype(BF), grad))
        part = matmul(turned[:HDIM], grad_scores)
        grad_query = part if grad_query is None else grad_query + part
    return grad_query * SCALE, grads


def dense_forward_kernel(place_ref, q_ref, kv_ref, start_ref, out_ref, turned_ref, lse_ref):
    group, _, half, _ = q_ref.shape
    ring, _, _, block, _ = kv_ref.shape
    place = place_ref[0]
    span = ring * block
    pieces = []
    for g in range(group):
        pair = kv_ref[:, g, 0].reshape(span, 2 * HDIM)
        pieces.append((pair, pair.T, g * span))
    for g in range(group):
        query = unpack_low(q_ref[g, 0]) * jnp.asarray(SCALE, BF)
        qpos = g * span + place * block + lax.broadcasted_iota(jnp.int32, (1, block), 1)
        mixed, lse = forward_block(
            query, pieces[: g + 1], qpos, start_ref[0, g], [i == g for i in range(g + 1)]
        )
        turned_ref[0, g] = mixed.astype(BF)
        lse_ref[0, g] = lse
        out_ref[g, 0] = pack_turned(mixed).astype(BF)


def dense_forward(place, q, kv, start):
    group, seqs, half, lanes = q.shape
    ring, _, _, block, _ = kv.shape
    grid = pltpu.PrefetchScalarGridSpec(
        num_scalar_prefetch=1,
        grid=(seqs,),
        in_specs=[
            pl.BlockSpec((group, 1, half, lanes), lambda s, _: (0, s, 0, 0)),
            pl.BlockSpec((ring, group, 1, block, lanes), lambda s, _: (0, 0, s, 0, 0)),
            pl.BlockSpec((1, group, 1, block), lambda s, _: (s, 0, 0, 0)),
        ],
        out_specs=[
            pl.BlockSpec((group, 1, half, lanes), lambda s, _: (0, s, 0, 0)),
            pl.BlockSpec((1, group, HDIM, block), lambda s, _: (s, 0, 0, 0)),
            pl.BlockSpec((1, group, 1, block), lambda s, _: (s, 0, 0, 0)),
        ],
    )
    return pl.pallas_call(
        dense_forward_kernel,
        grid_spec=grid,
        out_shape=[
            jax.ShapeDtypeStruct(q.shape, BF),
            jax.ShapeDtypeStruct((seqs, group, HDIM, block), BF),
            jax.ShapeDtypeStruct((seqs, group, 1, block), F32),
        ],
        compiler_params=pltpu.CompilerParams(vmem_limit_bytes=VMEM),
        name="dense_attention",
    )(place, q, kv, start)


def dense_backward_kernel(
    place_ref, q_ref, g_ref, kv_ref, start_ref, turned_ref, lse_ref, dq_ref, dkv_ref, acc_ref
):
    group, _, half, _ = q_ref.shape
    ring, _, _, block, _ = kv_ref.shape
    place = place_ref[0]
    span = ring * block
    pieces = []
    for g in range(group):
        pair = kv_ref[:, g, 0].reshape(span, 2 * HDIM)
        pieces.append((pair, pair.T, g * span))
    for g in reversed(range(group)):
        query = unpack_low(q_ref[g, 0]) * jnp.asarray(SCALE, BF)
        packed = g_ref[g, 0]
        grad = unpack_high(packed)
        flat = packed.T
        grad_turned = jnp.concatenate([flat[:HDIM], flat[HDIM:]], axis=1)
        qpos = g * span + place * block + lax.broadcasted_iota(jnp.int32, (1, block), 1)
        grad_query, grads = backward_block(
            query,
            grad,
            grad_turned,
            turned_ref[0, g],
            lse_ref[0, g],
            pieces[: g + 1],
            qpos,
            start_ref[0, g],
            [i == g for i in range(g + 1)],
        )
        dq_ref[g, 0] = pack_turned(grad_query).astype(BF)
        for i, item in enumerate(grads):
            if g == group - 1:
                acc_ref[i] = item
            else:
                acc_ref[i] += item
    for g in range(group):
        dkv_ref[:, g, 0] = acc_ref[g].reshape(ring, block, 2 * HDIM).astype(BF)


def dense_backward(place, q, grad, kv, start, turned, lse):
    group, seqs, half, lanes = q.shape
    ring, _, _, block, _ = kv.shape
    grid = pltpu.PrefetchScalarGridSpec(
        num_scalar_prefetch=1,
        grid=(seqs,),
        in_specs=[
            pl.BlockSpec((group, 1, half, lanes), lambda s, _: (0, s, 0, 0)),
            pl.BlockSpec((group, 1, half, lanes), lambda s, _: (0, s, 0, 0)),
            pl.BlockSpec((ring, group, 1, block, lanes), lambda s, _: (0, 0, s, 0, 0)),
            pl.BlockSpec((1, group, 1, block), lambda s, _: (s, 0, 0, 0)),
            pl.BlockSpec((1, group, HDIM, block), lambda s, _: (s, 0, 0, 0)),
            pl.BlockSpec((1, group, 1, block), lambda s, _: (s, 0, 0, 0)),
        ],
        out_specs=[
            pl.BlockSpec((group, 1, half, lanes), lambda s, _: (0, s, 0, 0)),
            pl.BlockSpec((ring, group, 1, block, lanes), lambda s, _: (0, 0, s, 0, 0)),
        ],
        scratch_shapes=[pltpu.VMEM((group, ring * block, lanes), F32)],
    )
    return pl.pallas_call(
        dense_backward_kernel,
        grid_spec=grid,
        out_shape=[
            jax.ShapeDtypeStruct(q.shape, BF),
            jax.ShapeDtypeStruct(kv.shape, BF),
        ],
        compiler_params=pltpu.CompilerParams(vmem_limit_bytes=VMEM),
        name="dense_attention_grad",
    )(place, q, grad, kv, start, turned, lse)


def routed_parts(place, q_ref, kv_ref, s):
    group, _, block, lanes = q_ref.shape
    ring = kv_ref.shape[0]
    span = ring * block
    query = jnp.concatenate([q_ref[g, s] for g in range(group)], axis=0)
    pair = jnp.concatenate([kv_ref[:, g, s].reshape(span, lanes) for g in range(group)], axis=0)
    index = lax.broadcasted_iota(jnp.int32, (1, group * block), 1)
    slots = (index // block) * span + place * block + lax.rem(index, block)
    return query, pair, slots


def routed_forward_kernel(place_ref, q_ref, kv_ref, start_ref, out_ref, turned_ref, lse_ref):
    group, seqs, block, lanes = q_ref.shape
    for s in range(seqs):
        query, pair, slots = routed_parts(place_ref[0], q_ref, kv_ref, s)
        query = query * jnp.asarray(SCALE, BF)
        mixed, lse = forward_block(query, [(pair, pair.T, 0)], slots, start_ref[s], [True])
        turned_ref[s] = mixed.astype(BF)
        lse_ref[s] = lse
        padded = jnp.concatenate([jnp.zeros_like(mixed), mixed], axis=0).T.astype(BF)
        for g in range(group):
            out_ref[g, s] = padded[g * block : (g + 1) * block]


def routed_forward(place, q, kv, start):
    group, seqs, block, lanes = q.shape
    queries = group * block
    vmem = pl.BlockSpec(memory_space=pltpu.VMEM)
    return pl.pallas_call(
        routed_forward_kernel,
        in_specs=[pl.BlockSpec(memory_space=pltpu.SMEM)] + [vmem] * 3,
        out_specs=[vmem] * 3,
        out_shape=[
            jax.ShapeDtypeStruct(q.shape, BF),
            jax.ShapeDtypeStruct((seqs, HDIM, queries), BF),
            jax.ShapeDtypeStruct((seqs, 1, queries), F32),
        ],
        compiler_params=pltpu.CompilerParams(vmem_limit_bytes=VMEM),
        name="routed_attention",
    )(place, q, kv, start)


def routed_backward_kernel(
    place_ref, q_ref, g_ref, kv_ref, start_ref, turned_ref, lse_ref, dq_ref, dkv_ref
):
    group, seqs, block, lanes = q_ref.shape
    ring = kv_ref.shape[0]
    span = ring * block
    for s in range(seqs):
        query, pair, slots = routed_parts(place_ref[0], q_ref, kv_ref, s)
        query = query * jnp.asarray(SCALE, BF)
        grad = jnp.concatenate([g_ref[g, s] for g in range(group)], axis=0)
        grad_query, grads = backward_block(
            query,
            grad,
            grad.T[HDIM:],
            turned_ref[s],
            lse_ref[s],
            [(pair, pair.T, 0)],
            slots,
            start_ref[s],
            [True],
        )
        padded = jnp.concatenate([grad_query, jnp.zeros_like(grad_query)], axis=0).T.astype(BF)
        for g in range(group):
            dq_ref[g, s] = padded[g * block : (g + 1) * block]
            dkv_ref[:, g, s] = (
                grads[0][g * span : (g + 1) * span].reshape(ring, block, lanes).astype(BF)
            )


def routed_backward(place, q, grad, kv, start, turned, lse):
    vmem = pl.BlockSpec(memory_space=pltpu.VMEM)
    return pl.pallas_call(
        routed_backward_kernel,
        in_specs=[pl.BlockSpec(memory_space=pltpu.SMEM)] + [vmem] * 6,
        out_specs=[vmem] * 2,
        out_shape=[
            jax.ShapeDtypeStruct(q.shape, BF),
            jax.ShapeDtypeStruct(kv.shape, BF),
        ],
        compiler_params=pltpu.CompilerParams(vmem_limit_bytes=VMEM),
        name="routed_attention_grad",
    )(place, q, grad, kv, start, turned, lse)


def inverse_rms(value):
    return lax.rsqrt(jnp.mean(value * value, axis=-1, keepdims=True) + EPS)


def row_scalars(values, width):
    rows = values.reshape(-1, width) if values.shape[0] >= width else jnp.pad(values, (0, width - values.shape[0]))[None]
    high = rows.astype(BF)
    low = (rows - high.astype(F32)).astype(BF)
    both = jnp.concatenate([high, low], axis=0)
    return jnp.pad(both, ((0, -both.shape[0] % 16), (0, 0)))


def read_scalars(rows, count):
    width = rows.shape[1]
    used = max(1, count // width)
    return (rows[:used] + rows[used : 2 * used]).reshape(-1)[:count]


def on_device(
    stream_in,
    segment_ids,
    chosen_rows,
    cotangent,
    dense_prenorm,
    dense_query,
    dense_keys,
    dense_values,
    dense_output,
    dense_midnorm,
    dense_expand,
    dense_shrink,
    routed_prenorm,
    routed_query,
    routed_keys,
    routed_values,
    routed_output,
    routed_midnorm,
    routed_expand,
    routed_shrink,
    router_weight,
):
    sections, dp = lax.axis_size("section"), lax.axis_size("dp")
    section, rank = lax.axis_index("section"), lax.axis_index("dp")
    seqs, rows, width = stream_in.shape
    tokens = seqs * rows
    part = width // sections
    group = HEADS // sections
    ring = dp // group
    total_sel = chosen_rows.shape[1]
    sel = total_sel // dp
    slots = seqs * sel
    place = lax.rem(rank, ring).astype(jnp.int32).reshape(1)
    swap = Exchanger(dp, group)

    def own_columns(value):
        return lax.dynamic_slice_in_dim(value, section * part, part, value.ndim - 1)

    def own_hidden(expand, shrink):
        inner = expand.shape[1] // dp
        share = inner // sections
        cut = expand.reshape(expand.shape[0], dp, sections, share)
        cut = lax.dynamic_index_in_dim(cut, section, 2, keepdims=False).reshape(expand.shape[0], dp * share)
        return cut, lax.dynamic_slice_in_dim(shrink, section * share, share, 0)

    def own_attention(query, keys, values):
        local = query.shape[0]
        pair = jnp.stack(
            [own_columns(keys).reshape(local, group, HDIM), own_columns(values).reshape(local, group, HDIM)],
            axis=2,
        ).reshape(local, 2 * part)
        return jnp.concatenate([pair, own_columns(query)], axis=1)

    def gather(value):
        return lax.all_gather(value, "dp", axis=0, tiled=True)

    def layer_weights(query, keys, values, output, expand, shrink):
        expand_cut, shrink_cut = own_hidden(expand, shrink)
        qkv = gather(own_attention(query, keys, values))
        out = gather(own_columns(output))
        return qkv, out, gather(expand_cut), gather(shrink_cut)

    dense = layer_weights(dense_query, dense_keys, dense_values, dense_output, dense_expand, dense_shrink)
    routed = layer_weights(
        routed_query, routed_keys, routed_values, routed_output, routed_expand, routed_shrink
    )
    gains = jnp.stack([dense_prenorm, dense_midnorm, routed_prenorm, routed_midnorm, router_weight])
    gains = jnp.pad(gains, ((0, 16 - gains.shape[0]), (0, 0)))
    (gains,) = swap("dp", [gains], [((dp,) + gains.shape, BF)], [(0, whole, 0, slot)], "gains")
    gains = jnp.transpose(gains, (1, 0, 2)).reshape(16, width).astype(F32)
    gain_pre, gain_mid, routed_pre, routed_mid, router = [gains[i] for i in range(5)]

    first_of = jnp.sum(
        (segment_ids[:, None, :] < jnp.arange(DOCS, dtype=jnp.int32)[None, :, None]).astype(jnp.int32), axis=2
    )

    def document(positions):
        shape = (seqs,) + (1,) * (positions.ndim - 1)
        found = jnp.zeros(positions.shape, jnp.int32)
        for c in range(1, DOCS):
            found = found + (positions >= first_of[:, c].reshape(shape)).astype(jnp.int32)
        return found

    def pick(table, index):
        shape = (seqs,) + (1,) * (index.ndim - 1)
        out = jnp.zeros(index.shape, jnp.int32)
        for c in range(DOCS):
            out = jnp.where(index == c, table[:, c].reshape(shape), out)
        return out

    blocks = jnp.arange(group, dtype=jnp.int32) * ring + place[0]
    attended_pos = blocks[:, None] * rows + jnp.arange(rows, dtype=jnp.int32)[None, :]
    attended_pos = jnp.broadcast_to(attended_pos[None], (seqs, group, rows))
    start = pick(first_of, document(attended_pos))[:, :, None, :]
    chosen_doc = document(chosen_rows)
    first_slot = jnp.sum(
        (chosen_doc[:, None, :] < jnp.arange(DOCS, dtype=jnp.int32)[None, :, None]).astype(jnp.int32), axis=2
    )
    chosen_start = pick(first_slot, chosen_doc).reshape(seqs, group, ring, sel)
    routed_start = lax.dynamic_index_in_dim(chosen_start, place[0], 2, keepdims=False)
    routed_start = routed_start.reshape(seqs, 1, group * sel)

    def pack(value):
        value = value.reshape(seqs, 2, rows // 2, group, HDIM)
        return jnp.transpose(value, (0, 2, 3, 1, 4)).reshape(tokens // 2, 2 * part)

    def unpack(value):
        value = value.reshape(seqs, rows // 2, group, 2, HDIM)
        return jnp.transpose(value, (0, 3, 1, 2, 4)).reshape(tokens, part)

    lanes = 2 * HDIM

    def to_heads(arrays, name):
        shapes = [((group, a.shape[0], lanes), a.dtype) for a in arrays]
        plan = [(i, columns(lanes), i, slot) for i in range(len(arrays))]
        return swap("z", arrays, shapes, plan, name)

    def from_heads(arrays, name):
        shapes = [((a.shape[1], group * lanes), a.dtype) for a in arrays]
        plan = [(i, slot, i, columns(lanes)) for i in range(len(arrays))]
        return swap("z", arrays, shapes, plan, name)

    def share_pairs(kv, name):
        if ring == 1:
            return kv[None]
        (kv,) = swap("core", [kv], [((ring,) + kv.shape, kv.dtype)], [(0, whole, 0, slot)], name)
        return kv

    def sum_pairs(kv, name):
        if ring == 1:
            return kv[0]
        (kv,) = swap("core", [kv], [(kv.shape, kv.dtype)], [(0, slot, 0, slot)], name)
        return jnp.sum(kv.astype(F32), axis=0).astype(BF)

    value = stream_in.reshape(tokens, width).astype(F32)
    grad_top = cotangent.reshape(tokens, width)
    inv_in = inverse_rms(value)
    normed = (value * inv_in * gain_pre).astype(BF)
    qkv = matmul(normed, dense[0]).astype(BF)
    pairs, queries = qkv[:, : 2 * part], pack(qkv[:, 2 * part :])
    pairs, queries = to_heads([pairs, queries], "dense_to_heads")
    queries = queries.reshape(group, seqs, rows // 2, lanes)
    pairs = share_pairs(pairs, "dense_pairs").reshape(ring, group, seqs, rows, lanes)
    mixed, mixed_turned, lse = dense_forward(place, queries, pairs, start)
    (mixed,) = from_heads([mixed.reshape(group, tokens // 2, lanes)], "dense_mixed")
    mixed = unpack(mixed)
    (mixed,) = gather_columns(swap, [mixed], "dense_mixed_columns")
    attended = matmul(mixed, dense[1]).astype(BF)
    (attended,) = gather_columns(swap, [attended], "dense_attended")
    middle_value = value + attended.astype(F32)
    inv_mid = inverse_rms(middle_value)
    normed_mid = (middle_value * inv_mid * gain_mid).astype(BF)
    hidden_pre = matmul(normed_mid, dense[2])
    hidden = jax.nn.gelu(hidden_pre).astype(BF)
    fed = scatter_columns(swap, matmul(hidden, dense[3]).astype(BF), None, "dense_fed")
    middle_own = own_columns(middle_value)
    after_dense = middle_own + fed

    qpos = rank * rows + jnp.arange(rows, dtype=jnp.int32)
    table = (chosen_rows[:, :, None] == qpos[None, None, :]).astype(BF)

    def take_rows(source, name):
        picked = jnp.einsum(
            "skt,stc->skc", table, source.reshape(seqs, rows, part), preferred_element_type=F32
        ).astype(BF)
        (got,) = swap(
            "dp", [picked], [((dp, seqs, sel, part), BF)], [(0, middle(sel), 0, slot)], name + "_slots"
        )
        got = jnp.sum(got.astype(F32), axis=0).astype(BF).reshape(slots, part)
        (got,) = gather_columns(swap, [got], name + "_columns")
        return got

    grad_sent = take_rows(own_columns(grad_top), "grad_rows").astype(F32)
    picked = take_rows(after_dense.astype(BF), "value_rows").astype(F32)

    def routed_to_heads(arrays, name):
        return [a.reshape(group, seqs, sel, lanes) for a in to_heads(arrays, name)]

    def spread(value, side):
        value = value.reshape(slots, group, HDIM)
        zero = jnp.zeros_like(value)
        both = [value, zero] if side == 0 else [zero, value]
        return jnp.stack(both, axis=2).reshape(slots, 2 * part)

    def narrow(value, side):
        return value.reshape(slots, group, 2, HDIM)[:, :, side].reshape(slots, part)

    r_inv_in = inverse_rms(picked)
    r_normed = (picked * r_inv_in * routed_pre).astype(BF)
    r_qkv = matmul(r_normed, routed[0]).astype(BF)
    r_pairs, r_queries = routed_to_heads(
        [r_qkv[:, : 2 * part], spread(r_qkv[:, 2 * part :], 0)], "routed_to_heads"
    )
    r_pairs = share_pairs(r_pairs, "routed_pairs")
    r_mixed, r_turned, r_lse = routed_forward(place, r_queries, r_pairs, routed_start)
    (r_mixed,) = from_heads([r_mixed.reshape(group, slots, lanes)], "routed_mixed")
    (r_mixed,) = gather_columns(swap, [narrow(r_mixed, 1)], "routed_mixed_columns")
    r_attended_own = matmul(r_mixed, routed[1])
    (r_attended,) = gather_columns(swap, [r_attended_own.astype(BF)], "routed_attended")
    r_middle = picked + r_attended.astype(F32)
    r_inv_mid = inverse_rms(r_middle)
    r_normed_mid = (r_middle * r_inv_mid * routed_mid).astype(BF)
    r_hidden_pre = matmul(r_normed_mid, routed[2])
    r_hidden = jax.nn.gelu(r_hidden_pre).astype(BF)
    gate = jax.nn.sigmoid(jnp.sum(picked * router, axis=1))
    r_fed_part = matmul(r_hidden, routed[3])
    own_attended_part = jnp.sum(own_columns(grad_sent) * r_attended_own, axis=1)
    gate_part = jnp.sum(grad_sent * r_fed_part, axis=1) + own_attended_part
    r_fed, gate_rows = scatter_columns(swap, r_fed_part.astype(BF), row_scalars(gate_part, part), "routed_fed")
    delta_own = r_attended_own + r_fed
    sent_own = (gate[:, None] * delta_own).astype(BF)
    grad_gate = read_scalars(gate_rows, slots)
    grad_logit = grad_gate * gate * (1.0 - gate)
    grad_delta = gate[:, None] * grad_sent
    grad_router = jnp.sum(grad_logit[:, None] * own_columns(picked), axis=0)

    def back_out(kept, weights, gain, grad_fed, extra_middle, extra_attended, names):
        mixed_all, middle_all, inv, normed_all, pre, hid = kept
        count = middle_all.shape[0]
        fed_low = grad_fed.astype(BF)
        grad_shrink = contract(hid, fed_low, 0, 0).astype(BF)
        grad_hidden = contract(fed_low, weights[3], 1, 1)
        _, gelu_pull = jax.vjp(jax.nn.gelu, pre)
        grad_pre = gelu_pull(grad_hidden)[0].astype(BF)
        grad_expand = contract(normed_all, grad_pre, 0, 0).astype(BF)
        grad_normed = contract(grad_pre, weights[2], 1, 1)
        scalar = jnp.sum(grad_normed * middle_all * gain, axis=1)
        grad_normed, scalar = scatter_columns(
            swap, grad_normed.astype(BF), row_scalars(scalar, part), names[0]
        )
        scalar = read_scalars(scalar, count)[:, None] * (1.0 / width)
        own = own_columns(middle_all)
        grad_gain = jnp.sum(grad_normed * own * inv, axis=0)
        grad_middle = inv * (grad_normed * own_columns(gain)) - own * (inv * inv * inv) * scalar
        grad_middle = grad_middle + extra_middle
        grad_attended = (grad_middle + extra_attended).astype(BF)
        grad_output = contract(mixed_all, grad_attended, 0, 0).astype(BF)
        grad_mixed = contract(grad_attended, weights[1], 1, 1).astype(BF)
        grad_mixed = scatter_columns(swap, grad_mixed, None, names[1]).astype(BF)
        return grad_middle, grad_mixed, (grad_output, grad_gain, grad_expand, grad_shrink)

    def back_in(value_all, inv, normed_all, weights, gain, grad_qkv, name):
        count = value_all.shape[0]
        grad_weights = contract(normed_all, grad_qkv, 0, 0).astype(BF)
        grad_normed = contract(grad_qkv, weights[0], 1, 1)
        scalar = jnp.sum(grad_normed * value_all * gain, axis=1)
        grad_normed, scalar = scatter_columns(swap, grad_normed.astype(BF), row_scalars(scalar, part), name)
        scalar = read_scalars(scalar, count)[:, None] * (1.0 / width)
        own = own_columns(value_all)
        grad_gain = jnp.sum(grad_normed * own * inv, axis=0)
        grad_value = inv * (grad_normed * own_columns(gain)) - own * (inv * inv * inv) * scalar
        return grad_value, grad_gain, grad_weights

    def reduce_dp(value):
        return lax.psum_scatter(value, "dp", scatter_dimension=0, tiled=True)

    own_grad_delta = own_columns(grad_delta)
    r_grad_middle, r_grad_mixed, r_outer = back_out(
        (r_mixed, r_middle, r_inv_mid, r_normed_mid, r_hidden_pre, r_hidden),
        routed,
        routed_mid,
        grad_delta,
        0.0,
        own_grad_delta,
        ("routed_back_mid", "routed_back_mixed"),
    )
    (r_grad_heads,) = routed_to_heads([spread(r_grad_mixed, 1)], "routed_grad_to_heads")
    r_dq, r_dkv = routed_backward(
        place, r_queries, r_grad_heads, r_pairs, routed_start, r_turned, r_lse
    )
    r_dkv = sum_pairs(r_dkv, "routed_pair_grads")
    r_dq, r_dkv = from_heads(
        [r_dq.reshape(group, slots, lanes), r_dkv.reshape(group, slots, lanes)], "routed_grad_tokens"
    )
    r_grad_qkv = jnp.concatenate([r_dkv, narrow(r_dq, 0)], axis=1)
    r_grad_in, r_grad_pre, r_grad_qkv_w = back_in(
        picked, r_inv_in, r_normed, routed, routed_pre, r_grad_qkv, "routed_back_in"
    )
    grad_chosen = (r_grad_middle + r_grad_in + grad_logit[:, None] * own_columns(router)).astype(BF)

    def to_positions(value, name):
        cols = value.shape[1]
        (got,) = swap(
            "z",
            [value.reshape(seqs, sel, cols)],
            [((group, seqs, sel, cols), BF)],
            [(0, whole, 0, slot)],
            name + "_z",
        )
        got = share_pairs(got, name + "_core").reshape(ring, group, seqs, sel, cols)
        got = jnp.transpose(got, (2, 1, 0, 3, 4)).reshape(seqs, total_sel, cols)
        return jnp.einsum("skt,skc->stc", table, got, preferred_element_type=F32).reshape(tokens, cols)

    (grad_chosen_all,) = gather_columns(swap, [grad_chosen], "grad_chosen_columns")
    returned = to_positions(grad_chosen_all, "grad_chosen")
    added = to_positions(sent_own, "sent")
    stream_out = (after_dense + added).astype(BF).reshape(seqs, rows, part)

    grad_after = grad_top.astype(F32) + returned
    grad_middle, grad_mixed, outer = back_out(
        (mixed, middle_value, inv_mid, normed_mid, hidden_pre, hidden),
        dense,
        gain_mid,
        grad_after,
        own_columns(grad_after),
        0.0,
        ("dense_back_mid", "dense_back_mixed"),
    )
    (grad_heads,) = to_heads([pack(grad_mixed)], "dense_grad_to_heads")
    dq, dkv = dense_backward(
        place,
        queries,
        grad_heads.reshape(group, seqs, rows // 2, lanes),
        pairs,
        start,
        mixed_turned,
        lse,
    )
    dkv = sum_pairs(dkv, "dense_pair_grads")
    dq, dkv = from_heads(
        [dq.reshape(group, tokens // 2, lanes), dkv.reshape(group, tokens, lanes)], "dense_grad_tokens"
    )
    grad_qkv = jnp.concatenate([dkv, unpack(dq)], axis=1)
    grad_in, grad_pre, grad_qkv_w = back_in(
        value, inv_in, normed, dense, gain_pre, grad_qkv, "dense_back_in"
    )
    stream_grad = (grad_middle + grad_in).astype(BF).reshape(seqs, rows, part)

    def finish(grad_qkv_weight, outer_grads, name):
        grad_output, _, grad_expand, grad_shrink = outer_grads
        shards = [reduce_dp(g) for g in (grad_qkv_weight, grad_output, grad_expand, grad_shrink)]
        got_qkv, got_out, got_expand, got_shrink = swap(
            "section",
            shards,
            [
                ((sections,) + shards[0].shape, BF),
                ((shards[1].shape[0], width), BF),
                ((sections,) + shards[2].shape, BF),
                ((sections,) + shards[3].shape, BF),
            ],
            [(0, whole, 0, slot), (1, whole, 1, columns(part)), (2, whole, 2, slot), (3, whole, 3, slot)],
            name,
        )
        local = got_qkv.shape[1]
        pair = got_qkv[:, :, : 2 * part].reshape(sections, local, group, 2, HDIM)
        keys = jnp.transpose(pair[:, :, :, 0], (1, 0, 2, 3)).reshape(local, width).astype(F32)
        values = jnp.transpose(pair[:, :, :, 1], (1, 0, 2, 3)).reshape(local, width).astype(F32)
        query = jnp.transpose(got_qkv[:, :, 2 * part :], (1, 0, 2)).reshape(local, width).astype(F32)
        share = got_shrink.shape[1]
        expand = got_expand.reshape(sections, local, dp, share)
        expand = jnp.transpose(expand, (1, 2, 0, 3)).reshape(local, sections * dp * share).astype(F32)
        shrink = got_shrink.reshape(sections * share, width).astype(F32)
        return query, keys, values, got_out.astype(F32), expand, shrink

    routed_grads = finish(r_grad_qkv_w, r_outer, "routed_weight_grads")
    dense_grads = finish(grad_qkv_w, outer, "dense_weight_grads")

    vectors = jnp.stack([grad_pre, outer[1], r_grad_pre, r_outer[1], grad_router])
    vectors = jnp.pad(vectors, ((0, 8 - vectors.shape[0]), (0, 0)))
    (vectors,) = gather_columns(swap, [vectors], "vector_columns")
    vectors = jnp.transpose(vectors.reshape(8, dp, width // dp), (1, 0, 2))
    (vectors,) = swap("dp", [vectors], [(vectors.shape, F32)], [(0, slot, 0, slot)], "vector_shards")
    vectors = jnp.sum(vectors, axis=0)
    return (
        stream_out,
        stream_grad,
        vectors[0],
        dense_grads[0],
        dense_grads[1],
        dense_grads[2],
        dense_grads[3],
        vectors[1],
        dense_grads[4],
        dense_grads[5],
        vectors[2],
        routed_grads[0],
        routed_grads[1],
        routed_grads[2],
        routed_grads[3],
        vectors[3],
        routed_grads[4],
        routed_grads[5],
        vectors[4],
    )


def solution(mesh):
    streams, row, vector, copied = P(None, "dp", None), P("dp", None), P("dp"), P()
    layer = (vector, row, row, row, row, vector, row, row)
    outs = (P(None, "dp", "section"),) * 2 + layer + layer + (vector,)
    return jax.shard_map(
        on_device,
        mesh=mesh,
        in_specs=(streams, copied, copied, streams) + layer + layer + (vector,),
        out_specs=outs,
        check_vma=False,
    )
```

time: 2110 us -> 993 us (0.47)
  waiting for transfers between devices: 1520 us -> 129 us
  Pallas kernels: 0 us -> 588 us
  matrix products: 256 us -> 74.2 us
  blocking collectives: 131 us -> 35.4 us
  local copies, waits for them, and re-layouts: 115 us -> 77 us
    pallas_call x0 -> x42, Pallas kernels: none -> 588 us  [the longest x38 557 us: __call__(): pl.pallas_call(functools.partial(exchange_kernel, line, plan, len(arrays)...]
    reduce_scatter x15 -> x8, waiting for transfers between devices: 712 us -> 128 us  [reduce_dp(): return lax.psum_scatter(value, 'dp', scatter_dimension=0, tiled=True)]
    all_gather x16 -> x6, waiting for transfers between devices: 522 us -> 0.01 us  [gather(): return lax.all_gather(value, 'dp', axis=0, tiled=True)]
    psum x2 -> x0, waiting for transfers between devices: 185 us -> none  [broadcast(): return lax.psum(kept, axis)]
    dot_general x61 -> x28, matrix products: 256 us -> 74.2 us  [the longest x16 42.3 us: contract(): lax.dot_general(left, right, (((ldim,), (rdim,)), ((), ())), preferred_el...]
    unnamed x35 -> x14, waiting for transfers between devices: 96.5 us -> 0.23 us
    all_gather x8 -> x2, blocking collectives: 92.1 us -> 35.4 us  [gather(): return lax.all_gather(value, 'dp', axis=0, tiled=True)]
    unnamed x1 -> x0, blocking collectives: 29.3 us -> none
  transfers between devices with their start and end apart: 36 -> 14, of which waited for: 31 -> 4; matrix products, arithmetic and copies ran while one was open for 11% -> 13% of each run, Pallas kernels for 0% -> 43%
where the time goes in v1:
time: 993 us; the launch traced here: 983 us
  Pallas kernels  588 us (59%)
  waiting for transfers between devices  129 us (13%)
  local copies, waits for them, and re-layouts  77 us (8%)
  matrix products  74.2 us (7%)
  other arithmetic  63.8 us (6%)
  blocking collectives  35.4 us (4%)
  between operations  16.1 us (2%)
    pallas_call x38, Pallas kernels, __call__(): pl.pallas_call(functools.partial(exchange_kernel, line, plan, len(arrays)...  557 us
    reduce_scatter x8, waiting for transfers between devices, reduce_dp(): return lax.psum_scatter(value, 'dp', scatter_dimension=0, tiled=True)  128 us
    dot_general x16, matrix products, contract(): lax.dot_general(left, right, (((ldim,), (rdim,)), ((), ())), preferred_el...  42.3 us
    all_gather x2, blocking collectives, gather(): return lax.all_gather(value, 'dp', axis=0, tiled=True)  35.4 us
    dot_general x8, matrix products, matmul(): return jnp.dot(left, right, preferred_element_type=F32)  28.4 us
  transfers between devices with their start and end apart: 14, of which 4 were waited for; matrix products, arithmetic and copies ran while one was open for 13% of the time, Pallas kernels for 43%

profile of v1, /device:TPU:0, one launch (start us, length us, event | category | flops | bytes accessed | tf_op | source)
XLA Modules:
  0.0 983.3 jit_solution(15758673540776142142)
XLA Ops:
  20.7 7.9 gains.1
  31.7 17.0 %all_gather.25 = bf16[1024,256]{1,0:T(8,128)(2,1)} all-gather(bf16[128,256]{1,0:T(8,128)(2,1)S(1)} %constant_dynamic-slice_fusion.15), channel_id=1, replica_groups=mesh['section'=4,'dp'=8] {'dp'}, dimensions={0}, use_global_device_ids=true | all-gather | bytes 589824 | tf_op jit(solution)/shard_map/all_gather | solution.py:503
  51.1 13.9 %grad_rows_slots.1 = bf16[8,3,32,256]{3,2,1,0:T(8,128)(2,1)} custom-call(bf16[3,256,256]{2,1,0:T(8,128)(2,1)} %fusion.18.refs_0_), custom_call_target="tpu_custom_call" | custom-call | tf_op jit(solution)/shard_map/grad_rows_slots/pallas_call | solution.py:98
  66.6 8.1 grad_rows_columns.1
  78.7 18.3 %all_gather.29 = bf16[1024,256]{1,0:T(8,128)(2,1)S(1)} all-gather(bf16[128,256]{1,0:T(8,128)(2,1)S(1)} %constant_dynamic-slice_fusion.8), channel_id=1, replica_groups=mesh['section'=4,'dp'=8] {'dp'}, dimensions={0}, use_global_device_ids=true | all-gather | bytes 589824 | tf_op jit(solution)/shard_map/all_gather | solution.py:503
  100.5 3.3 convolution_convert_fusion.8
  107.2 29.0 %dense_to_heads.1 = (bf16[4,768,128]{2,1,0:T(8,128)(2,1)}, bf16[4,384,128]{2,1,0:T(8,128)(2,1)}) custom-call(bf16[768,512]{1,0:T(8,128)(2,1)} %slice.253.refs_0_, bf16[384,512]{1,0:T(8,128)(2,1)} %reshape.618.refs_1_), custom_call_target="tpu_custom_call" | custom-call | tf_op jit(solution)/shard_map/dense_to_heads/pallas_call | solution.py:98
  136.2 25.0 %dense_pairs.1 = bf16[2,4,768,128]{3,2,1,0:T(8,128)(2,1)} custom-call(bf16[4,768,128]{2,1,0:T(8,128)(2,1)} %get-tuple-element.56.refs_0_), custom_call_target="tpu_custom_call" | custom-call | tf_op jit(solution)/shard_map/dense_pairs/pallas_call | solution.py:98
  161.2 10.9 %dense_attention.1 = (bf16[4,3,128,128]{3,2,1,0:T(8,128)(2,1)}, bf16[3,4,64,256]{3,2,1,0:T(8,128)(2,1)}, f32[3,4,1,256]{3,2,1,0:T(1,128)}) custom-call(s32[1]{0:T(128)} %bitcast.1.place_ref, bf16[4,3,128,128]{3,2,1,0:T(8,128)(2,1)} %bitcast.253, bf16[2,4,3,256,128]{4,3,2,1,0:T(8,128)(2,1)} %bitcast.233, s32[3,4,1,256]{3,2,1,0:T(1,128)} %compare_select_fusion.7.start_ref), custom_call_target="tpu_custom_call" | custom-call | tf_op jit(solution)/shard_map/dense_attention/pallas_call | solution.py:260
  172.2 23.7 %dense_mixed.1 = bf16[384,512]{1,0:T(8,128)(2,1)} custom-call(bf16[4,384,128]{2,1,0:T(8,128)(2,1)} %bitcast.272), custom_call_target="tpu_custom_call" | custom-call | tf_op jit(solution)/shard_map/dense_mixed/pallas_call | solution.py:98
  201.4 21.1 %dense_mixed_columns.1 = bf16[768,1024]{1,0:T(8,128)(2,1)} custom-call(bf16[768,256]{1,0:T(8,128)(2,1)} %reshape.619.refs_0_), custom_call_target="tpu_custom_call" | custom-call | tf_op jit(solution)/shard_map/dense_mixed_columns/pallas_call | solution.py:98
  222.5 2.8 convolution_convert_fusion.11.refs_0_
  225.4 20.8 %dense_attended.1 = bf16[768,1024]{1,0:T(8,128)(2,1)} custom-call(bf16[768,256]{1,0:T(8,128)(2,1)} %convolution_convert_fusion.11.refs_0_), custom_call_target="tpu_custom_call" | custom-call | tf_op jit(solution)/shard_map/dense_attended/pallas_call | solution.py:98
  246.1 3.5 multiply_reduce_fusion.2
  250.3 6.1 fusion.100
  256.3 5.7 convolution_convert_fusion.7.refs_0_
  262.1 19.0 %dense_fed.1 = bf16[4,768,256]{2,1,0:T(8,128)(2,1)} custom-call(bf16[768,1024]{1,0:T(8,128)(2,1)} %convolution_convert_fusion.7.refs_0_), custom_call_target="tpu_custom_call" | custom-call | tf_op jit(solution)/shard_map/dense_fed/pallas_call | solution.py:98
  285.3 13.7 %value_rows_slots.1 = bf16[8,3,32,256]{3,2,1,0:T(8,128)(2,1)} custom-call(bf16[3,256,256]{2,1,0:T(8,128)(2,1)} %fusion.15.refs_0_), custom_call_target="tpu_custom_call" | custom-call | tf_op jit(solution)/shard_map/value_rows_slots/pallas_call | solution.py:98
  300.7 6.7 value_rows_columns.1
  314.9 9.3 routed_to_heads.1
  324.2 4.2 routed_pairs.1.kv_ref
  330.7 7.0 routed_mixed.1
  339.4 5.9 routed_mixed_columns.1
  347.3 5.9 routed_attended.1
  354.9 3.2 fusion.98
  358.2 3.0 multiply_reduce_fusion.7
  361.9 6.1 routed_fed.1
  374.6 6.1 routed_back_mid.1
  384.6 5.9 routed_back_mixed.1
  392.4 6.5 routed_grad_to_heads.1
  401.5 4.2 routed_pair_grads.1
  407.3 8.7 routed_grad_tokens.1
  420.5 6.4 routed_back_in.1
  431.1 5.9 grad_chosen_columns.1
  437.0 16.0 %grad_chosen_z.1.refs_0_ = bf16[4,3,32,1024]{3,2,1,0:T(8,128)(2,1)} custom-call(bf16[3,32,1024]{2,1,0:T(8,128)(2,1)} %bitcast.266), custom_call_target="tpu_custom_call" | custom-call | tf_op jit(solution)/shard_map/grad_chosen_z/pallas_call | solution.py:98
  453.1 25.0 %grad_chosen_core.1 = bf16[2,4,3,32,1024]{4,3,2,1,0:T(8,128)(2,1)} custom-call(bf16[4,3,32,1024]{3,2,1,0:T(8,128)(2,1)} %grad_chosen_z.1.refs_0_), custom_call_target="tpu_custom_call" | custom-call | tf_op jit(solution)/shard_map/grad_chosen_core/pallas_call | solution.py:98
  483.6 3.6 fusion.6
  487.3 3.1 multiply_reduce_fusion.1
  490.9 21.3 %dense_back_mid.1 = (bf16[4,768,256]{2,1,0:T(8,128)(2,1)}, bf16[4,16,256]{2,1,0:T(8,128)(2,1)}) custom-call(bf16[768,1024]{1,0:T(8,128)(2,1)} %get-tuple-element.220.refs_0_, bf16[16,256]{1,0:T(8,128)(2,1)} %fusion.82.refs_1_), custom_call_target="tpu_custom_call" | custom-call | tf_op jit(solution)/shard_map/dense_back_mid/pallas_call | solution.py:98
  516.2 10.1 %sent_z.1.refs_0_ = bf16[4,3,32,256]{3,2,1,0:T(8,128)(2,1)} custom-call(bf16[3,32,256]{2,1,0:T(8,128)(2,1)} %bitcast.289), custom_call_target="tpu_custom_call" | custom-call | tf_op jit(solution)/shard_map/sent_z/pallas_call | solution.py:98
  526.4 7.1 sent_core.1
  535.0 3.2 multiply_reduce_fusion.4
  541.5 21.1 %dense_back_mixed.1 = bf16[4,768,256]{2,1,0:T(8,128)(2,1)} custom-call(bf16[768,1024]{1,0:T(8,128)(2,1)} %convolution_convert_fusion.6.refs_0_), custom_call_target="tpu_custom_call" | custom-call | tf_op jit(solution)/shard_map/dense_back_mixed/pallas_call | solution.py:98
  569.2 11.1 %dense_grad_to_heads.1 = bf16[4,384,128]{2,1,0:T(8,128)(2,1)} custom-call(bf16[384,512]{1,0:T(8,128)(2,1)} %reshape.620.refs_0_), custom_call_target="tpu_custom_call" | custom-call | tf_op jit(solution)/shard_map/dense_grad_to_heads/pallas_call | solution.py:98
  580.3 14.3 %dense_attention_grad.1 = (bf16[4,3,128,128]{3,2,1,0:T(8,128)(2,1)}, bf16[2,4,3,256,128]{4,3,2,1,0:T(8,128)(2,1)}) custom-call(s32[1]{0:T(128)} %bitcast.1.place_ref, bf16[4,3,128,128]{3,2,1,0:T(8,128)(2,1)} %bitcast.254, bf16[4,3,128,128]{3,2,1,0:T(8,128)(2,1)} %bitcast.255, bf16[2,4,3,256,128]{4,3,2,1,0:T(8,128)(2,1)} %bitcast.234, ...), custom_call_target="tpu_custom_call" | custom-call | tf_op jit(solution)/shard_map/dense_attention_grad/pallas_call | solution.py:332
  594.6 25.0 %dense_pair_grads.1 = bf16[2,4,3,256,128]{4,3,2,1,0:T(8,128)(2,1)} custom-call(bf16[2,4,3,256,128]{4,3,2,1,0:T(8,128)(2,1)} %get-tuple-element.78.refs_0_), custom_call_target="tpu_custom_call" | custom-call | tf_op jit(solution)/shard_map/dense_pair_grads/pallas_call | solution.py:98
  619.6 2.8 reduce_sum.368
  622.4 25.5 %dense_grad_tokens.1 = (bf16[384,512]{1,0:T(8,128)(2,1)}, bf16[768,512]{1,0:T(8,128)(2,1)}) custom-call(bf16[4,384,128]{2,1,0:T(8,128)(2,1)} %bitcast.275, bf16[4,768,128]{2,1,0:T(8,128)(2,1)} %bitcast.239), custom_call_target="tpu_custom_call" | custom-call | tf_op jit(solution)/shard_map/dense_grad_tokens/pallas_call | solution.py:98
  659.0 5.7 convolution_convert_fusion.3
  664.7 6.2 convolution_convert_fusion.2
  675.3 2.8 convolution_convert_fusion.1
  686.9 20.9 %dense_back_in.1 = (bf16[4,768,256]{2,1,0:T(8,128)(2,1)}, bf16[4,16,256]{2,1,0:T(8,128)(2,1)}) custom-call(bf16[768,1024]{1,0:T(8,128)(2,1)} %get-tuple-element.218.refs_0_, bf16[16,256]{1,0:T(8,128)(2,1)} %fusion.83.refs_1_), custom_call_target="tpu_custom_call" | custom-call | tf_op jit(solution)/shard_map/dense_back_in/pallas_call | solution.py:98
  713.3 15.3 %vector_columns.1 = f32[8,1024]{1,0:T(8,128)} custom-call(f32[8,256]{1,0:T(8,128)} %pad.46.refs_0_), custom_call_target="tpu_custom_call" | custom-call | tf_op jit(solution)/shard_map/vector_columns/pallas_call | solution.py:98
  728.5 11.8 %vector_shards.1 = f32[8,8,128]{2,1,0:T(8,128)} custom-call(f32[8,8,128]{2,1,0:T(8,128)} %bitcast.292), custom_call_target="tpu_custom_call" | custom-call | tf_op jit(solution)/shard_map/vector_shards/pallas_call | solution.py:98
  741.6 30.8 %reduce-scatter.15.cloned.1.call-done.refs_3_ = bf16[128,1024]{1,0:T(8,128)(2,1)} async-done(((bf16[1024,1024]{1,0:T(8,128)(2,1)}), bf16[128,1024]{1,0:T(8,128)(2,1)}) %reduce-scatter.15.cloned.1.call-update) | async-done | bytes 262160 | tf_op jit(solution)/shard_map/reduce_scatter | solution.py:703
  772.5 41.4 %dense_weight_grads.1 = (bf16[4,128,768]{2,1,0:T(8,128)(2,1)}, bf16[128,1024]{1,0:T(8,128)(2,1)}, bf16[4,128,1024]{2,1,0:T(8,128)(2,1)}, bf16[4,128,1024]{2,1,0:T(8,128)(2,1)}) custom-call(bf16[128,768]{1,0:T(8,128)(2,1)} %reduce-scatter.9.cloned.1.call-done.refs_0_, bf16[128,256]{1,0:T(8,128)(2,1)} %reduce-scatter.11.cloned.1.call-done.refs_1_, ...), custom_call_target="tpu_custom_call" | custom-call | tf_op jit(solution)/shard_map/dense_weight_grads/pallas_call | solution.py:98
  816.0 23.6 %reduce-scatter.17.cloned.1.call-done.refs_0_ = bf16[128,768]{1,0:T(8,128)(2,1)} async-done(((bf16[1024,768]{1,0:T(8,128)(2,1)}), bf16[128,768]{1,0:T(8,128)(2,1)}) %reduce-scatter.17.cloned.1.call-update) | async-done | bytes 196624 | tf_op jit(solution)/shard_map/reduce_scatter | solution.py:703
  839.6 36.8 %reduce-scatter.21.cloned.1.call-done.refs_2_ = bf16[128,1024]{1,0:T(8,128)(2,1)} async-done(((bf16[1024,1024]{1,0:T(8,128)(2,1)}), bf16[128,1024]{1,0:T(8,128)(2,1)}) %reduce-scatter.21.cloned.1.call-update) | async-done | bytes 262160 | tf_op jit(solution)/shard_map/reduce_scatter | solution.py:703
  876.4 37.1 %reduce-scatter.23.cloned.1.call-done.refs_3_ = bf16[128,1024]{1,0:T(8,128)(2,1)} async-done(((bf16[1024,1024]{1,0:T(8,128)(2,1)}), bf16[128,1024]{1,0:T(8,128)(2,1)}) %reduce-scatter.23.cloned.1.call-update) | async-done | bytes 262160 | tf_op jit(solution)/shard_map/reduce_scatter | solution.py:703
  913.5 34.9 %routed_weight_grads.1 = (bf16[4,128,768]{2,1,0:T(8,128)(2,1)}, bf16[128,1024]{1,0:T(8,128)(2,1)}, bf16[4,128,1024]{2,1,0:T(8,128)(2,1)}, bf16[4,128,1024]{2,1,0:T(8,128)(2,1)}) custom-call(bf16[128,768]{1,0:T(8,128)(2,1)} %reduce-scatter.17.cloned.1.call-done.refs_0_, bf16[128,256]{1,0:T(8,128)(2,1)} %reduce-scatter.19.cloned.1.call-done.refs_1_, ...), custom_call_target="tpu_custom_call" | custom-call | tf_op jit(solution)/shard_map/routed_weight_grads/pallas_call | solution.py:98
  956.5 2.7 copy.284
  959.2 3.1 reshape.605
  968.9 2.7 copy.287
  971.5 3.2 reshape.610
  (378 shorter events, 154.1 us)
Async XLA Ops:
  7.2 5.5 copy-start
  7.2 93.3 %all-gather.7.cloned.1.call-start = ((), (), s32[]{:S(2)}) async-start(), calls=%async_computation.8 | async-start | bytes 1769472 | tf_op jit(solution)/shard_map/all_gather | solution.py:503
  10.2 240.0 %all-gather.9.cloned.1.call-start = ((), (), s32[]{:S(2)}) async-start(), calls=%async_computation.9 | async-start | bytes 2359296 | tf_op jit(solution)/shard_map/all_gather | solution.py:503
  12.7 243.7 %all-gather.11.cloned.1.call-start = ((), (), s32[]{:S(2)}) async-start(), calls=%async_computation.10 | async-start | bytes 2359296 | tf_op jit(solution)/shard_map/all_gather | solution.py:503
  13.5 297.2 %all-gather.13.cloned.1.call-start = ((), (), s32[]{:S(2)}) async-start(), calls=%async_computation.11 | async-start | bytes 1769472 | tf_op jit(solution)/shard_map/all_gather | solution.py:503
  14.8 5.2 copy-start.62
  14.8 5.2 copy-start.63
  14.8 5.2 copy-start.64
  14.9 5.2 copy-start.65
  14.9 5.2 copy-start.66
  15.6 14.4 %copy-start.2 = (bf16[3,256,1024]{2,1,0:T(8,128)(2,1)S(1)}, bf16[3,256,1024]{2,1,0:T(8,128)(2,1)}, u32[]{:S(2)}) copy-start(bf16[3,256,1024]{2,1,0:T(8,128)(2,1)} %param.21) | copy-start | bytes 4718596
  15.6 339.3 %all-gather.15.cloned.1.call-start = ((), (), s32[]{:S(2)}) async-start(), calls=%async_computation.12 | async-start | bytes 2359296 | tf_op jit(solution)/shard_map/all_gather | solution.py:503
  17.4 13.0 %copy-start.35 = (s32[3,2048]{1,0:T(4,128)S(1)}, s32[3,2048]{1,0:T(4,128)}, u32[]{:S(2)}) copy-start(s32[3,2048]{1,0:T(4,128)} %param.22) | copy-start | bytes 73732
  18.1 31.7 %copy-start.33 = (s32[3,256]{1,0:T(4,128)S(1)}, s32[3,256]{1,0:T(4,128)}, u32[]{:S(2)}) copy-start(s32[3,256]{1,0:T(4,128)} %param.23) | copy-start | bytes 9220
  18.2 340.0 %all-gather.17.cloned.1.call-start = ((), (), s32[]{:S(2)}) async-start(), calls=%async_computation.13 | async-start | bytes 2359296 | tf_op jit(solution)/shard_map/all_gather | solution.py:503
  19.9 721.7 %reduce-scatter.11.cloned.1.call-start = ((), (), s32[]{:S(2)}) async-start(), calls=%async_computation.15 | async-start | bytes 589824 | tf_op jit(solution)/shard_map/reduce_scatter | solution.py:703
  29.9 220.3 %copy-start.53 = (f32[1,8,128]{2,0,1:T(1,128)}, f32[1,8,128]{2,0,1:T(1,128)S(1)}, u32[]{:S(2)}) copy-start(f32[1,8,128]{2,0,1:T(1,128)S(1)} %get-tuple-element.246) | copy-start | bytes 12292
  48.8 235.3 %copy-start.37 = (s32[256]{0:T(256)}, s32[256]{0:T(256)S(1)}, u32[]{:S(2)}) copy-start(s32[256]{0:T(256)S(1)} %iota_add_fusion.1) | copy-start | bytes 3076
  250.3 6.1 copy-start.39
  313.3 39.9 %copy-start.3 = (bf16[96,1024]{1,0:T(8,128)(2,1)S(1)}, bf16[96,1024]{1,0:T(8,128)(2,1)}, u32[]{:S(2)}) copy-start(bf16[96,1024]{1,0:T(8,128)(2,1)} %value_rows_columns.1) | copy-start | bytes 589828
  313.4 39.9 %copy-start.36 = (f32[1,8,128]{2,0,1:T(1,128)S(1)}, f32[1,8,128]{2,0,1:T(1,128)}, u32[]{:S(2)}) copy-start(f32[1,8,128]{2,0,1:T(1,128)} %get-tuple-element.245) | copy-start | bytes 12292
  345.3 12.9 %copy-start.6 = (bf16[96,1024]{1,0:T(8,128)(2,1)S(1)}, bf16[96,1024]{1,0:T(8,128)(2,1)}, u32[]{:S(2)}) copy-start(bf16[96,1024]{1,0:T(8,128)(2,1)} %grad_rows_columns.1) | copy-start | bytes 589828
  354.9 73.8 %copy-start.41 = (f32[96]{0:T(128)}, f32[96]{0:T(128)S(1)}, u32[]{:S(2)}) copy-start(f32[96]{0:T(128)S(1)} %get-tuple-element.264) | copy-start | bytes 1156
  369.3 3.4 copy-start.42
  369.3 3.4 copy-start.4
  369.3 3.4 copy-start.8
  382.5 16.4 %copy-start.58 = (f32[96]{0:T(128)}, f32[96]{0:T(128)S(1)}, u32[]{:S(2)}) copy-start(f32[96]{0:T(128)S(1)} %fusion.94) | copy-start | bytes 1156
  383.6 36.2 %copy-start.24 = (bf16[96,256]{1,0:T(8,128)(2,1)}, bf16[96,256]{1,0:T(8,128)(2,1)S(1)}, u32[]{:S(2)}) copy-start(bf16[96,256]{1,0:T(8,128)(2,1)S(1)} %add_convert_fusion.2) | copy-start | bytes 147460
  401.5 27.2 %copy-start.46 = (f32[96]{0:T(128)S(1)}, f32[96]{0:T(128)}, u32[]{:S(2)}) copy-start(f32[96]{0:T(128)} %copy-done.45) | copy-start | bytes 1156
  401.5 27.2 %copy-start.48 = (f32[1,256]{1,0:T(1,128)S(1)}, f32[1,256]{1,0:T(1,128)}, u32[]{:S(2)}) copy-start(f32[1,256]{1,0:T(1,128)} %get-tuple-element.271) | copy-start | bytes 3076
  401.5 27.2 %copy-start.49 = (f32[1,256]{1,0:T(1,128)S(1)}, f32[1,256]{1,0:T(1,128)}, u32[]{:S(2)}) copy-start(f32[1,256]{1,0:T(1,128)} %get-tuple-element.272) | copy-start | bytes 3076
  401.5 27.3 %copy-start.57 = (f32[96]{0:T(128)S(1)}, f32[96]{0:T(128)}, u32[]{:S(2)}) copy-start(f32[96]{0:T(128)} %get-tuple-element.263) | copy-start | bytes 1156
  401.5 27.2 %copy-start.59 = (f32[96]{0:T(128)S(1)}, f32[96]{0:T(128)}, u32[]{:S(2)}) copy-start(f32[96]{0:T(128)} %copy-done.58) | copy-start | bytes 1156
  401.5 27.2 %copy-start.60 = (f32[96]{0:T(128)S(1)}, f32[96]{0:T(128)}, u32[]{:S(2)}) copy-start(f32[96]{0:T(128)} %get-tuple-element.210) | copy-start | bytes 1156
  401.5 27.2 %copy-start.61 = (f32[96]{0:T(128)S(1)}, f32[96]{0:T(128)}, u32[]{:S(2)}) copy-start(f32[96]{0:T(128)} %get-tuple-element.261) | copy-start | bytes 1156
  417.2 35.9 %copy-start.26 = (bf16[96,256]{1,0:T(8,128)(2,1)}, bf16[96,256]{1,0:T(8,128)(2,1)S(1)}, u32[]{:S(2)}) copy-start(bf16[96,256]{1,0:T(8,128)(2,1)S(1)} %copy.274) | copy-start | bytes 147460
  483.6 3.6 copy-start.7
  483.6 3.6 copy-start.5
  483.6 3.6 copy-start.54
  483.6 3.7 copy-start.67
  487.2 3.1 copy-start.71
  490.3 25.2 %copy-start.32 = (bf16[4,96,256]{2,1,0:T(8,128)(2,1)S(1)}, bf16[4,96,256]{2,1,0:T(8,128)(2,1)}, u32[]{:S(2)}) copy-start(bf16[4,96,256]{2,1,0:T(8,128)(2,1)} %get-tuple-element.61) | copy-start | bytes 589828
  490.9 24.6 %copy-start.29 = (f32[96,256]{1,0:T(8,128)S(1)}, f32[96,256]{1,0:T(8,128)}, u32[]{:S(2)}) copy-start(f32[96,256]{1,0:T(8,128)} %get-tuple-element.265) | copy-start | bytes 294916
  490.9 24.6 %copy-start.43 = (f32[96]{0:T(128)S(1)}, f32[96]{0:T(128)}, u32[]{:S(2)}) copy-start(f32[96]{0:T(128)} %copy-done.42) | copy-start | bytes 1156
  535.0 3.2 copy-start.16
  539.7 202.0 %reduce-scatter.9.cloned.1.call-start = ((), (), s32[]{:S(2)}) async-start(), calls=%async_computation.14 | async-start | bytes 1769472 | tf_op jit(solution)/shard_map/reduce_scatter | solution.py:703
  652.9 3.4 copy-start.15
  656.3 2.7 copy-start.55
  658.9 82.7 %reduce-scatter.13.cloned.1.call-start = ((), (), s32[]{:S(2)}) async-start(), calls=%async_computation.16 | async-start | bytes 2359296 | tf_op jit(solution)/shard_map/reduce_scatter | solution.py:703
  664.7 107.8 %reduce-scatter.15.cloned.1.call-start = ((), (), s32[]{:S(2)}) async-start(), calls=%async_computation.17 | async-start | bytes 2359296 | tf_op jit(solution)/shard_map/reduce_scatter | solution.py:703
  671.0 144.9 %reduce-scatter.19.cloned.1.call-start = ((), (), s32[]{:S(2)}) async-start(), calls=%async_computation.19 | async-start | bytes 589824 | tf_op jit(solution)/shard_map/reduce_scatter | solution.py:703
  673.1 166.5 %reduce-scatter.17.cloned.1.call-start = ((), (), s32[]{:S(2)}) async-start(), calls=%async_computation.18 | async-start | bytes 1769472 | tf_op jit(solution)/shard_map/reduce_scatter | solution.py:703
  675.2 3.0 copy-start.10
  675.2 3.0 copy-start.44
  675.3 201.2 %reduce-scatter.21.cloned.1.call-start = ((), (), s32[]{:S(2)}) async-start(), calls=%async_computation.20 | async-start | bytes 2359296 | tf_op jit(solution)/shard_map/reduce_scatter | solution.py:703
  678.1 235.4 %reduce-scatter.23.cloned.1.call-start = ((), (), s32[]{:S(2)}) async-start(), calls=%async_computation.21 | async-start | bytes 2359296 | tf_op jit(solution)/shard_map/reduce_scatter | solution.py:703
  708.6 4.0 copy-start.50
  708.6 4.0 copy-start.51
  708.6 4.0 copy-start.52
  708.6 4.0 copy-start.56
  959.2 3.2 copy-start.17
  965.5 3.0 copy-start.19
  971.5 3.2 copy-start.18
  971.5 4.8 copy-start.1
  (22 other events, 40.7 us)
Sparse Core Ops, SparseCore 0:
  10.4 32.1 all-gather.6
  44.8 37.3 all-gather.8
  84.3 31.1 all-gather.10
  117.5 34.6 all-gather.12
  154.2 31.1 all-gather.14
  187.4 28.2 all-gather.16
  539.8 31.1 reduce-scatter.10
  659.0 39.4 reduce-scatter.8
  701.5 33.4 reduce-scatter.12
  737.8 34.5 reduce-scatter.14
  775.4 29.5 reduce-scatter.18
  807.2 32.3 reduce-scatter.16
  842.5 33.9 reduce-scatter.20
  879.1 34.3 reduce-scatter.22

commit v2 on v1

v2 whole, which is shorter than its diff:
```python
import functools

import jax
import jax.numpy as jnp
from jax import lax
from jax.experimental import pallas as pl
from jax.experimental.pallas import tpu as pltpu
from jax.sharding import PartitionSpec as P

HEADS = 16
HDIM = 64
DOCS = 8
EPS = 1e-06
NEG = -1e30
SCALE = HDIM ** (-0.5)
VMEM = 32 * 2**20
MESH = pl.DeviceIdType.MESH
BF = jnp.bfloat16
F32 = jnp.float32


def matmul(left, right):
    return jnp.dot(left, right, preferred_element_type=F32)


def contract(left, right, ldim, rdim):
    return lax.dot_general(left, right, (((ldim,), (rdim,)), ((), ())), preferred_element_type=F32)


class Lines:
    def __init__(self, sections, dp, group):
        self.sizes = {"section": sections, "z": group, "core": dp // group}
        self.ring = dp // group

    def place(self, kind):
        if kind == "section":
            return lax.axis_index("section")
        index = lax.axis_index("dp")
        return index // self.ring if kind == "z" else lax.rem(index, self.ring)

    def device(self, kind, place):
        if kind == "section":
            return {"section": place}
        index = lax.axis_index("dp")
        if kind == "z":
            return {"dp": place * self.ring + lax.rem(index, self.ring)}
        return {"dp": (index // self.ring) * self.ring + place}

    def peers(self, kind):
        size = self.sizes[kind]
        me = self.place(kind)
        return [lax.rem(me + step, size) for step in range(1, size)]


class Copies:
    def __init__(self, lines, send, recv):
        self.lines, self.send, self.recv, self.used = lines, send, recv, 0

    def greet(self, kinds):
        barrier = pltpu.get_barrier_semaphore()
        count = 0
        for kind in kinds:
            for peer in self.lines.peers(kind):
                pl.semaphore_signal(
                    barrier, inc=1, device_id=self.lines.device(kind, peer), device_id_type=MESH
                )
                count += 1
        pl.semaphore_wait(barrier, count)

    def start(self, kind, peer, src, dst):
        copy = pltpu.make_async_remote_copy(
            src_ref=src,
            dst_ref=dst,
            send_sem=self.send.at[self.used],
            recv_sem=self.recv.at[self.used],
            device_id=self.lines.device(kind, peer),
            device_id_type=MESH,
        )
        self.used += 1
        copy.start()
        return copy

    def swap(self, kind, src, dst):
        me = self.lines.place(kind)
        return [self.start(kind, peer, src(peer), dst(me)) for peer in self.lines.peers(kind)]


def wait(copies):
    for copy in copies:
        copy.wait()


def semaphores(count):
    return [pltpu.SemaphoreType.DMA((count,)), pltpu.SemaphoreType.DMA((count,))]


def communicate(kernel, ident, arrays, shapes, scratch, name, limit=24 * 2**20):
    vmem = pl.BlockSpec(memory_space=pltpu.VMEM)
    return pl.pallas_call(
        kernel,
        out_shape=[jax.ShapeDtypeStruct(s, d) for s, d in shapes],
        in_specs=[vmem] * len(arrays),
        out_specs=[vmem] * len(shapes),
        scratch_shapes=scratch,
        compiler_params=pltpu.CompilerParams(
            collective_id=ident, has_side_effects=True, vmem_limit_bytes=limit
        ),
        name=name,
    )(*arrays)


def span(place, width):
    return pl.ds(pl.multiple_of(place * width, width), width)


def square(lines):
    me = lines.place("section")
    low, high = lax.rem(me, 2), me // 2
    return high * 2 + 1 - low, (1 - high) * 2 + low, (1 - high) * 2 + 1 - low


def gather_columns(lines, ident, part, name):
    rows, width = part.shape
    half = rows // 2
    pieces = 2 if half % 32 == 0 else 1
    step = half // pieces

    def kernel(x_ref, o_ref, send, recv):
        copies = Copies(lines, send, recv)
        me = lines.place("section")
        near, far, _ = square(lines)
        copies.greet(["section"])
        first, rest = [], []
        for j in range(pieces):
            for h, (one, two) in enumerate(((near, far), (far, near))):
                at = pl.ds(h * half + j * step, step)
                first.append(copies.start("section", one, x_ref.at[at], o_ref.at[at, span(me, width)]))
        for j in range(pieces):
            for h, (one, two) in enumerate(((near, far), (far, near))):
                at = pl.ds(h * half + j * step, step)
                rest.append(copies.start("section", two, x_ref.at[at], o_ref.at[at, span(me, width)]))
        o_ref[:, span(me, width)] = x_ref[...]
        for j in range(pieces):
            for h, (one, two) in enumerate(((near, far), (far, near))):
                at = pl.ds(h * half + j * step, step)
                first[2 * j + h].wait_recv()
                place = o_ref.at[at, span(one, width)]
                rest.append(copies.start("section", two, place, place))
        for copy in first:
            copy.wait_send()
        wait(rest)

    (out,) = communicate(
        kernel, ident, [part], [((rows, lines.sizes["section"] * width), part.dtype)], semaphores(6 * pieces), name
    )
    return out


def scatter_columns(lines, ident, part, scalars, name):
    rows, full = part.shape
    sections = lines.sizes["section"]
    width = full // sections
    half = rows // 2
    pieces = 2 if half % 32 == 0 else 1
    step = half // pieces
    extra = scalars is not None
    arrays = [part]
    shapes = [((rows, width), F32)]
    scratch = semaphores(6 * pieces + 3) + [
        pltpu.VMEM((2, rows, width), part.dtype),
        pltpu.VMEM((rows, width), part.dtype),
        pltpu.VMEM((rows, width), part.dtype),
    ]
    if extra:
        lines_of = -(-rows // 128)
        padded = lines_of + -lines_of % 8
        block = jnp.pad(scalars, (0, padded * 128 - rows)).reshape(padded, 128)
        arrays.append(block)
        shapes.append((block.shape, F32))
        scratch.append(pltpu.VMEM((sections,) + block.shape, F32))

    def kernel(*refs):
        x_ref, refs = refs[0], refs[1:]
        if extra:
            e_ref, o_ref, eo_ref, send, recv, got, turn, last, e_got = refs
        else:
            o_ref, send, recv, got, turn, last = refs
        copies = Copies(lines, send, recv)
        me = lines.place("section")
        near, far, across = square(lines)
        copies.greet(["section"])
        first, second, others = [], [], []
        ways = ((near, far), (far, near))
        for j in range(pieces):
            for h, (one, two) in enumerate(ways):
                at = pl.ds(h * half + j * step, step)
                first.append(copies.start("section", one, x_ref.at[at, span(across, width)], got.at[0, at]))
                first.append(copies.start("section", one, x_ref.at[at, span(one, width)], got.at[1, at]))
        if extra:
            others = copies.swap("section", lambda peer: e_ref, lambda place: e_got.at[place])
        for j in range(pieces):
            for h, (one, two) in enumerate(ways):
                at = pl.ds(h * half + j * step, step)
                first[4 * j + 2 * h].wait_recv()
                turn[at] = (x_ref[at, span(two, width)].astype(F32) + got[0, at].astype(F32)).astype(part.dtype)
                second.append(copies.start("section", two, turn.at[at], last.at[at]))
        for j in range(pieces):
            for h in range(2):
                at = pl.ds(h * half + j * step, step)
                first[4 * j + 2 * h + 1].wait_recv()
                second[2 * j + h].wait_recv()
                o_ref[at] = (
                    x_ref[at, span(me, width)].astype(F32) + got[1, at].astype(F32) + last[at].astype(F32)
                )
        for copy in first + second:
            copy.wait_send()
        if extra:
            wait(others)
            e_got[me] = e_ref[...]
            total = e_got[0]
            for i in range(1, sections):
                total = total + e_got[i]
            eo_ref[...] = total

    got = communicate(kernel, ident, arrays, shapes, scratch, name)
    if not extra:
        return got[0]
    return got[0], got[1].reshape(-1)[:rows]


def gather_rows(lines, ident, part, name):
    group, ring = lines.sizes["z"], lines.sizes["core"]
    dp = group * ring

    def kernel(x_ref, o_ref, send, recv):
        copies = Copies(lines, send, recv)
        rank = lax.axis_index("dp")
        copies.greet(["z", "core"])
        along = copies.swap("z", lambda peer: x_ref, lambda place: o_ref.at[rank])
        handed = copies.swap("core", lambda peer: x_ref, lambda place: o_ref.at[rank])
        o_ref[rank] = x_ref[...]
        zplace, place = lines.place("z"), lines.place("core")
        for step in range(group - 1, 0, -1):
            along[group - 1 - step].wait_recv()
            source = lax.rem(zplace + step, group) * ring + place
            handed += copies.swap("core", lambda peer: o_ref.at[source], lambda _: o_ref.at[source])
        for copy in along:
            copy.wait_send()
        wait(handed)

    (out,) = communicate(
        kernel,
        ident,
        [part],
        [((dp,) + part.shape, part.dtype)],
        semaphores(group - 1 + group * (ring - 1)),
        name,
    )
    return out


def swap_blocks(lines, ident, kind, arrays, shapes, plan, name):
    size = lines.sizes[kind]

    def kernel(*refs):
        ins, outs = refs[: len(arrays)], refs[len(arrays) : len(arrays) + len(shapes)]
        copies = Copies(lines, *refs[len(arrays) + len(shapes) :])
        me = lines.place(kind)
        copies.greet([kind])
        pending = []
        for i, src, o, dst in plan:
            pending += copies.swap(
                kind, lambda peer: src(ins[i], peer), lambda place: dst(outs[o], place)
            )
        for i, src, o, dst in plan:
            view = dst(outs[o], me)
            view[...] = src(ins[i], me)[...]
        wait(pending)

    return communicate(kernel, ident, arrays, shapes, semaphores((size - 1) * len(plan)), name)


def dense_to_heads(lines, ident, pairs, queries, name):
    group, ring = lines.sizes["z"], lines.sizes["core"]
    lanes = 2 * HDIM

    def kernel(p_ref, q_ref, po_ref, qo_ref, send, recv):
        copies = Copies(lines, send, recv)
        zplace, place = lines.place("z"), lines.place("core")
        copies.greet(["z", "core"])
        along, pending = [], []
        for peer in lines.peers("z"):
            along.append(copies.start("z", peer, p_ref.at[:, span(peer, lanes)], po_ref.at[place, zplace]))
        for peer in lines.peers("z"):
            pending.append(copies.start("z", peer, q_ref.at[:, span(peer, lanes)], qo_ref.at[zplace]))
        own = p_ref.at[:, span(zplace, lanes)]
        pending += copies.swap("core", lambda peer: own, lambda _: po_ref.at[place, zplace])
        po_ref[place, zplace] = own[...]
        qo_ref[zplace] = q_ref[:, span(zplace, lanes)]
        for step in range(group - 1, 0, -1):
            along[group - 1 - step].wait_recv()
            block = po_ref.at[place, lax.rem(zplace + step, group)]
            pending += copies.swap("core", lambda peer: block, lambda _: block)
        for copy in along:
            copy.wait_send()
        wait(pending)

    return communicate(
        kernel,
        ident,
        [pairs, queries],
        [((ring, group, pairs.shape[0], lanes), BF), ((group, queries.shape[0], lanes), BF)],
        semaphores(2 * (group - 1) + group * (ring - 1)),
        name,
    )


def dense_from_heads(lines, ident, pairs, queries, name):
    group, ring = lines.sizes["z"], lines.sizes["core"]
    _, _, rows, lanes = pairs.shape

    def kernel(p_ref, q_ref, po_ref, qo_ref, send, recv, got, turn):
        copies = Copies(lines, send, recv)
        zplace, place = lines.place("z"), lines.place("core")
        copies.greet(["z", "core"])
        order = lines.peers("z") + [zplace]
        around, pending = [], []
        for g in order:
            around.append(copies.swap("core", lambda peer: p_ref.at[peer, g], lambda me: got.at[me, g]))
        for g in order[:-1]:
            pending.append(copies.start("z", g, q_ref.at[g], qo_ref.at[:, span(zplace, lanes)]))
        qo_ref[:, span(zplace, lanes)] = q_ref[zplace]
        for g, arrived in zip(order, around):
            for copy in arrived:
                copy.wait_recv()
            total = p_ref[place, g].astype(F32)
            for peer in lines.peers("core"):
                total = total + got[peer, g].astype(F32)
            if g is zplace:
                po_ref[:, span(zplace, lanes)] = total.astype(BF)
            else:
                turn[g] = total.astype(BF)
                pending.append(copies.start("z", g, turn.at[g], po_ref.at[:, span(zplace, lanes)]))
        for arrived in around:
            for copy in arrived:
                copy.wait_send()
        wait(pending)

    return communicate(
        kernel,
        ident,
        [pairs, queries],
        [((rows, group * lanes), BF), ((queries.shape[1], group * lanes), BF)],
        semaphores(2 * (group - 1) + group * (ring - 1))
        + [pltpu.VMEM((ring, group, rows, lanes), BF), pltpu.VMEM((group, rows, lanes), BF)],
        name,
    )


def whole(ref, place):
    return ref


def slot(ref, place):
    return ref.at[place]


def columns(width):
    def view(ref, place):
        return ref.at[:, span(place, width)]

    return view


def unpack_low(packed):
    lane = lax.broadcasted_iota(jnp.int32, packed.shape, 1)
    zero = jnp.zeros_like(packed)
    low = jnp.where(lane < HDIM, packed, zero)
    turned = jnp.concatenate([packed[:, HDIM:], packed[:, :HDIM]], axis=1)
    high = jnp.where(lane < HDIM, turned, zero)
    return jnp.concatenate([low, high], axis=0)


def unpack_high(packed):
    lane = lax.broadcasted_iota(jnp.int32, packed.shape, 1)
    zero = jnp.zeros_like(packed)
    turned = jnp.concatenate([packed[:, HDIM:], packed[:, :HDIM]], axis=1)
    low = jnp.where(lane >= HDIM, turned, zero)
    high = jnp.where(lane >= HDIM, packed, zero)
    return jnp.concatenate([low, high], axis=0)


def pack_turned(turned):
    half = turned.shape[1] // 2
    return jnp.concatenate([turned[:, :half], turned[:, half:]], axis=0).T


def forward_block(query, pieces, qpos, start, causal):
    scores = []
    peak = None
    for index, (pair, _, first) in enumerate(pieces):
        item = contract(pair, query, 1, 1)
        kpos = first + lax.broadcasted_iota(jnp.int32, item.shape, 0)
        allowed = kpos >= start
        if causal[index]:
            allowed = allowed & (kpos <= qpos)
        item = jnp.where(allowed, item, NEG)
        top = jnp.max(item, axis=0, keepdims=True)
        peak = top if peak is None else jnp.maximum(peak, top)
        scores.append(item)
    total = jnp.zeros_like(peak)
    mixed = None
    for item, (_, turned, _) in zip(scores, pieces):
        weight = jnp.exp(item - peak)
        total = total + jnp.sum(weight, axis=0, keepdims=True)
        part = matmul(turned[HDIM:], weight.astype(BF))
        mixed = part if mixed is None else mixed + part
    return mixed / total, peak + jnp.log(total)


def backward_block(query, grad, grad_turned, mixed_turned, lse, pieces, qpos, start, causal):
    row_sum = jnp.sum(grad_turned.astype(F32) * mixed_turned.astype(F32), axis=0, keepdims=True)
    grad_query = None
    grads = []
    for index, (pair, turned, first) in enumerate(pieces):
        scores = contract(pair, query, 1, 1)
        kpos = first + lax.broadcasted_iota(jnp.int32, scores.shape, 0)
        allowed = kpos >= start
        if causal[index]:
            allowed = allowed & (kpos <= qpos)
        probs = jnp.where(allowed, jnp.exp(scores - lse), 0.0)
        grad_probs = contract(pair, grad, 1, 1)
        grad_scores = (probs * (grad_probs - row_sum)).astype(BF)
        grads.append(matmul(grad_scores, query) + matmul(probs.astype(BF), grad))
        part = matmul(turned[:HDIM], grad_scores)
        grad_query = part if grad_query is None else grad_query + part
    return grad_query * SCALE, grads


def dense_forward_kernel(place_ref, q_ref, kv_ref, start_ref, out_ref, turned_ref, lse_ref):
    group, _, half, _ = q_ref.shape
    ring, _, _, block, _ = kv_ref.shape
    place = place_ref[0]
    span = ring * block
    pieces = []
    for g in range(group):
        pair = kv_ref[:, g, 0].reshape(span, 2 * HDIM)
        pieces.append((pair, pair.T, g * span))
    for g in range(group):
        query = unpack_low(q_ref[g, 0]) * jnp.asarray(SCALE, BF)
        qpos = g * span + place * block + lax.broadcasted_iota(jnp.int32, (1, block), 1)
        mixed, lse = forward_block(
            query, pieces[: g + 1], qpos, start_ref[0, g], [i == g for i in range(g + 1)]
        )
        turned_ref[0, g] = mixed.astype(BF)
        lse_ref[0, g] = lse
        out_ref[g, 0] = pack_turned(mixed).astype(BF)


def dense_forward(place, q, kv, start):
    group, seqs, half, lanes = q.shape
    ring, _, _, block, _ = kv.shape
    grid = pltpu.PrefetchScalarGridSpec(
        num_scalar_prefetch=1,
        grid=(seqs,),
        in_specs=[
            pl.BlockSpec((group, 1, half, lanes), lambda s, _: (0, s, 0, 0)),
            pl.BlockSpec((ring, group, 1, block, lanes), lambda s, _: (0, 0, s, 0, 0)),
            pl.BlockSpec((1, group, 1, block), lambda s, _: (s, 0, 0, 0)),
        ],
        out_specs=[
            pl.BlockSpec((group, 1, half, lanes), lambda s, _: (0, s, 0, 0)),
            pl.BlockSpec((1, group, HDIM, block), lambda s, _: (s, 0, 0, 0)),
            pl.BlockSpec((1, group, 1, block), lambda s, _: (s, 0, 0, 0)),
        ],
    )
    return pl.pallas_call(
        dense_forward_kernel,
        grid_spec=grid,
        out_shape=[
            jax.ShapeDtypeStruct(q.shape, BF),
            jax.ShapeDtypeStruct((seqs, group, HDIM, block), BF),
            jax.ShapeDtypeStruct((seqs, group, 1, block), F32),
        ],
        compiler_params=pltpu.CompilerParams(vmem_limit_bytes=VMEM),
        name="dense_attention",
    )(place, q, kv, start)


def dense_backward_kernel(
    place_ref, q_ref, g_ref, kv_ref, start_ref, turned_ref, lse_ref, dq_ref, dkv_ref, acc_ref
):
    group, _, half, _ = q_ref.shape
    ring, _, _, block, _ = kv_ref.shape
    place = place_ref[0]
    span = ring * block
    pieces = []
    for g in range(group):
        pair = kv_ref[:, g, 0].reshape(span, 2 * HDIM)
        pieces.append((pair, pair.T, g * span))
    for g in reversed(range(group)):
        query = unpack_low(q_ref[g, 0]) * jnp.asarray(SCALE, BF)
        packed = g_ref[g, 0]
        grad = unpack_high(packed)
        flat = packed.T
        grad_turned = jnp.concatenate([flat[:HDIM], flat[HDIM:]], axis=1)
        qpos = g * span + place * block + lax.broadcasted_iota(jnp.int32, (1, block), 1)
        grad_query, grads = backward_block(
            query,
            grad,
            grad_turned,
            turned_ref[0, g],
            lse_ref[0, g],
            pieces[: g + 1],
            qpos,
            start_ref[0, g],
            [i == g for i in range(g + 1)],
        )
        dq_ref[g, 0] = pack_turned(grad_query).astype(BF)
        for i, item in enumerate(grads):
            if g == group - 1:
                acc_ref[i] = item
            else:
                acc_ref[i] += item
    for g in range(group):
        dkv_ref[:, g, 0] = acc_ref[g].reshape(ring, block, 2 * HDIM).astype(BF)


def dense_backward(place, q, grad, kv, start, turned, lse):
    group, seqs, half, lanes = q.shape
    ring, _, _, block, _ = kv.shape
    grid = pltpu.PrefetchScalarGridSpec(
        num_scalar_prefetch=1,
        grid=(seqs,),
        in_specs=[
            pl.BlockSpec((group, 1, half, lanes), lambda s, _: (0, s, 0, 0)),
            pl.BlockSpec((group, 1, half, lanes), lambda s, _: (0, s, 0, 0)),
            pl.BlockSpec((ring, group, 1, block, lanes), lambda s, _: (0, 0, s, 0, 0)),
            pl.BlockSpec((1, group, 1, block), lambda s, _: (s, 0, 0, 0)),
            pl.BlockSpec((1, group, HDIM, block), lambda s, _: (s, 0, 0, 0)),
            pl.BlockSpec((1, group, 1, block), lambda s, _: (s, 0, 0, 0)),
        ],
        out_specs=[
            pl.BlockSpec((group, 1, half, lanes), lambda s, _: (0, s, 0, 0)),
            pl.BlockSpec((ring, group, 1, block, lanes), lambda s, _: (0, 0, s, 0, 0)),
        ],
        scratch_shapes=[pltpu.VMEM((group, ring * block, lanes), F32)],
    )
    return pl.pallas_call(
        dense_backward_kernel,
        grid_spec=grid,
        out_shape=[
            jax.ShapeDtypeStruct(q.shape, BF),
            jax.ShapeDtypeStruct(kv.shape, BF),
        ],
        compiler_params=pltpu.CompilerParams(vmem_limit_bytes=VMEM),
        name="dense_attention_grad",
    )(place, q, grad, kv, start, turned, lse)


def inverse_rms(value):
    return lax.rsqrt(jnp.mean(value * value, axis=-1, keepdims=True) + EPS)


def gelu_terms(value):
    scale = 0.7978845608028654
    square = value * value
    bend = jnp.tanh(scale * (value + 0.044715 * square * value))
    half = 0.5 * (1.0 + bend)
    slope = half + 0.5 * value * (1.0 - bend * bend) * scale * (1.0 + 0.134145 * square)
    return value * half, slope


def side_by_side(blocks):
    return jnp.concatenate(blocks, axis=1)


def routed_kernel(
    lines,
    shape,
    source_ref,
    column_ref,
    row_ref,
    start_ref,
    gains_ref,
    main_ref,
    shrink_ref,
    returned_ref,
    added_ref,
    normed_ref,
    dqkv_ref,
    mixed_ref,
    attended_ref,
    normed_mid_ref,
    dpre_ref,
    hidden_ref,
    fed_ref,
    vectors_ref,
    send,
    recv,
    picked_buf,
    picked_got,
    slots_buf,
    slots_got,
    rows_buf,
    rows_got,
    heads_buf,
    heads_got,
    pairs_all,
    out_buf,
    out_got,
    mixed_all,
    own_buf,
    attended_all,
    fed_buf,
    fed_got,
    gate_buf,
    gate_got,
    wide_buf,
    mid_got,
    scalar_buf,
    scalar_got,
    do_buf,
    do_got,
    grad_buf,
    grad_got,
    turn_buf,
    turn_got,
    back_buf,
    back_got,
    in_buf,
    in_got,
    in_scalar,
    in_scalar_got,
    keep_ref,
    final_buf,
    final_all,
):
    seqs, sel, rows, width, part = shape
    sections, group, ring = (lines.sizes[k] for k in ("section", "z", "core"))
    dp = group * ring
    lanes = 2 * HDIM
    slots = seqs * sel
    copies = Copies(lines, send, recv)
    section, zplace, place = (lines.place(k) for k in ("section", "z", "core"))
    rank = lax.axis_index("dp")
    copies.greet(["section", "z", "core"])
    own = span(section, part)
    gain_pre, gain_mid, router = (gains_ref[i : i + 1, :] for i in range(3))
    own_pre, own_mid, own_router = (gains_ref[i : i + 1, own] for i in range(3))
    qkv_w = main_ref.at[:, : 3 * part]
    out_w = main_ref.at[:, 3 * part : 4 * part]
    expand_w = main_ref.at[:, 4 * part :]

    def sum_columns(value, buf, got, scalars, sbuf, sgot):
        buf[...] = value.astype(BF)
        pending = copies.swap("section", lambda peer: buf.at[:, span(peer, part)], lambda me: got.at[me])
        if scalars is not None:
            sbuf[...] = jnp.broadcast_to(scalars, sbuf.shape)
            pending += copies.swap("section", lambda peer: sbuf, lambda me: sgot.at[me])
        return pending

    def summed(pending, buf, got, sbuf, sgot):
        wait(pending)
        got[section] = buf[:, own]
        total = got[0].astype(F32)
        for i in range(1, sections):
            total = total + got[i].astype(F32)
        if sbuf is None:
            return total
        sgot[section] = sbuf[...]
        scalar = sgot[0]
        for i in range(1, sections):
            scalar = scalar + sgot[i]
        return total, scalar[:, :1]

    def all_columns(value, dst):
        dst[section] = value
        wait(copies.swap("section", lambda peer: dst.at[section], lambda me: dst.at[me]))
        return side_by_side([dst[i] for i in range(sections)])

    position = rank * rows + lax.broadcasted_iota(jnp.int32, (1, rows), 1)
    for q in range(seqs):
        table = (column_ref[q] == position).astype(F32).astype(BF)
        found = matmul(table, source_ref[q]).astype(BF)
        for d in range(dp):
            picked_buf[d % ring, d // ring, q * sel : (q + 1) * sel] = found[d * sel : (d + 1) * sel]
    wait(copies.swap("core", lambda peer: picked_buf.at[peer], lambda me: picked_got.at[me]))
    total = picked_buf[place].astype(F32)
    for peer in lines.peers("core"):
        total = total + picked_got[peer].astype(F32)
    slots_buf[...] = total.astype(BF)
    wait(copies.swap("z", lambda peer: slots_buf.at[peer], lambda me: slots_got.at[me]))
    total = slots_buf[zplace].astype(F32)
    for peer in lines.peers("z"):
        total = total + slots_got[peer].astype(F32)
    rows_got[section] = total.astype(BF)
    wait(copies.swap("section", lambda peer: rows_got.at[section], lambda me: rows_got.at[me]))
    picked = side_by_side([rows_got[i, :, :part] for i in range(sections)]).astype(F32)
    grad_sent = side_by_side([rows_got[i, :, part:] for i in range(sections)]).astype(F32)

    inv_in = inverse_rms(picked)
    normed = (picked * inv_in * gain_pre).astype(BF)
    normed_ref[...] = normed
    qkv = matmul(normed, qkv_w[...]).astype(BF)
    blank = jnp.zeros((slots, HDIM), BF)
    for g in range(group):
        heads_buf[g, :, :lanes] = side_by_side([qkv[:, 2 * part + g * HDIM : 2 * part + (g + 1) * HDIM], blank])
        heads_buf[g, :, lanes:] = qkv[:, g * lanes : (g + 1) * lanes]
    pending = copies.swap("z", lambda peer: heads_buf.at[peer], lambda me: heads_got.at[me])
    heads_got[zplace] = heads_buf[zplace]
    wait(pending)
    pairs_all[place] = heads_got[:, :, lanes:]
    wait(copies.swap("core", lambda peer: pairs_all.at[place], lambda me: pairs_all.at[me]))

    index = lax.broadcasted_iota(jnp.int32, (1, group * sel), 1)
    place_of = (index // sel) * (ring * sel) + place * sel + lax.rem(index, sel)

    def sequence(q):
        at = slice(q * sel, (q + 1) * sel)
        query = jnp.concatenate([heads_got[g, at, :lanes] for g in range(group)], axis=0)
        pair = jnp.concatenate([pairs_all[r, g, at] for g in range(group) for r in range(ring)], axis=0)
        return query * jnp.asarray(SCALE, BF), pair

    kept = []
    for q in range(seqs):
        query, pair = sequence(q)
        turned, lse = forward_block(query, [(pair, pair.T, 0)], place_of, start_ref[q], [True])
        kept.append((turned.astype(BF), lse))
        upright = jnp.concatenate([turned, jnp.zeros_like(turned)], axis=0).T.astype(BF)
        for g in range(group):
            out_buf[g, q * sel : (q + 1) * sel] = upright[g * sel : (g + 1) * sel]
    pending = copies.swap("z", lambda peer: out_buf.at[peer], lambda me: out_got.at[me])
    out_got[zplace] = out_buf[zplace]
    wait(pending)
    mixed = all_columns(side_by_side([out_got[g, :, :HDIM] for g in range(group)]), mixed_all)
    mixed_ref[...] = mixed
    attended_own = matmul(mixed, out_w[...]).astype(BF)
    attended = all_columns(attended_own, attended_all).astype(F32)

    middle = picked + attended
    inv_mid = inverse_rms(middle)
    normed_mid = (middle * inv_mid * gain_mid).astype(BF)
    normed_mid_ref[...] = normed_mid
    hidden_pre = matmul(normed_mid, expand_w[...])
    hidden, slope = gelu_terms(hidden_pre)
    hidden = hidden.astype(BF)
    hidden_ref[...] = hidden
    gate = jax.nn.sigmoid(jnp.sum(picked * router, axis=1, keepdims=True))
    grad_delta = gate * grad_sent
    fed_low = grad_delta.astype(BF)
    fed_ref[...] = fed_low

    grad_hidden = contract(fed_low, shrink_ref[...], 1, 1)
    grad_pre = (grad_hidden * slope).astype(BF)
    dpre_ref[...] = grad_pre
    grad_normed = contract(grad_pre, expand_w[...], 1, 1)
    scalar = jnp.sum(grad_normed * middle * gain_mid, axis=1, keepdims=True)
    pending = sum_columns(grad_normed, wide_buf, mid_got, scalar, scalar_buf, scalar_got)
    fed_part = matmul(hidden, shrink_ref[...])
    keep_ref[0] = middle
    keep_ref[1] = picked
    keep_ref[2] = grad_delta
    keep_ref[3] = grad_sent
    own_attended = attended_own.astype(F32)
    gate_part = jnp.sum(grad_sent * fed_part, axis=1, keepdims=True) + jnp.sum(
        keep_ref[3, :, own] * own_attended, axis=1, keepdims=True
    )
    middle_own, picked_own, grad_delta_own = keep_ref[0, :, own], keep_ref[1, :, own], keep_ref[2, :, own]
    grad_normed, scalar = summed(pending, wide_buf, mid_got, scalar_buf, scalar_got)
    fed_pending = sum_columns(fed_part, fed_buf, fed_got, gate_part, gate_buf, gate_got)
    vectors_ref[...] = jnp.zeros_like(vectors_ref)
    vectors_ref[1:2, :] = jnp.sum(grad_normed * middle_own * inv_mid, axis=0, keepdims=True)
    grad_middle = inv_mid * (grad_normed * own_mid) - middle_own * (inv_mid * inv_mid * inv_mid) * (
        scalar * (1.0 / width)
    )
    grad_attended = (grad_middle + grad_delta_own).astype(BF)
    attended_ref[...] = grad_attended

    pending = sum_columns(contract(grad_attended, out_w[...], 1, 1), own_buf, do_got, None, None, None)
    grad_mixed = summed(pending, own_buf, do_got, None, None).astype(BF)
    for g in range(group):
        grad_buf[g] = side_by_side([blank, grad_mixed[:, g * HDIM : (g + 1) * HDIM]])
    pending = copies.swap("z", lambda peer: grad_buf.at[peer], lambda me: grad_got.at[me])
    grad_got[zplace] = grad_buf[zplace]
    wait(pending)
    for q in range(seqs):
        at = slice(q * sel, (q + 1) * sel)
        query, pair = sequence(q)
        grad = jnp.concatenate([grad_got[g, at] for g in range(group)], axis=0)
        turned, lse = kept[q]
        grad_query, grad_pairs = backward_block(
            query, grad, grad.T[HDIM:], turned, lse, [(pair, pair.T, 0)], place_of, start_ref[q], [True]
        )
        upright = jnp.concatenate([grad_query, jnp.zeros_like(grad_query)], axis=0).T.astype(BF)
        low = grad_pairs[0].astype(BF)
        for g in range(group):
            back_buf[g, at, :lanes] = upright[g * sel : (g + 1) * sel]
            for r in range(ring):
                first = (g * ring + r) * sel
                turn_buf[r, g, at] = low[first : first + sel]
    wait(copies.swap("core", lambda peer: turn_buf.at[peer], lambda me: turn_got.at[me]))
    total = turn_buf[place].astype(F32)
    for peer in lines.peers("core"):
        total = total + turn_got[peer].astype(F32)
    back_buf[:, :, lanes:] = total.astype(BF)
    pending = copies.swap("z", lambda peer: back_buf.at[peer], lambda me: back_got.at[me])
    back_got[zplace] = back_buf[zplace]
    wait(pending)
    grad_qkv = side_by_side(
        [back_got[g, :, lanes:] for g in range(group)] + [back_got[g, :, :HDIM] for g in range(group)]
    )
    dqkv_ref[...] = grad_qkv
    grad_normed = contract(grad_qkv, qkv_w[...], 1, 1)
    scalar = jnp.sum(grad_normed * picked * gain_pre, axis=1, keepdims=True)
    pending = sum_columns(grad_normed, in_buf, in_got, scalar, in_scalar, in_scalar_got)

    fed, grad_gate = summed(fed_pending, fed_buf, fed_got, gate_buf, gate_got)
    sent = (gate * (own_attended + fed)).astype(BF)
    grad_logit = grad_gate * gate * (1.0 - gate)
    vectors_ref[2:3, :] = jnp.sum(grad_logit * picked_own, axis=0, keepdims=True)

    grad_normed, scalar = summed(pending, in_buf, in_got, in_scalar, in_scalar_got)
    vectors_ref[0:1, :] = jnp.sum(grad_normed * picked_own * inv_in, axis=0, keepdims=True)
    grad_in = inv_in * (grad_normed * own_pre) - picked_own * (inv_in * inv_in * inv_in) * (scalar * (1.0 / width))
    grad_chosen = (grad_middle + grad_in + grad_logit * own_router).astype(BF)

    final_buf[:, :part] = grad_chosen
    final_buf[:, part:] = sent
    along = copies.swap("z", lambda peer: final_buf, lambda me: rows_buf.at[me])
    rows_buf[zplace] = final_buf[...]
    spread = []

    def hand_on(i):
        view = rows_buf.at[i, :, pl.ds(0, part)]
        dst = final_all.at[place, i, :, own]
        dst[...] = view[...]
        final_all[place, i, :, width:] = rows_buf[i, :, part:]
        return copies.swap("section", lambda peer: view, lambda me: dst)

    spread += hand_on(zplace)
    for step in range(group - 1, 0, -1):
        along[group - 1 - step].wait_recv()
        spread += hand_on(lax.rem(zplace + step, group))
    for copy in along:
        copy.wait_send()
    wait(spread)
    wait(copies.swap("core", lambda peer: final_all.at[place], lambda me: final_all.at[me]))
    slot_of = rank * rows + lax.broadcasted_iota(jnp.int32, (rows, 1), 0)
    for q in range(seqs):
        at = slice(q * sel, (q + 1) * sel)
        table = (row_ref[q] == slot_of).astype(F32).astype(BF)
        found = jnp.concatenate([final_all[r, g, at] for g in range(group) for r in range(ring)], axis=0)
        placed = matmul(table, found).astype(BF)
        returned_ref[q] = placed[:, :width]
        added_ref[q] = placed[:, width:]


def routed_layer(lines, ident, source, chosen, start, gains, main, shrink, shape):
    seqs, sel, rows, width, part = shape
    sections, group, ring = (lines.sizes[k] for k in ("section", "z", "core"))
    slots = seqs * sel
    lanes = 2 * HDIM
    hidden = shrink.shape[0]
    outs = [
        ((seqs, rows, width), BF),
        ((seqs, rows, part), BF),
        ((slots, width), BF),
        ((slots, 3 * part), BF),
        ((slots, width), BF),
        ((slots, part), BF),
        ((slots, width), BF),
        ((slots, hidden), BF),
        ((slots, hidden), BF),
        ((slots, width), BF),
        ((8, part), F32),
    ]
    z = group - 1
    s = sections - 1
    c = ring - 1
    count = 4 * c + (1 + 1 + 1 + 1 + 1 + 1) * z + (1 + 1 + 1 + 2 + 2 + 1 + 2) * s + group * s
    vmem = pltpu.VMEM
    scratch = semaphores(count) + [
        vmem((ring, group, slots, 2 * part), BF),
        vmem((ring, group, slots, 2 * part), BF),
        vmem((group, slots, 2 * part), BF),
        vmem((group, slots, 2 * part), BF),
        vmem((group, slots, 2 * part), BF),
        vmem((sections, slots, 2 * part), BF),
        vmem((group, slots, 2 * lanes), BF),
        vmem((group, slots, 2 * lanes), BF),
        vmem((ring, group, slots, lanes), BF),
        vmem((group, slots, lanes), BF),
        vmem((group, slots, lanes), BF),
        vmem((sections, slots, part), BF),
        vmem((slots, width), BF),
        vmem((sections, slots, part), BF),
        vmem((slots, width), BF),
        vmem((sections, slots, part), BF),
        vmem((slots, 128), F32),
        vmem((sections, slots, 128), F32),
        vmem((slots, width), BF),
        vmem((sections, slots, part), BF),
        vmem((slots, 128), F32),
        vmem((sections, slots, 128), F32),
        vmem((slots, width), BF),
        vmem((sections, slots, part), BF),
        vmem((group, slots, lanes), BF),
        vmem((group, slots, lanes), BF),
        vmem((ring, group, slots, lanes), BF),
        vmem((ring, group, slots, lanes), BF),
        vmem((group, slots, 2 * lanes), BF),
        vmem((group, slots, 2 * lanes), BF),
        vmem((slots, width), BF),
        vmem((sections, slots, part), BF),
        vmem((slots, 128), F32),
        vmem((sections, slots, 128), F32),
        vmem((4, slots, width), F32),
        vmem((slots, 2 * part), BF),
        vmem((ring, group, slots, width + part), BF),
    ]
    return communicate(
        functools.partial(routed_kernel, lines, shape),
        ident,
        [source, chosen[:, :, None], chosen[:, None, :], start, gains, main, shrink],
        outs,
        scratch,
        "routed_layer",
        limit=48 * 2**20,
    )


def on_device(
    stream_in,
    segment_ids,
    chosen_rows,
    cotangent,
    dense_prenorm,
    dense_query,
    dense_keys,
    dense_values,
    dense_output,
    dense_midnorm,
    dense_expand,
    dense_shrink,
    routed_prenorm,
    routed_query,
    routed_keys,
    routed_values,
    routed_output,
    routed_midnorm,
    routed_expand,
    routed_shrink,
    router_weight,
):
    sections, dp = lax.axis_size("section"), lax.axis_size("dp")
    section, rank = lax.axis_index("section"), lax.axis_index("dp")
    seqs, rows, width = stream_in.shape
    tokens = seqs * rows
    part = width // sections
    group = HEADS // sections
    ring = dp // group
    total_sel = chosen_rows.shape[1]
    sel = total_sel // dp
    place = lax.rem(rank, ring).astype(jnp.int32).reshape(1)
    lines = Lines(sections, dp, group)
    lanes = 2 * HDIM

    def own_columns(value):
        return lax.dynamic_slice_in_dim(value, section * part, part, value.ndim - 1)

    def own_hidden(expand, shrink):
        inner = expand.shape[1] // dp
        share = inner // sections
        cut = expand.reshape(expand.shape[0], dp, sections, share)
        cut = lax.dynamic_index_in_dim(cut, section, 2, keepdims=False).reshape(expand.shape[0], dp * share)
        return cut, lax.dynamic_slice_in_dim(shrink, section * share, share, 0)

    def own_attention(query, keys, values):
        local = query.shape[0]
        pair = jnp.stack(
            [own_columns(keys).reshape(local, group, HDIM), own_columns(values).reshape(local, group, HDIM)],
            axis=2,
        ).reshape(local, 2 * part)
        return jnp.concatenate([pair, own_columns(query)], axis=1)

    gains = jnp.stack([dense_prenorm, dense_midnorm, routed_prenorm, routed_midnorm, router_weight])
    gains = jnp.pad(gains, ((0, 16 - gains.shape[0]), (0, 0)))
    local = dense_query.shape[0]
    first = own_attention(dense_query, dense_keys, dense_values)
    gains = jnp.pad(gains, ((0, 0), (0, first.shape[1] - local)))
    first = gather_rows(lines, 1, jnp.concatenate([first, gains], axis=0), "first_weights")
    dense_qkv = first[:, :local].reshape(width, 3 * part)
    gains = jnp.transpose(first[:, local:, :local], (1, 0, 2)).reshape(16, width).astype(F32)
    gain_pre, gain_mid = gains[0], gains[1]

    def gather(value):
        value, _ = lax.optimization_barrier((value, first))
        return lax.all_gather(value, "dp", axis=0, tiled=True)

    expand_cut, shrink_cut = own_hidden(dense_expand, dense_shrink)
    rest = gather(jnp.concatenate([own_columns(dense_output), expand_cut, shrink_cut], axis=1))
    hidden_size = expand_cut.shape[1]
    dense_out, dense_exp, dense_shr = (
        rest[:, :part],
        rest[:, part : part + hidden_size],
        rest[:, part + hidden_size :],
    )
    expand_cut, shrink_cut = own_hidden(routed_expand, routed_shrink)
    routed_main = gather(
        jnp.concatenate(
            [own_attention(routed_query, routed_keys, routed_values), own_columns(routed_output), expand_cut],
            axis=1,
        )
    )
    routed_shr = gather(shrink_cut)

    first_of = jnp.sum(
        (segment_ids[:, None, :] < jnp.arange(DOCS, dtype=jnp.int32)[None, :, None]).astype(jnp.int32), axis=2
    )

    def document(positions):
        shape = (seqs,) + (1,) * (positions.ndim - 1)
        found = jnp.zeros(positions.shape, jnp.int32)
        for c in range(1, DOCS):
            found = found + (positions >= first_of[:, c].reshape(shape)).astype(jnp.int32)
        return found

    def pick(table, index):
        shape = (seqs,) + (1,) * (index.ndim - 1)
        out = jnp.zeros(index.shape, jnp.int32)
        for c in range(DOCS):
            out = jnp.where(index == c, table[:, c].reshape(shape), out)
        return out

    blocks = jnp.arange(group, dtype=jnp.int32) * ring + place[0]
    attended_pos = blocks[:, None] * rows + jnp.arange(rows, dtype=jnp.int32)[None, :]
    attended_pos = jnp.broadcast_to(attended_pos[None], (seqs, group, rows))
    start = pick(first_of, document(attended_pos))[:, :, None, :]
    chosen_doc = document(chosen_rows)
    first_slot = jnp.sum(
        (chosen_doc[:, None, :] < jnp.arange(DOCS, dtype=jnp.int32)[None, :, None]).astype(jnp.int32), axis=2
    )
    chosen_start = pick(first_slot, chosen_doc).reshape(seqs, group, ring, sel)
    routed_start = lax.dynamic_index_in_dim(chosen_start, place[0], 2, keepdims=False)
    routed_start = routed_start.reshape(seqs, 1, group * sel)

    def pack(value):
        value = value.reshape(seqs, 2, rows // 2, group, HDIM)
        return jnp.transpose(value, (0, 2, 3, 1, 4)).reshape(tokens // 2, 2 * part)

    def unpack(value):
        value = value.reshape(seqs, rows // 2, group, 2, HDIM)
        return jnp.transpose(value, (0, 3, 1, 2, 4)).reshape(tokens, part)

    value = stream_in.reshape(tokens, width).astype(F32)
    grad_top = cotangent.reshape(tokens, width)
    inv_in = inverse_rms(value)
    normed = (value * inv_in * gain_pre).astype(BF)
    qkv = matmul(normed, dense_qkv).astype(BF)
    pairs, queries = dense_to_heads(
        lines, 2, qkv[:, : 2 * part], pack(qkv[:, 2 * part :]), "dense_to_heads"
    )
    queries = queries.reshape(group, seqs, rows // 2, lanes)
    pairs = pairs.reshape(ring, group, seqs, rows, lanes)
    mixed, mixed_turned, lse = dense_forward(place, queries, pairs, start)
    packed = (tokens // 2, group * lanes)
    (mixed,) = swap_blocks(
        lines, 3, "z", [mixed.reshape(group, tokens // 2, lanes)], [(packed, BF)], [(0, slot, 0, columns(lanes))],
        "dense_mixed",
    )
    mixed = gather_columns(lines, 4, unpack(mixed), "dense_mixed_columns")
    attended = gather_columns(lines, 5, matmul(mixed, dense_out).astype(BF), "dense_attended")
    middle_value = value + attended.astype(F32)
    inv_mid = inverse_rms(middle_value)
    normed_mid = (middle_value * inv_mid * gain_mid).astype(BF)
    hidden_pre = matmul(normed_mid, dense_exp)
    hidden = jax.nn.gelu(hidden_pre).astype(BF)
    fed = scatter_columns(lines, 6, matmul(hidden, dense_shr).astype(BF), None, "dense_fed")
    after_dense = own_columns(middle_value) + fed

    source = jnp.concatenate([after_dense.astype(BF), own_columns(grad_top)], axis=1)
    (
        returned,
        added,
        r_normed,
        r_grad_qkv,
        r_mixed,
        r_grad_attended,
        r_normed_mid,
        r_grad_pre,
        r_hidden,
        r_fed_low,
        r_vectors,
    ) = routed_layer(
        lines,
        7,
        source.reshape(seqs, rows, 2 * part),
        chosen_rows,
        routed_start,
        gains[2:5],
        routed_main,
        routed_shr,
        (seqs, sel, rows, width, part),
    )
    stream_out = (after_dense + added.reshape(tokens, part).astype(F32)).astype(BF).reshape(seqs, rows, part)

    def outer(left, right):
        return contract(left, right, 0, 0).astype(BF)

    def column(vector):
        wide = lax.dynamic_update_slice(jnp.zeros((width,), F32), vector, (section * part,))
        return wide[:, None]

    def reduce_dp(parts, vectors):
        last = jnp.concatenate([column(v) for v in vectors], axis=1)
        last = jnp.pad(last, ((0, 0), (0, 128 - last.shape[1]))).astype(BF)
        return lax.psum_scatter(jnp.concatenate(parts + [last], axis=1), "dp", scatter_dimension=0, tiled=True)

    routed_shard = reduce_dp(
        [
            outer(r_normed, r_grad_qkv),
            outer(r_mixed, r_grad_attended),
            outer(r_normed_mid, r_grad_pre),
            outer(r_hidden, r_fed_low),
        ],
        [r_vectors[0], r_vectors[1], r_vectors[2]],
    )

    grad_after = grad_top.astype(F32) + returned.reshape(tokens, width).astype(F32)
    fed_low = grad_after.astype(BF)
    _, gelu_pull = jax.vjp(jax.nn.gelu, hidden_pre)
    grad_pre = gelu_pull(contract(fed_low, dense_shr, 1, 1))[0].astype(BF)
    grad_normed = contract(grad_pre, dense_exp, 1, 1)
    scalar = jnp.sum(grad_normed * middle_value * gain_mid, axis=1)
    grad_normed, scalar = scatter_columns(lines, 8, grad_normed.astype(BF), scalar, "dense_back_mid")
    middle_own = own_columns(middle_value)
    grad_gain_mid = jnp.sum(grad_normed * middle_own * inv_mid, axis=0)
    grad_middle = (
        inv_mid * (grad_normed * own_columns(gain_mid))
        - middle_own * (inv_mid * inv_mid * inv_mid) * (scalar * (1.0 / width))[:, None]
        + own_columns(grad_after)
    )
    grad_attended = grad_middle.astype(BF)
    grad_mixed = scatter_columns(
        lines, 9, contract(grad_attended, dense_out, 1, 1).astype(BF), None, "dense_back_mixed"
    ).astype(BF)
    (grad_heads,) = swap_blocks(
        lines, 10, "z", [pack(grad_mixed)], [((group, tokens // 2, lanes), BF)], [(0, columns(lanes), 0, slot)],
        "dense_grad_to_heads",
    )
    dq, dkv = dense_backward(
        place,
        queries,
        grad_heads.reshape(group, seqs, rows // 2, lanes),
        pairs,
        start,
        mixed_turned,
        lse,
    )
    dkv, dq = dense_from_heads(
        lines, 11, dkv.reshape(ring, group, tokens, lanes), dq.reshape(group, tokens // 2, lanes), "dense_from_heads"
    )
    grad_qkv = jnp.concatenate([dkv, unpack(dq)], axis=1)
    grad_normed = contract(grad_qkv, dense_qkv, 1, 1)
    scalar = jnp.sum(grad_normed * value * gain_pre, axis=1)
    grad_normed, scalar = scatter_columns(lines, 12, grad_normed.astype(BF), scalar, "dense_back_in")
    value_own = own_columns(value)
    grad_gain_pre = jnp.sum(grad_normed * value_own * inv_in, axis=0)
    grad_in = (
        inv_in * (grad_normed * own_columns(gain_pre))
        - value_own * (inv_in * inv_in * inv_in) * (scalar * (1.0 / width))[:, None]
    )
    stream_grad = (grad_middle + grad_in).astype(BF).reshape(seqs, rows, part)
    dense_shard = reduce_dp(
        [outer(normed, grad_qkv), outer(mixed, grad_attended), outer(normed_mid, grad_pre), outer(hidden, fed_low)],
        [grad_gain_pre, grad_gain_mid],
    )

    def finish(ident, shard, count, name):
        local, wide = shard.shape
        got = gather_columns(lines, ident, shard, name).reshape(local, sections, wide)
        got = jnp.transpose(got, (1, 0, 2))
        pair = got[:, :, : 2 * part].reshape(sections, local, group, 2, HDIM)
        keys = jnp.transpose(pair[:, :, :, 0], (1, 0, 2, 3)).reshape(local, width).astype(F32)
        values = jnp.transpose(pair[:, :, :, 1], (1, 0, 2, 3)).reshape(local, width).astype(F32)
        query = jnp.transpose(got[:, :, 2 * part : 3 * part], (1, 0, 2)).reshape(local, width).astype(F32)
        output = jnp.transpose(got[:, :, 3 * part : 4 * part], (1, 0, 2)).reshape(local, width).astype(F32)
        share = hidden_size // dp
        expand = got[:, :, 4 * part : 4 * part + hidden_size].reshape(sections, local, dp, share)
        expand = jnp.transpose(expand, (1, 2, 0, 3)).reshape(local, sections * hidden_size).astype(F32)
        shrink = got[:, :, 4 * part + hidden_size : 4 * part + hidden_size + width]
        shrink = shrink.reshape(sections * local, width).astype(F32)
        vectors = jnp.sum(got[:, :, 4 * part + hidden_size + width :].astype(F32), axis=0)
        return [vectors[:, i] for i in range(count)], [query, keys, values, output, expand, shrink]

    r_vector, r_grads = finish(13, routed_shard, 3, "routed_weight_grads")
    d_vector, d_grads = finish(14, dense_shard, 2, "dense_weight_grads")
    return (
        (stream_out, stream_grad)
        + (d_vector[0], *d_grads[:4], d_vector[1], *d_grads[4:])
        + (r_vector[0], *r_grads[:4], r_vector[1], *r_grads[4:])
        + (r_vector[2],)
    )


def solution(mesh):
    streams, row, vector, copied = P(None, "dp", None), P("dp", None), P("dp"), P()
    layer = (vector, row, row, row, row, vector, row, row)
    outs = (P(None, "dp", "section"),) * 2 + layer + layer + (vector,)
    return jax.shard_map(
        on_device,
        mesh=mesh,
        in_specs=(streams, copied, copied, streams) + layer + layer + (vector,),
        out_specs=outs,
        check_vma=False,
    )
```

time: 993 us -> 700 us (0.70)
  Pallas kernels: 588 us -> 406 us
  matrix products: 74.2 us -> 33.6 us
  blocking collectives: 35.4 us -> 0 us
  waiting for transfers between devices: 129 us -> 96.1 us
  local copies, waits for them, and re-layouts: 77 us -> 105 us
  other arithmetic: 63.8 us -> 37.2 us
    pallas_call x40 -> x14, Pallas kernels: 562 us -> 384 us  [communicate(): pl.pallas_call(kernel, out_shape=[jax.ShapeDtypeStruct(s, d) for s, d in...]
    all_gather x2 -> x0, blocking collectives: 35.4 us -> none  [gather(): return lax.all_gather(value, 'dp', axis=0, tiled=True)]
    reduce_scatter x8 -> x2, waiting for transfers between devices: 128 us -> 95.3 us  [reduce_dp(): lax.psum_scatter(jnp.concatenate(parts + [last], axis=1), 'dp', scatter_d...]
    reduce_sum x22 -> x4, other arithmetic: 31.3 us -> 5.67 us  [the longest x1 2.28 us: on_device(): grad_gain_mid = jnp.sum(grad_normed * middle_own * inv_mid, axis=0)]
    dot_general x8 -> x4, matrix products: 28.4 us -> 6.94 us  [matmul(): return jnp.dot(left, right, preferred_element_type=F32)]
    dot_general x16 -> x12, matrix products: 42.3 us -> 26.7 us  [contract(): lax.dot_general(left, right, (((ldim,), (rdim,)), ((), ())), preferred_el...]
    unnamed x161 -> x165, local copies, waits for them, and re-layouts: 18.8 us -> 32 us
    reshape x4 -> x8, local copies, waits for them, and re-layouts: 1.51 us -> 12.3 us  [the longest x2 7.06 us: finish(): gather_columns(lines, ident, shard, name).reshape(local, sections, wide)]
  transfers between devices with their start and end apart: 14 -> 5, of which waited for: 4 -> 2; matrix products, arithmetic and copies ran while one was open for 13% -> 9% of each run, Pallas kernels for 43% -> 22%
where the time goes in v2:
time: 700 us; the launch traced here: 693 us
  Pallas kernels  406 us (58%)
  local copies, waits for them, and re-layouts  105 us (15%)
  waiting for transfers between devices  96.1 us (14%)
  other arithmetic  37.2 us (5%)
  matrix products  33.6 us (5%)
  between operations  15.6 us (2%)
    pallas_call x14, Pallas kernels, communicate(): pl.pallas_call(kernel, out_shape=[jax.ShapeDtypeStruct(s, d) for s, d in...  384 us
    reduce_scatter x2, waiting for transfers between devices, reduce_dp(): lax.psum_scatter(jnp.concatenate(parts + [last], axis=1), 'dp', scatter_d...  95.3 us
    unnamed x165, local copies, waits for them, and re-layouts  32 us
    dot_general x12, matrix products, contract(): lax.dot_general(left, right, (((ldim,), (rdim,)), ((), ())), preferred_el...  26.7 us
  transfers between devices with their start and end apart: 5, of which 2 were waited for; matrix products, arithmetic and copies ran while one was open for 9% of the time, Pallas kernels for 22%

profile of v2, /device:TPU:0, one launch (start us, length us, event | category | flops | bytes accessed | tf_op | source)
XLA Modules:
  0.0 693.4 jit_solution(6736204041394078148)
XLA Ops:
  10.2 22.4 %first_weights.1 = bf16[8,144,768]{2,1,0:T(8,128)(2,1)S(1)} custom-call(bf16[144,768]{1,0:T(8,128)(2,1)S(1)} %fusion.37.x_ref), custom_call_target="tpu_custom_call" | custom-call | tf_op jit(solution)/shard_map/first_weights/pallas_call | solution.py:99
  32.6 1.8 reshape.455
  34.4 2.6 reshape.448
  37.0 4.3 dynamic-slice_reduce_fusion
  41.3 1.8 constant_dynamic-slice_fusion.2
  48.5 1.8 pad_maximum_fusion.2
  56.1 57.6 %dense_to_heads.1 = (bf16[2,4,768,128]{3,2,1,0:T(8,128)(2,1)S(1)}, bf16[4,384,128]{2,1,0:T(8,128)(2,1)S(1)}) custom-call(bf16[768,512]{1,0:T(8,128)(2,1)S(1)} %slice.237.p_ref, bf16[384,512]{1,0:T(8,128)(2,1)S(1)} %reshape.493.q_ref), custom_call_target="tpu_custom_call" | custom-call | tf_op jit(solution)/shard_map/dense_to_heads/pallas_call | solution.py:99
  114.8 9.2 %dense_attention.1 = (bf16[4,3,128,128]{3,2,1,0:T(8,128)(2,1)S(1)}, bf16[3,4,64,256]{3,2,1,0:T(8,128)(2,1)S(1)}, f32[3,4,1,256]{3,2,1,0:T(1,128)S(1)}) custom-call(s32[1]{0:T(128)} %bitcast.1.place_ref, bf16[4,3,128,128]{3,2,1,0:T(8,128)(2,1)S(1)} %bitcast.184, bf16[2,4,3,256,128]{4,3,2,1,0:T(8,128)(2,1)S(1)} %bitcast.181, ...), custom_call_target="tpu_custom_call" | custom-call | tf_op jit(solution)/shard_map/dense_attention/pallas_call | solution.py:477
  126.1 19.8 %dense_mixed.1 = bf16[384,512]{1,0:T(8,128)(2,1)S(1)} custom-call(bf16[4,384,128]{2,1,0:T(8,128)(2,1)S(1)} %bitcast.188), custom_call_target="tpu_custom_call" | custom-call | tf_op jit(solution)/shard_map/dense_mixed/pallas_call | solution.py:99
  147.7 13.2 %dense_mixed_columns.1 = bf16[768,1024]{1,0:T(8,128)(2,1)S(1)} custom-call(bf16[768,256]{1,0:T(8,128)(2,1)S(1)} %reshape.494.x_ref), custom_call_target="tpu_custom_call" | custom-call | tf_op jit(solution)/shard_map/dense_mixed_columns/pallas_call | solution.py:99
  171.7 1.8 constant_dynamic-slice_fusion.8
  176.1 3.5 bitcast_convert_fusion
  179.6 1.7 convolution_convert_fusion.6.x_ref
  181.4 12.5 %dense_attended.1 = bf16[768,1024]{1,0:T(8,128)(2,1)S(1)} custom-call(bf16[768,256]{1,0:T(8,128)(2,1)S(1)} %convolution_convert_fusion.6.x_ref), custom_call_target="tpu_custom_call" | custom-call | tf_op jit(solution)/shard_map/dense_attended/pallas_call | solution.py:99
  198.0 1.8 fusion.15
  199.8 2.0 fusion.18.refs_0_
  201.8 11.9 %dense_fed.1 = f32[768,256]{1,0:T(8,128)S(1)} custom-call(bf16[768,1024]{1,0:T(8,128)(2,1)S(1)} %fusion.18.refs_0_), custom_call_target="tpu_custom_call" | custom-call | tf_op jit(solution)/shard_map/dense_fed/pallas_call | solution.py:99
  215.4 105.7 %routed_layer.1 = (bf16[3,256,1024]{2,1,0:T(8,128)(2,1)S(1)}, bf16[3,256,256]{2,1,0:T(8,128)(2,1)S(1)}, bf16[96,1024]{1,0:T(8,128)(2,1)S(1)}, bf16[96,768]{1,0:T...) custom-call(bf16[3,256,512]{2,1,0:T(8,128)(2,1)S(1)} %bitcast.183, ...), custom_call_target="tpu_custom_call" | custom-call | tf_op jit(solution)/shard_map/routed_layer/pallas_call | solution.py:99
  322.2 6.9 fusion.6
  329.2 2.0 multiply_reduce_fusion.1
  331.3 17.1 %dense_back_mid.1 = (f32[768,256]{1,0:T(8,128)S(1)}, f32[8,128]{1,0:T(8,128)S(1)}) custom-call(bf16[768,1024]{1,0:T(8,128)(2,1)S(1)} %get-tuple-element.200.refs_0_, f32[8,128]{1,0:T(8,128)S(1)} %pad_bitcast_fusion.1.refs_1_), custom_call_target="tpu_custom_call" | custom-call | tf_op jit(solution)/shard_map/dense_back_mid/pallas_call | solution.py:99
  348.4 2.3 multiply_reduce_fusion.4
  352.2 15.5 %dense_back_mixed.1 = f32[768,256]{1,0:T(8,128)S(1)} custom-call(bf16[768,1024]{1,0:T(8,128)(2,1)S(1)} %convolution_convert_fusion.2.refs_0_), custom_call_target="tpu_custom_call" | custom-call | tf_op jit(solution)/shard_map/dense_back_mixed/pallas_call | solution.py:99
  368.1 2.0 copy.317
  370.0 2.7 reshape.495.refs_0_
  372.7 11.6 %dense_grad_to_heads.1 = bf16[4,384,128]{2,1,0:T(8,128)(2,1)S(1)} custom-call(bf16[384,512]{1,0:T(8,128)(2,1)S(1)} %reshape.495.refs_0_), custom_call_target="tpu_custom_call" | custom-call | tf_op jit(solution)/shard_map/dense_grad_to_heads/pallas_call | solution.py:99
  384.3 12.5 %dense_attention_grad.1 = (bf16[4,3,128,128]{3,2,1,0:T(8,128)(2,1)S(1)}, bf16[2,4,3,256,128]{4,3,2,1,0:T(8,128)(2,1)S(1)}) custom-call(s32[1]{0:T(128)} %bitcast.1.place_ref, bf16[4,3,128,128]{3,2,1,0:T(8,128)(2,1)S(1)} %bitcast.185, bf16[4,3,128,128]{3,2,1,0:T(8,128)(2,1)S(1)} %bitcast.186, bf16[2,4,3,256,128]{4,3,2,1,0:T(8,128)(2,1)S(1)} %bitcast.182, ...), custom_call_target="tpu_custom_call" | custom-call | tf_op jit(solution)/shard_map/dense_attention_grad/pallas_call | solution.py:549
  396.9 27.0 %dense_from_heads.1 = (bf16[768,512]{1,0:T(8,128)(2,1)S(1)}, bf16[384,512]{1,0:T(8,128)(2,1)S(1)}) custom-call(bf16[2,4,768,128]{3,2,1,0:T(8,128)(2,1)S(1)} %bitcast.187, bf16[4,384,128]{2,1,0:T(8,128)(2,1)S(1)} %bitcast.189), custom_call_target="tpu_custom_call" | custom-call | tf_op jit(solution)/shard_map/dense_from_heads/pallas_call | solution.py:99
  427.4 3.5 multiply_reduce_fusion
  430.9 14.1 %dense_back_in.1 = (f32[768,256]{1,0:T(8,128)S(1)}, f32[8,128]{1,0:T(8,128)S(1)}) custom-call(bf16[768,1024]{1,0:T(8,128)(2,1)S(1)} %get-tuple-element.198.refs_0_, f32[8,128]{1,0:T(8,128)S(1)} %pad_bitcast_fusion.refs_1_), custom_call_target="tpu_custom_call" | custom-call | tf_op jit(solution)/shard_map/dense_back_in/pallas_call | solution.py:99
  448.6 2.1 convert_dynamic-update-slice_fusion.3
  451.5 2.1 convert_dynamic-update-slice_fusion.2
  460.2 1.8 fusion.17
  463.2 2.2 convert_dynamic-update-slice_fusion.1
  465.4 2.1 convert_dynamic-update-slice_fusion
  468.3 63.4 %reduce-scatter.3.cloned.1.call-done.x_ref = bf16[128,3200]{1,0:T(8,128)(2,1)} async-done(((bf16[1024,3200]{1,0:T(8,128)(2,1)}), bf16[128,3200]{1,0:T(8,128)(2,1)}) %reduce-scatter.3.cloned.1.call-update) | async-done | bytes 819216 | tf_op jit(solution)/shard_map/reduce_scatter | solution.py:1118
  532.9 27.8 %dense_weight_grads.1 = bf16[128,12800]{1,0:T(8,128)(2,1)S(1)} custom-call(bf16[128,3200]{1,0:T(8,128)(2,1)S(1)} %copy-done.6), custom_call_target="tpu_custom_call" | custom-call | tf_op jit(solution)/shard_map/dense_weight_grads/pallas_call | solution.py:99
  560.6 3.7 copy.319
  564.3 1.9 slice.247
  567.1 2.1 slice_convert_fusion.4
  569.2 3.4 slice_convert_fusion.1
  572.6 31.9 %reduce-scatter.5.cloned.1.call-done.x_ref = bf16[128,3200]{1,0:T(8,128)(2,1)} async-done(((bf16[1024,3200]{1,0:T(8,128)(2,1)}), bf16[128,3200]{1,0:T(8,128)(2,1)}) %reduce-scatter.5.cloned.1.call-update) | async-done | bytes 819216 | tf_op jit(solution)/shard_map/reduce_scatter | solution.py:1118
  605.7 27.8 %routed_weight_grads.1 = bf16[128,12800]{1,0:T(8,128)(2,1)S(1)} custom-call(bf16[128,3200]{1,0:T(8,128)(2,1)S(1)} %copy-done.7), custom_call_target="tpu_custom_call" | custom-call | tf_op jit(solution)/shard_map/routed_weight_grads/pallas_call | solution.py:99
  633.4 3.4 copy.320
  637.8 2.1 slice_convert_fusion.2
  639.9 1.9 slice.257
  641.8 1.7 slice_convert_fusion
  644.0 2.0 copy.299
  646.1 2.1 fusion.35
  648.2 2.0 copy.300
  650.2 2.0 copy.301
  652.3 2.0 copy.302
  654.3 2.8 convert_bitcast_fusion.1
  657.1 3.0 copy.289
  660.1 3.1 reshape.479
  663.2 2.9 copy.290
  666.6 2.0 copy.303
  668.6 2.1 fusion.33
  670.7 2.0 copy.304
  672.8 2.0 copy.305
  674.8 2.0 copy.306
  678.4 3.2 copy.297
  681.6 3.1 reshape.485
  684.6 1.8 copy.298
  (263 shorter events, 63.7 us)
Async XLA Ops:
  7.2 172.4 %all-gather.4.cloned.1.call-start = ((), (), s32[]{:S(2)}) async-start(), calls=%async_computation.2 | async-start | bytes 5308416 | tf_op jit(solution)/shard_map/all_gather | solution.py:999
  44.0 170.0 %all-gather.8.cloned.1.call-start = ((), (), s32[]{:S(2)}) async-start(), calls=%async_computation.4 | async-start | bytes 2359296 | tf_op jit(solution)/shard_map/all_gather | solution.py:999
  44.8 169.2 %all-gather.6.cloned.1.call-start = ((), (), s32[]{:S(2)}) async-start(), calls=%async_computation.3 | async-start | bytes 4718592 | tf_op jit(solution)/shard_map/all_gather | solution.py:999
  45.6 5.2 copy-start.31
  50.4 481.4 %reduce-scatter.3.cloned.1.call-start = ((), (), s32[]{:S(2)}) async-start(), calls=%async_computation.5 | async-start | bytes 7372800 | tf_op jit(solution)/shard_map/reduce_scatter | solution.py:1118
  50.7 3.0 copy-start.44
  51.9 1.8 copy-start.52
  53.8 59.9 %copy-start.50 = (s32[3,2048]{1,0:T(4,128)S(1)}, s32[3,2048]{1,0:T(4,128)}, u32[]{:S(2)}) copy-start(s32[3,2048]{1,0:T(4,128)} %param.22) | copy-start | bytes 73732
  160.9 20.5 %copy-start.4 = (bf16[768,1024]{1,0:T(8,128)(2,1)}, bf16[768,1024]{1,0:T(8,128)(2,1)S(1)}, u32[]{:S(2)}) copy-start(bf16[768,1024]{1,0:T(8,128)(2,1)S(1)} %dense_mixed_columns.1) | copy-start | bytes 4718596
  179.6 14.2 %copy-start.32 = (bf16[3,256,1024]{2,1,0:T(8,128)(2,1)S(1)}, bf16[3,256,1024]{2,1,0:T(8,128)(2,1)}, u32[]{:S(2)}) copy-start(bf16[3,256,1024]{2,1,0:T(8,128)(2,1)} %param.21) | copy-start | bytes 4718596
  193.9 1.1 copy-start
  193.9 4.1 copy-start.48
  193.9 4.1 copy-start.65
  195.0 18.7 %copy-start.35 = (f32[768,1024]{1,0:T(8,128)}, f32[768,1024]{1,0:T(8,128)S(1)}, u32[]{:S(2)}) copy-start(f32[768,1024]{1,0:T(8,128)S(1)} %get-tuple-element.202) | copy-start | bytes 9437188
  199.8 2.0 copy-start.68
  201.8 12.1 %copy-start.45 = (bf16[768,256]{1,0:T(8,128)(2,1)S(1)}, bf16[768,256]{1,0:T(8,128)(2,1)}, u32[]{:S(2)}) copy-start(bf16[768,256]{1,0:T(8,128)(2,1)} %constant_dynamic-slice_fusion.8) | copy-start | bytes 1179652
  215.4 105.8 %copy-start.43 = (bf16[3,256,1024]{2,1,0:T(8,128)(2,1)S(1)}, bf16[3,256,1024]{2,1,0:T(8,128)(2,1)}, u32[]{:S(2)}) copy-start(bf16[3,256,1024]{2,1,0:T(8,128)(2,1)} %param.24) | copy-start | bytes 4718596
  215.4 106.8 %copy-start.69 = (f32[768,1024]{1,0:T(8,128)S(1)}, f32[768,1024]{1,0:T(8,128)}, u32[]{:S(2)}) copy-start(f32[768,1024]{1,0:T(8,128)} %copy-done.68) | copy-start | bytes 9437188
  321.1 1.0 copy-start.10
  321.1 1.0 copy-start.12
  321.1 1.0 copy-start.14
  321.1 1.0 copy-start.16
  321.2 1.0 copy-start.18
  321.2 1.0 copy-start.21
  321.2 1.0 copy-start.26
  321.2 1.0 copy-start.29
  321.2 7.9 %slice-start = ((s8[4718592]{0:T(1024)(128)(4,1)}), s8[4194304]{0:T(1024)(128)(4,1)S(1)}, s32[]{:S(2)}) async-start(s8[4718592]{0:T(1024)(128)(4,1)} %bitcast.233), calls=%async_computation.7 | async-start | bytes 8388608
  322.2 26.2 %copy-start.41 = (f32[768,1024]{1,0:T(8,128)}, f32[768,1024]{1,0:T(8,128)S(1)}, u32[]{:S(2)}) copy-start(f32[768,1024]{1,0:T(8,128)S(1)} %convert_add_fusion) | copy-start | bytes 9437188
  322.2 6.9 copy-start.1
  322.2 6.9 copy-start.33
  322.2 6.9 slice-start.1
  322.2 6.9 copy-start.66
  329.2 2.1 copy-start.71
  329.2 19.2 %copy-start.55 = (f32[768]{0:T(1024)S(1)}, f32[768]{0:T(1024)}, u32[]{:S(2)}) copy-start(f32[768]{0:T(1024)} %copy-done.54) | copy-start | bytes 9220
  329.2 19.2 %copy-start.56 = (f32[768]{0:T(1024)S(1)}, f32[768]{0:T(1024)}, u32[]{:S(2)}) copy-start(f32[768]{0:T(1024)} %get-tuple-element.216) | copy-start | bytes 9220
  329.2 19.2 %copy-start.67 = (f32[1,256]{1,0:T(1,128)S(1)}, f32[1,256]{1,0:T(1,128)}, u32[]{:S(2)}) copy-start(f32[1,256]{1,0:T(1,128)} %constant_dynamic-slice_fusion.1) | copy-start | bytes 3076
  367.7 16.6 %copy-start.3 = (bf16[4,384,128]{2,1,0:T(8,128)(2,1)S(1)}, bf16[4,384,128]{2,1,0:T(8,128)(2,1)}, u32[]{:S(2)}) copy-start(bf16[4,384,128]{2,1,0:T(8,128)(2,1)} %copy-done.2) | copy-start | bytes 1179652
  367.7 16.6 %copy-start.9 = (bf16[3,4,64,256]{3,2,1,0:T(8,128)(2,1)S(1)}, bf16[3,4,64,256]{3,2,1,0:T(8,128)(2,1)}, u32[]{:S(2)}) copy-start(bf16[3,4,64,256]{3,2,1,0:T(8,128)(2,1)} %copy-done.8) | copy-start | bytes 1179652
  367.7 16.6 %copy-start.24 = (f32[3,4,1,256]{3,2,1,0:T(1,128)S(1)}, f32[3,4,1,256]{3,2,1,0:T(1,128)}, u32[]{:S(2)}) copy-start(f32[3,4,1,256]{3,2,1,0:T(1,128)} %copy-done.23) | copy-start | bytes 36868
  423.9 3.4 copy-start.34
  423.9 3.4 copy-start.53
  427.3 17.6 %copy-start.40 = (f32[768,1024]{1,0:T(8,128)S(1)}, f32[768,1024]{1,0:T(8,128)}, u32[]{:S(2)}) copy-start(f32[768,1024]{1,0:T(8,128)} %bitcast_convert_fusion) | copy-start | bytes 9437188
  427.3 17.6 %copy-start.46 = (bf16[768,768]{1,0:T(8,128)(2,1)S(1)}, bf16[768,768]{1,0:T(8,128)(2,1)}, u32[]{:S(2)}) copy-start(bf16[768,768]{1,0:T(8,128)(2,1)} %constant_dynamic-update-slice_fusion) | copy-start | bytes 3538948
  427.4 17.6 %copy-start.49 = (f32[768]{0:T(1024)S(1)}, f32[768]{0:T(1024)}, u32[]{:S(2)}) copy-start(f32[768]{0:T(1024)} %rsqrt.28) | copy-start | bytes 9220
  445.0 1.6 copy-start.5
  445.0 1.6 copy-start.38
  445.0 2.3 copy-start.72
  446.6 2.0 copy-start.36
  448.6 2.1 copy-start.42
  448.6 2.8 copy-start.70
  451.5 2.2 copy-start.51
  451.5 2.2 copy-start.64
  453.6 2.9 copy-start.39
  457.5 2.7 copy-start.28
  457.5 2.7 copy-start.30
  457.5 4.5 copy-start.19
  457.5 4.5 copy-start.22
  457.5 5.7 copy-start.15
  457.5 5.7 copy-start.17
  457.6 7.8 %copy-start.11 = (bf16[96,1024]{1,0:T(8,128)(2,1)S(1)}, bf16[96,1024]{1,0:T(8,128)(2,1)}, u32[]{:S(2)}) copy-start(bf16[96,1024]{1,0:T(8,128)(2,1)} %copy-done.10) | copy-start | bytes 589828
  457.6 7.8 %copy-start.13 = (bf16[96,1024]{1,0:T(8,128)(2,1)S(1)}, bf16[96,1024]{1,0:T(8,128)(2,1)}, u32[]{:S(2)}) copy-start(bf16[96,1024]{1,0:T(8,128)(2,1)} %copy-done.12) | copy-start | bytes 589828
  457.6 147.0 %reduce-scatter.5.cloned.1.call-start = ((), (), s32[]{:S(2)}) async-start(), calls=%async_computation.6 | async-start | bytes 7372800 | tf_op jit(solution)/shard_map/reduce_scatter | solution.py:1118
  531.7 1.1 copy-start.6
  604.5 1.1 copy-start.7
  (16 other events, 10.7 us)
Sparse Core Ops, SparseCore 0:
  44.1 80.8 all-gather.3
  127.2 34.2 all-gather.7
  163.6 46.4 all-gather.5
  457.6 74.0 reduce-scatter.2
  533.9 70.6 reduce-scatter.4

commit v3 on v2

v3 whole, which is shorter than its diff:
```python
import functools

import jax
import jax.numpy as jnp
from jax import lax
from jax.experimental import pallas as pl
from jax.experimental.pallas import tpu as pltpu
from jax.sharding import PartitionSpec as P

HEADS = 16
HDIM = 64
DOCS = 8
EPS = 1e-06
NEG = -1e30
SCALE = HDIM ** (-0.5)
VMEM = 32 * 2**20
MESH = pl.DeviceIdType.MESH
BF = jnp.bfloat16
F32 = jnp.float32


def matmul(left, right):
    return jnp.dot(left, right, preferred_element_type=F32)


def contract(left, right, ldim, rdim):
    return lax.dot_general(left, right, (((ldim,), (rdim,)), ((), ())), preferred_element_type=F32)


class Lines:
    def __init__(self, sections, dp, group):
        self.sizes = {"section": sections, "z": group, "core": dp // group}
        self.ring = dp // group

    def place(self, kind):
        if kind == "section":
            return lax.axis_index("section")
        index = lax.axis_index("dp")
        return index // self.ring if kind == "z" else lax.rem(index, self.ring)

    def device(self, kind, place):
        if kind == "section":
            return {"section": place}
        index = lax.axis_index("dp")
        if kind == "z":
            return {"dp": place * self.ring + lax.rem(index, self.ring)}
        return {"dp": (index // self.ring) * self.ring + place}

    def peers(self, kind):
        size = self.sizes[kind]
        me = self.place(kind)
        return [lax.rem(me + step, size) for step in range(1, size)]


class Copies:
    def __init__(self, lines, send, recv):
        self.lines, self.send, self.recv, self.used = lines, send, recv, 0

    def greet(self, kinds):
        barrier = pltpu.get_barrier_semaphore()
        count = 0
        for kind in kinds:
            for peer in self.lines.peers(kind):
                pl.semaphore_signal(
                    barrier, inc=1, device_id=self.lines.device(kind, peer), device_id_type=MESH
                )
                count += 1
        pl.semaphore_wait(barrier, count)

    def start(self, kind, peer, src, dst):
        copy = pltpu.make_async_remote_copy(
            src_ref=src,
            dst_ref=dst,
            send_sem=self.send.at[self.used],
            recv_sem=self.recv.at[self.used],
            device_id=self.lines.device(kind, peer),
            device_id_type=MESH,
        )
        self.used += 1
        copy.start()
        return copy

    def swap(self, kind, src, dst):
        me = self.lines.place(kind)
        return [self.start(kind, peer, src(peer), dst(me)) for peer in self.lines.peers(kind)]


def wait(copies):
    for copy in copies:
        copy.wait()


def semaphores(count):
    return [pltpu.SemaphoreType.DMA((count,)), pltpu.SemaphoreType.DMA((count,))]


def communicate(kernel, ident, arrays, shapes, scratch, name, limit=24 * 2**20):
    vmem = pl.BlockSpec(memory_space=pltpu.VMEM)
    return pl.pallas_call(
        kernel,
        out_shape=[jax.ShapeDtypeStruct(s, d) for s, d in shapes],
        in_specs=[vmem] * len(arrays),
        out_specs=[vmem] * len(shapes),
        scratch_shapes=scratch,
        compiler_params=pltpu.CompilerParams(
            collective_id=ident, has_side_effects=True, vmem_limit_bytes=limit
        ),
        name=name,
    )(*arrays)


def span(place, width):
    return pl.ds(pl.multiple_of(place * width, width), width)


def square(lines):
    me = lines.place("section")
    low, high = lax.rem(me, 2), me // 2
    return high * 2 + 1 - low, (1 - high) * 2 + low, (1 - high) * 2 + 1 - low


def pieces_of(rows):
    half = rows // 2
    return (2, half // 2) if half % 32 == 0 else (1, half)


class SquareGather:
    @staticmethod
    def count(rows):
        return 6 * pieces_of(rows)[0]

    def __init__(self, copies, x_ref, o_ref):
        self.copies, self.x_ref, self.o_ref = copies, x_ref, o_ref
        self.width = x_ref.shape[1]
        self.me = copies.lines.place("section")
        near, far, _ = square(copies.lines)
        pieces, step = pieces_of(x_ref.shape[0])
        half = x_ref.shape[0] // 2
        self.parts = [
            (pl.ds(h * half + j * step, step), one, two)
            for j in range(pieces)
            for h, (one, two) in enumerate(((near, far), (far, near)))
        ]

    def send(self, at, to):
        dst = self.o_ref.at[at, span(self.me, self.width)]
        return self.copies.start("section", to, self.x_ref.at[at], dst)

    def start(self):
        self.first = [self.send(at, one) for at, one, _ in self.parts]
        self.rest = [self.send(at, two) for at, _, two in self.parts]
        self.o_ref[:, span(self.me, self.width)] = self.x_ref[...]

    def forward(self):
        for (at, one, two), copy in zip(self.parts, self.first):
            copy.wait_recv()
            place = self.o_ref.at[at, span(one, self.width)]
            self.rest.append(self.copies.start("section", two, place, place))

    def finish(self):
        for copy in self.first:
            copy.wait_send()
        wait(self.rest)


class SquareScatter:
    @staticmethod
    def count(rows):
        return 6 * pieces_of(rows)[0]

    @staticmethod
    def scratch(rows, width):
        return [pltpu.VMEM((2, rows, width), BF), pltpu.VMEM((rows, width), BF), pltpu.VMEM((rows, width), BF)]

    def __init__(self, copies, x_ref, got, turn, last):
        self.copies, self.x_ref, self.got, self.turn, self.last = copies, x_ref, got, turn, last
        self.width = turn.shape[1]
        self.me = copies.lines.place("section")
        near, far, self.across = square(copies.lines)
        pieces, step = pieces_of(x_ref.shape[0])
        half = x_ref.shape[0] // 2
        self.parts = [
            (pl.ds(h * half + j * step, step), one, two)
            for j in range(pieces)
            for h, (one, two) in enumerate(((near, far), (far, near)))
        ]

    def read(self, at, place):
        return self.x_ref[at, span(place, self.width)].astype(F32)

    def start(self):
        self.passed, self.kept = [], []
        for at, one, _ in self.parts:
            for place, k, out in ((self.across, 0, self.passed), (one, 1, self.kept)):
                src = self.x_ref.at[at, span(place, self.width)]
                out.append(self.copies.start("section", one, src, self.got.at[k, at]))

    def forward(self):
        self.second = []
        for (at, _, two), copy in zip(self.parts, self.passed):
            copy.wait_recv()
            self.turn[at] = (self.read(at, two) + self.got[0, at].astype(F32)).astype(BF)
            self.second.append(self.copies.start("section", two, self.turn.at[at], self.last.at[at]))

    def finish(self, o_ref):
        for i, (at, _, _) in enumerate(self.parts):
            self.kept[i].wait_recv()
            self.second[i].wait_recv()
            o_ref[at] = self.read(at, self.me) + self.got[1, at].astype(F32) + self.last[at].astype(F32)
        for copy in self.passed + self.kept + self.second:
            copy.wait_send()


def gather_columns(lines, ident, part, name):
    rows, width = part.shape

    def kernel(x_ref, o_ref, send, recv):
        copies = Copies(lines, send, recv)
        copies.greet(["section"])
        gather = SquareGather(copies, x_ref, o_ref)
        gather.start()
        gather.forward()
        gather.finish()

    shape = ((rows, lines.sizes["section"] * width), part.dtype)
    (out,) = communicate(kernel, ident, [part], [shape], semaphores(SquareGather.count(rows)), name)
    return out


def scalar_block(scalars):
    count = -(-scalars.shape[0] // 128)
    count += -count % 8
    return jnp.pad(scalars, (0, count * 128 - scalars.shape[0])).reshape(count, 128)


def sum_places(ref):
    total = ref[0].astype(F32)
    for i in range(1, ref.shape[0]):
        total = total + ref[i].astype(F32)
    return total


def scatter_columns(lines, ident, part, scalars, name):
    rows, full = part.shape
    sections = lines.sizes["section"]
    width = full // sections
    extra = scalars is not None
    arrays = [part]
    shapes = [((rows, width), F32)]
    scratch = semaphores(SquareScatter.count(rows) + sections - 1) + SquareScatter.scratch(rows, width)
    if extra:
        arrays.append(scalar_block(scalars))
        shapes.append((arrays[1].shape, F32))
        scratch.append(pltpu.VMEM((sections,) + arrays[1].shape, F32))

    def kernel(*refs):
        x_ref, refs = refs[0], refs[1:]
        if extra:
            e_ref, o_ref, eo_ref, send, recv, got, turn, last, e_got = refs
        else:
            o_ref, send, recv, got, turn, last = refs
        copies = Copies(lines, send, recv)
        copies.greet(["section"])
        scatter = SquareScatter(copies, x_ref, got, turn, last)
        scatter.start()
        if extra:
            others = copies.swap("section", lambda peer: e_ref, lambda place: e_got.at[place])
            e_got[lines.place("section")] = e_ref[...]
        scatter.forward()
        scatter.finish(o_ref)
        if extra:
            wait(others)
            eo_ref[...] = sum_places(e_got)

    got = communicate(kernel, ident, arrays, shapes, scratch, name)
    if not extra:
        return got[0]
    return got[0], got[1].reshape(-1)[:rows]


def gather_rows(lines, ident, parts, name):
    group, ring = lines.sizes["z"], lines.sizes["core"]
    dp = group * ring
    many = len(parts)

    def kernel(*refs):
        ins, outs, (send, recv) = refs[:many], refs[many : 2 * many], refs[2 * many :]
        copies = Copies(lines, send, recv)
        rank = lax.axis_index("dp")
        zplace, place = lines.place("z"), lines.place("core")
        copies.greet(["z", "core"])
        along, handed = [], []
        for x_ref, o_ref in zip(ins, outs):
            along.append(copies.swap("z", lambda peer: x_ref, lambda _: o_ref.at[rank]))
        for x_ref, o_ref in zip(ins, outs):
            handed += copies.swap("core", lambda peer: x_ref, lambda _: o_ref.at[rank])
            o_ref[rank] = x_ref[...]
        for step in range(group - 1, 0, -1):
            source = lax.rem(zplace + step, group) * ring + place
            for arrived, o_ref in zip(along, outs):
                arrived[group - 1 - step].wait_recv()
                handed += copies.swap("core", lambda peer: o_ref.at[source], lambda _: o_ref.at[source])
        for arrived in along:
            for copy in arrived:
                copy.wait_send()
        wait(handed)

    return communicate(
        kernel,
        ident,
        parts,
        [((dp,) + part.shape, part.dtype) for part in parts],
        semaphores(many * (group - 1 + group * (ring - 1))),
        name,
    )


def swap_blocks(lines, ident, kind, arrays, shapes, plan, name):
    size = lines.sizes[kind]

    def kernel(*refs):
        ins, outs = refs[: len(arrays)], refs[len(arrays) : len(arrays) + len(shapes)]
        copies = Copies(lines, *refs[len(arrays) + len(shapes) :])
        me = lines.place(kind)
        copies.greet([kind])
        pending = []
        for i, src, o, dst in plan:
            pending += copies.swap(
                kind, lambda peer: src(ins[i], peer), lambda place: dst(outs[o], place)
            )
        for i, src, o, dst in plan:
            view = dst(outs[o], me)
            view[...] = src(ins[i], me)[...]
        wait(pending)

    return communicate(kernel, ident, arrays, shapes, semaphores((size - 1) * len(plan)), name)


def slot(ref, place):
    return ref.at[place]


def columns(width):
    def view(ref, place):
        return ref.at[:, span(place, width)]

    return view


def dense_to_heads(lines, ident, pairs, queries, name):
    group, ring = lines.sizes["z"], lines.sizes["core"]
    lanes = 2 * HDIM

    def kernel(p_ref, q_ref, po_ref, qo_ref, send, recv):
        copies = Copies(lines, send, recv)
        zplace, place = lines.place("z"), lines.place("core")
        copies.greet(["z", "core"])
        along, pending = [], []
        for peer in lines.peers("z"):
            along.append(copies.start("z", peer, p_ref.at[:, span(peer, lanes)], po_ref.at[place, zplace]))
        for peer in lines.peers("z"):
            pending.append(copies.start("z", peer, q_ref.at[:, span(peer, lanes)], qo_ref.at[zplace]))
        own = p_ref.at[:, span(zplace, lanes)]
        pending += copies.swap("core", lambda peer: own, lambda _: po_ref.at[place, zplace])
        po_ref[place, zplace] = own[...]
        qo_ref[zplace] = q_ref[:, span(zplace, lanes)]
        for step in range(group - 1, 0, -1):
            along[group - 1 - step].wait_recv()
            block = po_ref.at[place, lax.rem(zplace + step, group)]
            pending += copies.swap("core", lambda peer: block, lambda _: block)
        for copy in along:
            copy.wait_send()
        wait(pending)

    return communicate(
        kernel,
        ident,
        [pairs, queries],
        [((ring, group, pairs.shape[0], lanes), BF), ((group, queries.shape[0], lanes), BF)],
        semaphores(2 * (group - 1) + group * (ring - 1)),
        name,
    )


def dense_from_heads(lines, ident, pairs, queries, shards, name):
    group, ring = lines.sizes["z"], lines.sizes["core"]
    _, _, rows, lanes = pairs.shape
    many = len(shards)

    def kernel(p_ref, q_ref, *refs):
        s_refs, refs = refs[:many], refs[many:]
        po_ref, qo_ref, refs = refs[0], refs[1], refs[2:]
        so_refs, (send, recv, got, turn) = refs[:many], refs[many:]
        copies = Copies(lines, send, recv)
        zplace, place = lines.place("z"), lines.place("core")
        copies.greet(["z", "core", "section"])
        order = lines.peers("z") + [zplace]
        around, pending = [], []
        for g in order:
            around.append(copies.swap("core", lambda peer: p_ref.at[peer, g], lambda me: got.at[me, g]))
        for g in order[:-1]:
            pending.append(copies.start("z", g, q_ref.at[g], qo_ref.at[:, span(zplace, lanes)]))
        gathers = [SquareGather(copies, x, o) for x, o in zip(s_refs, so_refs)]
        for gather in gathers:
            gather.start()
        qo_ref[:, span(zplace, lanes)] = q_ref[zplace]
        for i, (g, arrived) in enumerate(zip(order, around)):
            for copy in arrived:
                copy.wait_recv()
            total = p_ref[place, g].astype(F32)
            for peer in lines.peers("core"):
                total = total + got[peer, g].astype(F32)
            if i == len(order) - 1:
                po_ref[:, span(zplace, lanes)] = total.astype(BF)
            else:
                turn[g] = total.astype(BF)
                pending.append(copies.start("z", g, turn.at[g], po_ref.at[:, span(zplace, lanes)]))
        for gather in gathers:
            gather.forward()
        for arrived in around:
            for copy in arrived:
                copy.wait_send()
        wait(pending)
        for gather in gathers:
            gather.finish()

    sections = lines.sizes["section"]
    got = communicate(
        kernel,
        ident,
        [pairs, queries] + shards,
        [((rows, group * lanes), BF), ((queries.shape[1], group * lanes), BF)]
        + [((x.shape[0], sections * x.shape[1]), x.dtype) for x in shards],
        semaphores(
            2 * (group - 1) + group * (ring - 1) + sum(SquareGather.count(x.shape[0]) for x in shards)
        )
        + [pltpu.VMEM((ring, group, rows, lanes), BF), pltpu.VMEM((group, rows, lanes), BF)],
        name,
    )
    return got[0], got[1], got[2:]


def dense_finish(lines, ident, part, scalars, scaled, weight, shards, name):
    group, ring, sections = (lines.sizes[k] for k in ("z", "core", "section"))
    dp = group * ring
    rows, full = part.shape
    width = full // sections
    many = len(shards)
    local = weight.shape[0] // dp
    wide = weight.shape[1]
    block = scalar_block(scalars)
    weight = weight.reshape(dp, local, wide)

    def kernel(x_ref, e_ref, scaled_ref, w_ref, *refs):
        s_refs, refs = refs[:many], refs[many:]
        o_ref, eo_ref, v_ref, wo_ref, refs = refs[0], refs[1], refs[2], refs[3], refs[4:]
        so_refs, refs = refs[:many], refs[many:]
        send, recv, got, turn, last, e_got, w_got, w_turn, w_all, w_own, v_buf, v_z, v_core, v_all = refs
        copies = Copies(lines, send, recv)
        zplace, place, section = (lines.place(k) for k in ("z", "core", "section"))
        copies.greet(["z", "core", "section"])
        order = lines.peers("z") + [zplace]
        scatter = SquareScatter(copies, x_ref, got, turn, last)
        scatter.start()
        around = [
            copies.swap("core", lambda peer: w_ref.at[g * ring + peer], lambda me: w_got.at[me, g]) for g in order
        ]
        others = copies.swap("section", lambda peer: e_ref, lambda me: e_got.at[me])
        e_got[section] = e_ref[...]
        along = []
        for i, (g, arrived) in enumerate(zip(order, around)):
            for copy in arrived:
                copy.wait_recv()
            total = w_ref[g * ring + place].astype(F32)
            for peer in lines.peers("core"):
                total = total + w_got[peer, g].astype(F32)
            w_turn[g] = total.astype(BF)
            if i < len(order) - 1:
                along.append(copies.start("z", g, w_turn.at[g], w_all.at[zplace]))
        scatter.forward()
        gathers = [SquareGather(copies, x, o) for x, o in zip(s_refs, so_refs)]
        for gather in gathers:
            gather.start()
        scatter.finish(o_ref)
        wait(others)
        eo_ref[...] = sum_places(e_got)
        v_buf[...] = jnp.broadcast_to(jnp.sum(o_ref[...] * scaled_ref[...], axis=0, keepdims=True), v_buf.shape)
        pending = copies.swap("z", lambda peer: v_buf, lambda me: v_z.at[me])
        v_z[zplace] = v_buf[...]
        for gather in gathers:
            gather.forward()
        wait(along)
        w_all[zplace] = w_turn[zplace]
        w_own[...] = sum_places(w_all).astype(BF)
        last_gather = SquareGather(copies, w_own, wo_ref)
        last_gather.start()
        wait(pending)
        v_core[place] = sum_places(v_z)
        wait(copies.swap("core", lambda peer: v_core.at[place], lambda me: v_core.at[me]))
        v_all[section] = sum_places(v_core)
        pending = copies.swap("section", lambda peer: v_all.at[section], lambda me: v_all.at[me])
        last_gather.forward()
        wait(pending)
        for i in range(sections):
            v_ref[:, i * width : (i + 1) * width] = v_all[i]
        for arrived in around:
            for copy in arrived:
                copy.wait_send()
        for gather in gathers:
            gather.finish()
        last_gather.finish()

    z, c, s = group - 1, ring - 1, sections - 1
    vector = (8, width)
    result = communicate(
        kernel,
        ident,
        [part, block, scaled, weight] + shards,
        [((rows, width), F32), (block.shape, F32), ((8, full), F32), ((local, sections * wide), BF)]
        + [((x.shape[0], sections * x.shape[1]), x.dtype) for x in shards],
        semaphores(
            SquareScatter.count(rows)
            + group * c
            + s
            + z
            + sum(SquareGather.count(x.shape[0]) for x in shards)
            + SquareGather.count(local)
            + z
            + c
            + s
        )
        + SquareScatter.scratch(rows, width)
        + [
            pltpu.VMEM((sections,) + block.shape, F32),
            pltpu.VMEM((ring, group, local, wide), BF),
            pltpu.VMEM((group, local, wide), BF),
            pltpu.VMEM((group, local, wide), BF),
            pltpu.VMEM((local, wide), BF),
            pltpu.VMEM(vector, F32),
            pltpu.VMEM((group,) + vector, F32),
            pltpu.VMEM((ring,) + vector, F32),
            pltpu.VMEM((sections,) + vector, F32),
        ],
        name,
        limit=32 * 2**20,
    )
    summed, scalar, vector, gathered = result[0], result[1].reshape(-1)[:rows], result[2][0], result[3]
    return summed, scalar, vector, gathered, result[4:]


def assemble(pieces, share, name):
    arrays = []
    for _, array, _, _ in pieces:
        if not any(array is other for other in arrays):
            arrays.append(array)
    where = [next(i for i, other in enumerate(arrays) if other is array) for _, array, _, _ in pieces]
    local = arrays[0].shape[0]
    steps = local // 32 if local % 32 == 0 else 1
    rows = local // steps
    sections = lax.axis_size("section")
    shapes, specs = [], []
    for kind, _, _, width in pieces:
        many = 2 if kind == "pair" else 1
        for _ in range(many):
            if kind == "stack":
                shapes.append(jax.ShapeDtypeStruct((sections, local, width), F32))
                specs.append(pl.BlockSpec((sections, rows, width), lambda i: (0, i, 0)))
            else:
                total = width if kind == "sum" else sections * width // many
                shapes.append(jax.ShapeDtypeStruct((local, total), F32))
                specs.append(pl.BlockSpec((rows, total), lambda i: (i, 0)))

    def kernel(*refs):
        ins, outs = refs[: len(arrays)], list(refs[len(arrays) :])
        for (kind, array, first, width), i in zip(pieces, where):
            wide = array.shape[1] // sections
            blocks = [ins[i][:, s * wide + first : s * wide + first + width].astype(F32) for s in range(sections)]
            out = outs.pop(0)
            if kind == "columns":
                for s, item in enumerate(blocks):
                    out[:, s * width : (s + 1) * width] = item
            elif kind == "stack":
                for s, item in enumerate(blocks):
                    out[s] = item
            elif kind == "sum":
                total = blocks[0]
                for item in blocks[1:]:
                    total = total + item
                out[...] = total
            elif kind == "hidden":
                for d in range(width // share):
                    out[:, d * share * sections : (d + 1) * share * sections] = jnp.concatenate(
                        [item[:, d * share : (d + 1) * share] for item in blocks], axis=1
                    )
            else:
                other = outs.pop(0)
                half = width // 2
                for s, item in enumerate(blocks):
                    for side, dst in ((0, out), (1, other)):
                        heads = [
                            item[:, (2 * g + side) * HDIM : (2 * g + side + 1) * HDIM]
                            for g in range(width // (2 * HDIM))
                        ]
                        dst[:, s * half : (s + 1) * half] = jnp.concatenate(heads, axis=1)

    return pl.pallas_call(
        kernel,
        grid=(steps,),
        in_specs=[pl.BlockSpec((rows, a.shape[1]), lambda i: (i, 0)) for a in arrays],
        out_specs=specs,
        out_shape=shapes,
        compiler_params=pltpu.CompilerParams(vmem_limit_bytes=24 * 2**20),
        name=name,
    )(*arrays)


def unpack_low(packed):
    lane = lax.broadcasted_iota(jnp.int32, packed.shape, 1)
    zero = jnp.zeros_like(packed)
    low = jnp.where(lane < HDIM, packed, zero)
    turned = jnp.concatenate([packed[:, HDIM:], packed[:, :HDIM]], axis=1)
    high = jnp.where(lane < HDIM, turned, zero)
    return jnp.concatenate([low, high], axis=0)


def unpack_high(packed):
    lane = lax.broadcasted_iota(jnp.int32, packed.shape, 1)
    zero = jnp.zeros_like(packed)
    turned = jnp.concatenate([packed[:, HDIM:], packed[:, :HDIM]], axis=1)
    low = jnp.where(lane >= HDIM, turned, zero)
    high = jnp.where(lane >= HDIM, packed, zero)
    return jnp.concatenate([low, high], axis=0)


def pack_turned(turned):
    half = turned.shape[1] // 2
    return jnp.concatenate([turned[:, :half], turned[:, half:]], axis=0).T


def forward_block(query, pieces, qpos, start, causal):
    scores = []
    peak = None
    for index, (pair, _, first) in enumerate(pieces):
        item = contract(pair, query, 1, 1)
        kpos = first + lax.broadcasted_iota(jnp.int32, item.shape, 0)
        allowed = kpos >= start
        if causal[index]:
            allowed = allowed & (kpos <= qpos)
        item = jnp.where(allowed, item, NEG)
        top = jnp.max(item, axis=0, keepdims=True)
        peak = top if peak is None else jnp.maximum(peak, top)
        scores.append(item)
    total = jnp.zeros_like(peak)
    mixed = None
    for item, (_, turned, _) in zip(scores, pieces):
        weight = jnp.exp(item - peak)
        total = total + jnp.sum(weight, axis=0, keepdims=True)
        part = matmul(turned[HDIM:], weight.astype(BF))
        mixed = part if mixed is None else mixed + part
    return mixed / total, peak + jnp.log(total)


def backward_block(query, grad, grad_turned, mixed_turned, lse, pieces, qpos, start, causal):
    row_sum = jnp.sum(grad_turned.astype(F32) * mixed_turned.astype(F32), axis=0, keepdims=True)
    grad_query = None
    grads = []
    for index, (pair, turned, first) in enumerate(pieces):
        scores = contract(pair, query, 1, 1)
        kpos = first + lax.broadcasted_iota(jnp.int32, scores.shape, 0)
        allowed = kpos >= start
        if causal[index]:
            allowed = allowed & (kpos <= qpos)
        probs = jnp.where(allowed, jnp.exp(scores - lse), 0.0)
        grad_probs = contract(pair, grad, 1, 1)
        grad_scores = (probs * (grad_probs - row_sum)).astype(BF)
        grads.append(matmul(grad_scores, query) + matmul(probs.astype(BF), grad))
        part = matmul(turned[:HDIM], grad_scores)
        grad_query = part if grad_query is None else grad_query + part
    return grad_query * SCALE, grads


def dense_forward_kernel(place_ref, q_ref, kv_ref, start_ref, out_ref, turned_ref, lse_ref):
    group, _, half, _ = q_ref.shape
    ring, _, _, block, _ = kv_ref.shape
    place = place_ref[0]
    span = ring * block
    pieces = []
    for g in range(group):
        pair = kv_ref[:, g, 0].reshape(span, 2 * HDIM)
        pieces.append((pair, pair.T, g * span))
    for g in range(group):
        query = unpack_low(q_ref[g, 0]) * jnp.asarray(SCALE, BF)
        qpos = g * span + place * block + lax.broadcasted_iota(jnp.int32, (1, block), 1)
        mixed, lse = forward_block(
            query, pieces[: g + 1], qpos, start_ref[0, g], [i == g for i in range(g + 1)]
        )
        turned_ref[0, g] = mixed.astype(BF)
        lse_ref[0, g] = lse
        out_ref[g, 0] = pack_turned(mixed).astype(BF)


def dense_forward(place, q, kv, start):
    group, seqs, half, lanes = q.shape
    ring, _, _, block, _ = kv.shape
    grid = pltpu.PrefetchScalarGridSpec(
        num_scalar_prefetch=1,
        grid=(seqs,),
        in_specs=[
            pl.BlockSpec((group, 1, half, lanes), lambda s, _: (0, s, 0, 0)),
            pl.BlockSpec((ring, group, 1, block, lanes), lambda s, _: (0, 0, s, 0, 0)),
            pl.BlockSpec((1, group, 1, block), lambda s, _: (s, 0, 0, 0)),
        ],
        out_specs=[
            pl.BlockSpec((group, 1, half, lanes), lambda s, _: (0, s, 0, 0)),
            pl.BlockSpec((1, group, HDIM, block), lambda s, _: (s, 0, 0, 0)),
            pl.BlockSpec((1, group, 1, block), lambda s, _: (s, 0, 0, 0)),
        ],
    )
    return pl.pallas_call(
        dense_forward_kernel,
        grid_spec=grid,
        out_shape=[
            jax.ShapeDtypeStruct(q.shape, BF),
            jax.ShapeDtypeStruct((seqs, group, HDIM, block), BF),
            jax.ShapeDtypeStruct((seqs, group, 1, block), F32),
        ],
        compiler_params=pltpu.CompilerParams(vmem_limit_bytes=VMEM),
        name="dense_attention",
    )(place, q, kv, start)


def dense_backward_kernel(
    place_ref, q_ref, g_ref, kv_ref, start_ref, turned_ref, lse_ref, dq_ref, dkv_ref, acc_ref
):
    group, _, half, _ = q_ref.shape
    ring, _, _, block, _ = kv_ref.shape
    place = place_ref[0]
    span = ring * block
    pieces = []
    for g in range(group):
        pair = kv_ref[:, g, 0].reshape(span, 2 * HDIM)
        pieces.append((pair, pair.T, g * span))
    for g in reversed(range(group)):
        query = unpack_low(q_ref[g, 0]) * jnp.asarray(SCALE, BF)
        packed = g_ref[g, 0]
        grad = unpack_high(packed)
        flat = packed.T
        grad_turned = jnp.concatenate([flat[:HDIM], flat[HDIM:]], axis=1)
        qpos = g * span + place * block + lax.broadcasted_iota(jnp.int32, (1, block), 1)
        grad_query, grads = backward_block(
            query,
            grad,
            grad_turned,
            turned_ref[0, g],
            lse_ref[0, g],
            pieces[: g + 1],
            qpos,
            start_ref[0, g],
            [i == g for i in range(g + 1)],
        )
        dq_ref[g, 0] = pack_turned(grad_query).astype(BF)
        for i, item in enumerate(grads):
            if g == group - 1:
                acc_ref[i] = item
            else:
                acc_ref[i] += item
    for g in range(group):
        dkv_ref[:, g, 0] = acc_ref[g].reshape(ring, block, 2 * HDIM).astype(BF)


def dense_backward(place, q, grad, kv, start, turned, lse):
    group, seqs, half, lanes = q.shape
    ring, _, _, block, _ = kv.shape
    grid = pltpu.PrefetchScalarGridSpec(
        num_scalar_prefetch=1,
        grid=(seqs,),
        in_specs=[
            pl.BlockSpec((group, 1, half, lanes), lambda s, _: (0, s, 0, 0)),
            pl.BlockSpec((group, 1, half, lanes), lambda s, _: (0, s, 0, 0)),
            pl.BlockSpec((ring, group, 1, block, lanes), lambda s, _: (0, 0, s, 0, 0)),
            pl.BlockSpec((1, group, 1, block), lambda s, _: (s, 0, 0, 0)),
            pl.BlockSpec((1, group, HDIM, block), lambda s, _: (s, 0, 0, 0)),
            pl.BlockSpec((1, group, 1, block), lambda s, _: (s, 0, 0, 0)),
        ],
        out_specs=[
            pl.BlockSpec((group, 1, half, lanes), lambda s, _: (0, s, 0, 0)),
            pl.BlockSpec((ring, group, 1, block, lanes), lambda s, _: (0, 0, s, 0, 0)),
        ],
        scratch_shapes=[pltpu.VMEM((group, ring * block, lanes), F32)],
    )
    return pl.pallas_call(
        dense_backward_kernel,
        grid_spec=grid,
        out_shape=[
            jax.ShapeDtypeStruct(q.shape, BF),
            jax.ShapeDtypeStruct(kv.shape, BF),
        ],
        compiler_params=pltpu.CompilerParams(vmem_limit_bytes=VMEM),
        name="dense_attention_grad",
    )(place, q, grad, kv, start, turned, lse)


def inverse_rms(value):
    return lax.rsqrt(jnp.mean(value * value, axis=-1, keepdims=True) + EPS)


def gelu_terms(value):
    scale = 0.7978845608028654
    square = value * value
    bend = jnp.tanh(scale * (value + 0.044715 * square * value))
    half = 0.5 * (1.0 + bend)
    slope = half + 0.5 * value * (1.0 - bend * bend) * scale * (1.0 + 0.134145 * square)
    return value * half, slope


def side_by_side(blocks):
    return jnp.concatenate(blocks, axis=1)


def all_columns(copies, value, dst):
    section = copies.lines.place("section")
    dst[section] = value
    wait(copies.swap("section", lambda peer: dst.at[section], lambda me: dst.at[me]))
    return side_by_side([dst[i] for i in range(dst.shape[0])])


class ColumnSum:
    @staticmethod
    def count(sections, scalars):
        return (sections - 1) * (2 if scalars else 1)

    @staticmethod
    def scratch(sections, rows, width, scalars):
        buffers = [pltpu.VMEM((rows, sections * width), BF), pltpu.VMEM((sections, rows, width), BF)]
        if scalars:
            buffers += [pltpu.VMEM((rows, 128), F32), pltpu.VMEM((sections, rows, 128), F32)]
        return buffers

    def __init__(self, copies, buffers):
        self.copies, self.buffers = copies, buffers

    def start(self, value, scalars=None):
        buf, got = self.buffers[:2]
        width = got.shape[2]
        section = self.copies.lines.place("section")
        buf[...] = value.astype(BF)
        self.pending = self.copies.swap(
            "section", lambda peer: buf.at[:, span(peer, width)], lambda me: got.at[me]
        )
        got[section] = buf[:, span(section, width)]
        if scalars is not None:
            sbuf, sgot = self.buffers[2:]
            sbuf[...] = jnp.broadcast_to(scalars, sbuf.shape)
            self.pending += self.copies.swap("section", lambda peer: sbuf, lambda me: sgot.at[me])
            sgot[section] = sbuf[...]

    def finish(self):
        wait(self.pending)
        total = sum_places(self.buffers[1])
        if len(self.buffers) == 2:
            return total
        return total, sum_places(self.buffers[3])[:, :1]


def routed_slots(lines, sel):
    group, ring = lines.sizes["z"], lines.sizes["core"]
    index = lax.broadcasted_iota(jnp.int32, (1, group * sel), 1)
    return (index // sel) * (ring * sel) + lines.place("core") * sel + lax.rem(index, sel)


def routed_sequence(lines, heads_ref, pairs_ref, q, sel):
    group, ring = lines.sizes["z"], lines.sizes["core"]
    lanes = 2 * HDIM
    at = slice(q * sel, (q + 1) * sel)
    query = jnp.concatenate([heads_ref[g, at, :lanes] for g in range(group)], axis=0)
    pair = jnp.concatenate([pairs_ref[r, g, at] for g in range(group) for r in range(ring)], axis=0)
    return query * jnp.asarray(SCALE, BF), pair


def routed_enter(lines, ident, source, chosen, start, gain, qkv_w, sel):
    seqs, rows, wide = source.shape
    sections, group, ring = (lines.sizes[k] for k in ("section", "z", "core"))
    dp = group * ring
    part = wide // 2
    width = sections * part
    slots = seqs * sel
    lanes = 2 * HDIM

    def kernel(
        source_ref,
        column_ref,
        start_ref,
        gain_ref,
        qkv_ref,
        value_ref,
        grad_ref,
        normed_ref,
        heads_got,
        pairs_all,
        turned_ref,
        lse_ref,
        mixed_ref,
        send,
        recv,
        picked_buf,
        picked_got,
        slots_buf,
        slots_got,
        rows_got,
        heads_buf,
        out_buf,
        out_got,
        mixed_all,
    ):
        copies = Copies(lines, send, recv)
        section, zplace, place = (lines.place(k) for k in ("section", "z", "core"))
        rank = lax.axis_index("dp")
        copies.greet(["section", "z", "core"])
        position = rank * rows + lax.broadcasted_iota(jnp.int32, (1, rows), 1)
        for q in range(seqs):
            table = (column_ref[q] == position).astype(F32).astype(BF)
            found = matmul(table, source_ref[q]).astype(BF)
            for d in range(dp):
                picked_buf[d % ring, d // ring, q * sel : (q + 1) * sel] = found[d * sel : (d + 1) * sel]
        wait(copies.swap("core", lambda peer: picked_buf.at[peer], lambda me: picked_got.at[me]))
        total = picked_buf[place].astype(F32)
        for peer in lines.peers("core"):
            total = total + picked_got[peer].astype(F32)
        slots_buf[...] = total.astype(BF)
        pending = copies.swap("z", lambda peer: slots_buf.at[peer], lambda me: slots_got.at[me])
        slots_got[zplace] = slots_buf[zplace]
        wait(pending)
        rows_got[section] = sum_places(slots_got).astype(BF)
        wait(copies.swap("section", lambda peer: rows_got.at[section], lambda me: rows_got.at[me]))
        low = side_by_side([rows_got[i, :, :part] for i in range(sections)])
        value_ref[...] = low
        grad_ref[...] = side_by_side([rows_got[i, :, part:] for i in range(sections)])
        picked = low.astype(F32)

        normed = (picked * inverse_rms(picked) * gain_ref[...]).astype(BF)
        normed_ref[...] = normed
        qkv = matmul(normed, qkv_ref[...]).astype(BF)
        blank = jnp.zeros((slots, HDIM), BF)
        for g in range(group):
            query = qkv[:, 2 * part + g * HDIM : 2 * part + (g + 1) * HDIM]
            heads_buf[g, :, :lanes] = side_by_side([query, blank])
            heads_buf[g, :, lanes:] = qkv[:, g * lanes : (g + 1) * lanes]
        pending = copies.swap("z", lambda peer: heads_buf.at[peer], lambda me: heads_got.at[me])
        heads_got[zplace] = heads_buf[zplace]
        wait(pending)
        pairs_all[place] = heads_got[:, :, lanes:]
        wait(copies.swap("core", lambda peer: pairs_all.at[place], lambda me: pairs_all.at[me]))
        for q in range(seqs):
            query, pair = routed_sequence(lines, heads_got, pairs_all, q, sel)
            turned, lse = forward_block(
                query, [(pair, pair.T, 0)], routed_slots(lines, sel), start_ref[q], [True]
            )
            turned_ref[q] = turned.astype(BF)
            lse_ref[q] = lse
            upright = jnp.concatenate([turned, jnp.zeros_like(turned)], axis=0).T.astype(BF)
            for g in range(group):
                out_buf[g, q * sel : (q + 1) * sel] = upright[g * sel : (g + 1) * sel]
        pending = copies.swap("z", lambda peer: out_buf.at[peer], lambda me: out_got.at[me])
        out_got[zplace] = out_buf[zplace]
        wait(pending)
        own = side_by_side([out_got[g, :, :HDIM] for g in range(group)])
        mixed_ref[...] = all_columns(copies, own, mixed_all)

    vmem = pltpu.VMEM
    queries = group * sel
    return communicate(
        kernel,
        ident,
        [source, chosen[:, :, None], start, gain, qkv_w],
        [
            ((slots, width), BF),
            ((slots, width), BF),
            ((slots, width), BF),
            ((group, slots, 2 * lanes), BF),
            ((ring, group, slots, lanes), BF),
            ((seqs, HDIM, queries), BF),
            ((seqs, 1, queries), F32),
            ((slots, width), BF),
        ],
        semaphores(2 * (ring - 1) + 3 * (group - 1) + 2 * (sections - 1))
        + [
            vmem((ring, group, slots, wide), BF),
            vmem((ring, group, slots, wide), BF),
            vmem((group, slots, wide), BF),
            vmem((group, slots, wide), BF),
            vmem((sections, slots, wide), BF),
            vmem((group, slots, 2 * lanes), BF),
            vmem((group, slots, lanes), BF),
            vmem((group, slots, lanes), BF),
            vmem((sections, slots, part), BF),
        ],
        "routed_enter",
    )


def routed_feed(lines, ident, picked, grad_sent, mixed, gains, weights, part):
    sections = lines.sizes["section"]
    slots, width = picked.shape
    hidden_size = weights.shape[1] - part - width

    def kernel(
        value_ref,
        grad_ref,
        mixed_ref,
        gains_ref,
        weights_ref,
        normed_ref,
        dpre_ref,
        hidden_ref,
        fed_ref,
        middle_ref,
        attended_ref,
        sent_ref,
        logit_ref,
        vectors_ref,
        send,
        recv,
        keep_ref,
        attended_all,
        *buffers,
    ):
        copies = Copies(lines, send, recv)
        copies.greet(["section"])
        own = span(lines.place("section"), part)
        out_w = weights_ref.at[:, :part]
        expand_w = weights_ref.at[:, part : part + hidden_size]
        shrink_w = weights_ref.at[:, part + hidden_size :]
        gain, router = gains_ref[0:1, :], gains_ref[1:2, :]
        attended_own = matmul(mixed_ref[...], out_w[...]).astype(BF)
        attended = all_columns(copies, attended_own, attended_all).astype(F32)
        picked = value_ref[...].astype(F32)
        grad_sent = grad_ref[...].astype(F32)
        middle = picked + attended
        inv = inverse_rms(middle)
        normed = (middle * inv * gain).astype(BF)
        normed_ref[...] = normed
        hidden, slope = gelu_terms(matmul(normed, expand_w[...]))
        hidden = hidden.astype(BF)
        hidden_ref[...] = hidden
        gate = jax.nn.sigmoid(jnp.sum(picked * router, axis=1, keepdims=True))
        grad_delta = gate * grad_sent
        fed_low = grad_delta.astype(BF)
        fed_ref[...] = fed_low
        grad_pre = (contract(fed_low, shrink_w[...], 1, 1) * slope).astype(BF)
        dpre_ref[...] = grad_pre
        grad_normed = contract(grad_pre, expand_w[...], 1, 1)
        scalar = jnp.sum(grad_normed * middle * gain, axis=1, keepdims=True)
        back = ColumnSum(copies, buffers[:4])
        back.start(grad_normed, scalar)
        fed_part = matmul(hidden, shrink_w[...])
        keep_ref[0] = middle
        keep_ref[1] = grad_delta
        keep_ref[2] = grad_sent
        own_attended = attended_own.astype(F32)
        gate_part = jnp.sum(grad_sent * fed_part, axis=1, keepdims=True) + jnp.sum(
            keep_ref[2, :, own] * own_attended, axis=1, keepdims=True
        )
        forth = ColumnSum(copies, buffers[4:])
        forth.start(fed_part, gate_part)
        middle_own, picked_own = keep_ref[0, :, own], value_ref[:, own].astype(F32)
        grad_normed, scalar = back.finish()
        vectors_ref[...] = jnp.zeros_like(vectors_ref)
        vectors_ref[0:1, :] = jnp.sum(grad_normed * middle_own * inv, axis=0, keepdims=True)
        grad_middle = inv * (grad_normed * gains_ref[0:1, own]) - middle_own * (inv * inv * inv) * (
            scalar * (1.0 / width)
        )
        middle_ref[...] = grad_middle
        attended_ref[...] = (grad_middle + keep_ref[1, :, own]).astype(BF)
        fed, grad_gate = forth.finish()
        sent_ref[...] = (gate * (own_attended + fed)).astype(BF)
        grad_logit = grad_gate * gate * (1.0 - gate)
        logit_ref[...] = jnp.broadcast_to(grad_logit, logit_ref.shape)
        vectors_ref[1:2, :] = jnp.sum(grad_logit * picked_own, axis=0, keepdims=True)

    return communicate(
        kernel,
        ident,
        [picked, grad_sent, mixed, gains, weights],
        [
            ((slots, width), BF),
            ((slots, hidden_size), BF),
            ((slots, hidden_size), BF),
            ((slots, width), BF),
            ((slots, part), F32),
            ((slots, part), BF),
            ((slots, part), BF),
            ((slots, 128), F32),
            ((8, part), F32),
        ],
        semaphores(sections - 1 + 2 * ColumnSum.count(sections, True))
        + [pltpu.VMEM((3, slots, width), F32), pltpu.VMEM((sections, slots, part), BF)]
        + 2 * ColumnSum.scratch(sections, slots, part, True),
        "routed_feed",
    )


def routed_leave(lines, ident, grad_attended, out_w, qkv_w, kept, start, picked, partial, gains, chosen, sel, rows):
    heads, pairs, turned, lse = kept
    grad_middle, grad_logit, sent = partial
    sections, group, ring = (lines.sizes[k] for k in ("section", "z", "core"))
    slots, width = picked.shape
    part = width // sections
    seqs = chosen.shape[0]
    lanes = 2 * HDIM

    def kernel(
        attended_ref,
        out_ref,
        qkv_ref,
        heads_ref,
        pairs_ref,
        turned_ref,
        lse_ref,
        start_ref,
        value_ref,
        middle_ref,
        logit_ref,
        sent_ref,
        gains_ref,
        row_ref,
        returned_ref,
        added_ref,
        dqkv_ref,
        vectors_ref,
        send,
        recv,
        grad_buf,
        grad_got,
        turn_buf,
        turn_got,
        back_buf,
        back_got,
        final_buf,
        final_got,
        final_all,
        *buffers,
    ):
        copies = Copies(lines, send, recv)
        section, zplace, place = (lines.place(k) for k in ("section", "z", "core"))
        rank = lax.axis_index("dp")
        copies.greet(["section", "z", "core"])
        own = span(section, part)
        outer = ColumnSum(copies, buffers[:2])
        outer.start(contract(attended_ref[...], out_ref[...], 1, 1))
        grad_mixed = outer.finish().astype(BF)
        blank = jnp.zeros((slots, HDIM), BF)
        for g in range(group):
            grad_buf[g] = side_by_side([blank, grad_mixed[:, g * HDIM : (g + 1) * HDIM]])
        pending = copies.swap("z", lambda peer: grad_buf.at[peer], lambda me: grad_got.at[me])
        grad_got[zplace] = grad_buf[zplace]
        wait(pending)
        for q in range(seqs):
            at = slice(q * sel, (q + 1) * sel)
            query, pair = routed_sequence(lines, heads_ref, pairs_ref, q, sel)
            grad = jnp.concatenate([grad_got[g, at] for g in range(group)], axis=0)
            grad_query, grad_pairs = backward_block(
                query,
                grad,
                grad.T[HDIM:],
                turned_ref[q],
                lse_ref[q],
                [(pair, pair.T, 0)],
                routed_slots(lines, sel),
                start_ref[q],
                [True],
            )
            upright = jnp.concatenate([grad_query, jnp.zeros_like(grad_query)], axis=0).T.astype(BF)
            low = grad_pairs[0].astype(BF)
            for g in range(group):
                back_buf[g, at, :lanes] = upright[g * sel : (g + 1) * sel]
                for r in range(ring):
                    first = (g * ring + r) * sel
                    turn_buf[r, g, at] = low[first : first + sel]
        wait(copies.swap("core", lambda peer: turn_buf.at[peer], lambda me: turn_got.at[me]))
        total = turn_buf[place].astype(F32)
        for peer in lines.peers("core"):
            total = total + turn_got[peer].astype(F32)
        back_buf[:, :, lanes:] = total.astype(BF)
        pending = copies.swap("z", lambda peer: back_buf.at[peer], lambda me: back_got.at[me])
        back_got[zplace] = back_buf[zplace]
        wait(pending)
        grad_qkv = side_by_side(
            [back_got[g, :, lanes:] for g in range(group)] + [back_got[g, :, :HDIM] for g in range(group)]
        )
        dqkv_ref[...] = grad_qkv
        grad_normed = contract(grad_qkv, qkv_ref[...], 1, 1)
        picked = value_ref[...].astype(F32)
        inv = inverse_rms(picked)
        inner = ColumnSum(copies, buffers[2:])
        inner.start(grad_normed, jnp.sum(grad_normed * picked * gains_ref[0:1, :], axis=1, keepdims=True))
        picked_own = value_ref[:, own].astype(F32)
        grad_normed, scalar = inner.finish()
        vectors_ref[...] = jnp.zeros_like(vectors_ref)
        vectors_ref[0:1, :] = jnp.sum(grad_normed * picked_own * inv, axis=0, keepdims=True)
        grad_in = inv * (grad_normed * gains_ref[0:1, own]) - picked_own * (inv * inv * inv) * (scalar * (1.0 / width))
        grad_in = middle_ref[...] + grad_in + logit_ref[:, :1] * gains_ref[1:2, own]

        final_buf[:, :part] = grad_in.astype(BF)
        final_buf[:, part:] = sent_ref[...]
        along = copies.swap("z", lambda peer: final_buf, lambda me: final_got.at[me])
        final_got[zplace] = final_buf[...]

        def hand_on(i):
            view = final_got.at[i, :, pl.ds(0, part)]
            dst = final_all.at[place, i, :, own]
            dst[...] = view[...]
            final_all[place, i, :, width:] = final_got[i, :, part:]
            return copies.swap("section", lambda peer: view, lambda me: dst)

        spread = hand_on(zplace)
        for step in range(group - 1, 0, -1):
            along[group - 1 - step].wait_recv()
            spread += hand_on(lax.rem(zplace + step, group))
        for copy in along:
            copy.wait_send()
        wait(spread)
        wait(copies.swap("core", lambda peer: final_all.at[place], lambda me: final_all.at[me]))
        slot_of = rank * rows + lax.broadcasted_iota(jnp.int32, (rows, 1), 0)
        for q in range(seqs):
            at = slice(q * sel, (q + 1) * sel)
            table = (row_ref[q] == slot_of).astype(F32).astype(BF)
            found = jnp.concatenate([final_all[r, g, at] for g in range(group) for r in range(ring)], axis=0)
            placed = matmul(table, found).astype(BF)
            returned_ref[q] = placed[:, :width]
            added_ref[q] = placed[:, width:]

    vmem = pltpu.VMEM
    return communicate(
        kernel,
        ident,
        [
            grad_attended,
            out_w,
            qkv_w,
            heads,
            pairs,
            turned,
            lse,
            start,
            picked,
            grad_middle,
            grad_logit,
            sent,
            gains,
            chosen[:, None, :],
        ],
        [
            ((seqs, rows, width), BF),
            ((seqs, rows, part), BF),
            ((slots, 3 * part), BF),
            ((8, part), F32),
        ],
        semaphores(
            2 * (ring - 1)
            + 3 * (group - 1)
            + ColumnSum.count(sections, False)
            + ColumnSum.count(sections, True)
            + group * (sections - 1)
        )
        + [
            vmem((group, slots, lanes), BF),
            vmem((group, slots, lanes), BF),
            vmem((ring, group, slots, lanes), BF),
            vmem((ring, group, slots, lanes), BF),
            vmem((group, slots, 2 * lanes), BF),
            vmem((group, slots, 2 * lanes), BF),
            vmem((slots, 2 * part), BF),
            vmem((group, slots, 2 * part), BF),
            vmem((ring, group, slots, width + part), BF),
        ]
        + ColumnSum.scratch(sections, slots, part, False)
        + ColumnSum.scratch(sections, slots, part, True),
        "routed_leave",
    )


def on_device(
    stream_in,
    segment_ids,
    chosen_rows,
    cotangent,
    dense_prenorm,
    dense_query,
    dense_keys,
    dense_values,
    dense_output,
    dense_midnorm,
    dense_expand,
    dense_shrink,
    routed_prenorm,
    routed_query,
    routed_keys,
    routed_values,
    routed_output,
    routed_midnorm,
    routed_expand,
    routed_shrink,
    router_weight,
):
    sections, dp = lax.axis_size("section"), lax.axis_size("dp")
    section, rank = lax.axis_index("section"), lax.axis_index("dp")
    seqs, rows, width = stream_in.shape
    tokens = seqs * rows
    part = width // sections
    group = HEADS // sections
    ring = dp // group
    total_sel = chosen_rows.shape[1]
    sel = total_sel // dp
    place = lax.rem(rank, ring).astype(jnp.int32).reshape(1)
    lines = Lines(sections, dp, group)
    lanes = 2 * HDIM

    def own_columns(value):
        return lax.dynamic_slice_in_dim(value, section * part, part, value.ndim - 1)

    def own_hidden(expand, shrink):
        inner = expand.shape[1] // dp
        share = inner // sections
        cut = expand.reshape(expand.shape[0], dp, sections, share)
        cut = lax.dynamic_index_in_dim(cut, section, 2, keepdims=False).reshape(expand.shape[0], dp * share)
        return cut, lax.dynamic_slice_in_dim(shrink, section * share, share, 0)

    def own_attention(query, keys, values):
        local = query.shape[0]
        pair = jnp.stack(
            [own_columns(keys).reshape(local, group, HDIM), own_columns(values).reshape(local, group, HDIM)],
            axis=2,
        ).reshape(local, 2 * part)
        return jnp.concatenate([pair, own_columns(query)], axis=1)

    gains = jnp.stack([dense_prenorm, dense_midnorm, routed_prenorm, routed_midnorm, router_weight])
    gains = jnp.pad(gains, ((0, 16 - gains.shape[0]), (0, 0)))
    first = own_attention(dense_query, dense_keys, dense_values)
    dense_qkv, gains = gather_rows(lines, 1, [first, gains], "first_weights")
    dense_qkv = dense_qkv.reshape(width, 3 * part)
    gains = jnp.transpose(gains, (1, 0, 2)).reshape(16, width).astype(F32)
    gain_pre, gain_mid = gains[0], gains[1]

    def gather(value):
        return lax.all_gather(value, "dp", axis=0, tiled=True)

    def after(value, other):
        return lax.optimization_barrier((value, other))[0]

    expand_cut, shrink_cut = own_hidden(dense_expand, dense_shrink)
    hidden_size = expand_cut.shape[1]
    rest = gather(jnp.concatenate([own_columns(dense_output), expand_cut, shrink_cut], axis=1))
    dense_out, dense_exp, dense_shr = (
        rest[:, :part],
        rest[:, part : part + hidden_size],
        rest[:, part + hidden_size :],
    )
    routed_qkv = gather(after(own_attention(routed_query, routed_keys, routed_values), dense_qkv))
    expand_cut, shrink_cut = own_hidden(routed_expand, routed_shrink)
    routed_rest = jnp.concatenate([own_columns(routed_output), expand_cut, shrink_cut], axis=1)

    first_of = jnp.sum(
        (segment_ids[:, None, :] < jnp.arange(DOCS, dtype=jnp.int32)[None, :, None]).astype(jnp.int32), axis=2
    )

    def document(positions):
        shape = (seqs,) + (1,) * (positions.ndim - 1)
        found = jnp.zeros(positions.shape, jnp.int32)
        for c in range(1, DOCS):
            found = found + (positions >= first_of[:, c].reshape(shape)).astype(jnp.int32)
        return found

    def pick(table, index):
        shape = (seqs,) + (1,) * (index.ndim - 1)
        out = jnp.zeros(index.shape, jnp.int32)
        for c in range(DOCS):
            out = jnp.where(index == c, table[:, c].reshape(shape), out)
        return out

    blocks = jnp.arange(group, dtype=jnp.int32) * ring + place[0]
    attended_pos = blocks[:, None] * rows + jnp.arange(rows, dtype=jnp.int32)[None, :]
    attended_pos = jnp.broadcast_to(attended_pos[None], (seqs, group, rows))
    start = pick(first_of, document(attended_pos))[:, :, None, :]
    chosen_doc = document(chosen_rows)
    first_slot = jnp.sum(
        (chosen_doc[:, None, :] < jnp.arange(DOCS, dtype=jnp.int32)[None, :, None]).astype(jnp.int32), axis=2
    )
    chosen_start = pick(first_slot, chosen_doc).reshape(seqs, group, ring, sel)
    routed_start = lax.dynamic_index_in_dim(chosen_start, place[0], 2, keepdims=False)
    routed_start = routed_start.reshape(seqs, 1, group * sel)

    def pack(value):
        value = value.reshape(seqs, 2, rows // 2, group, HDIM)
        return jnp.transpose(value, (0, 2, 3, 1, 4)).reshape(tokens // 2, 2 * part)

    def unpack(value):
        value = value.reshape(seqs, rows // 2, group, 2, HDIM)
        return jnp.transpose(value, (0, 3, 1, 2, 4)).reshape(tokens, part)

    value = stream_in.reshape(tokens, width).astype(F32)
    grad_top = cotangent.reshape(tokens, width)
    inv_in = inverse_rms(value)
    normed = (value * inv_in * gain_pre).astype(BF)
    qkv = matmul(normed, dense_qkv).astype(BF)
    pairs, queries = dense_to_heads(
        lines, 2, qkv[:, : 2 * part], pack(qkv[:, 2 * part :]), "dense_to_heads"
    )
    routed_rest = gather(after(routed_rest, queries))
    queries = queries.reshape(group, seqs, rows // 2, lanes)
    pairs = pairs.reshape(ring, group, seqs, rows, lanes)
    mixed, mixed_turned, lse = dense_forward(place, queries, pairs, start)
    packed = (tokens // 2, group * lanes)
    (mixed,) = swap_blocks(
        lines, 3, "z", [mixed.reshape(group, tokens // 2, lanes)], [(packed, BF)], [(0, slot, 0, columns(lanes))],
        "dense_mixed",
    )
    mixed = gather_columns(lines, 4, unpack(mixed), "dense_mixed_columns")
    attended = gather_columns(lines, 5, matmul(mixed, dense_out).astype(BF), "dense_attended")
    middle_value = value + attended.astype(F32)
    inv_mid = inverse_rms(middle_value)
    normed_mid = (middle_value * inv_mid * gain_mid).astype(BF)
    hidden_pre = matmul(normed_mid, dense_exp)
    hidden = jax.nn.gelu(hidden_pre).astype(BF)
    fed = scatter_columns(lines, 6, matmul(hidden, dense_shr).astype(BF), None, "dense_fed")
    after_dense = own_columns(middle_value) + fed

    def outer(left, right):
        return contract(left, right, 0, 0).astype(BF)

    def vector_columns(vectors):
        wide = jnp.zeros((width, 128), F32)
        stacked = jnp.pad(jnp.stack(vectors, axis=1), ((0, 0), (0, 128 - len(vectors))))
        return lax.dynamic_update_slice(wide, stacked, (section * part, 0)).astype(BF)

    def reduce_dp(value):
        return lax.psum_scatter(value, "dp", scatter_dimension=0, tiled=True)

    source = jnp.concatenate([after_dense.astype(BF), own_columns(grad_top)], axis=1)
    r_picked, r_grad_sent, r_normed, r_heads, r_pairs, r_turned, r_lse, r_mixed = routed_enter(
        lines, 7, source.reshape(seqs, rows, 2 * part), chosen_rows, routed_start, gains[2:3], routed_qkv, sel
    )
    (
        r_normed_mid,
        r_grad_pre,
        r_hidden,
        r_fed_low,
        r_grad_middle,
        r_grad_attended,
        r_sent,
        r_logit,
        r_vectors,
    ) = routed_feed(lines, 13, r_picked, r_grad_sent, r_mixed, gains[3:5], routed_rest, part)
    routed_grads = jnp.concatenate(
        [
            outer(r_normed_mid, r_grad_pre),
            outer(r_hidden, r_fed_low),
            vector_columns([r_vectors[0], r_vectors[1]]),
        ],
        axis=1,
    )
    routed_shard = reduce_dp(routed_grads)
    r_grad_attended = after(r_grad_attended, routed_grads)
    returned, added, r_grad_qkv, r_vectors = routed_leave(
        lines,
        14,
        r_grad_attended,
        routed_rest[:, :part],
        routed_qkv,
        (r_heads, r_pairs, r_turned, r_lse),
        routed_start,
        r_picked,
        (r_grad_middle, r_logit, r_sent),
        jnp.concatenate([gains[2:3], gains[4:5]], axis=0),
        chosen_rows,
        sel,
        rows,
    )
    routed_shard_in = reduce_dp(
        jnp.concatenate(
            [outer(r_normed, r_grad_qkv), outer(r_mixed, r_grad_attended), vector_columns([r_vectors[0]])], axis=1
        )
    )
    stream_out = (after_dense + added.reshape(tokens, part).astype(F32)).astype(BF).reshape(seqs, rows, part)

    grad_after = grad_top.astype(F32) + returned.reshape(tokens, width).astype(F32)
    fed_low = grad_after.astype(BF)
    _, gelu_pull = jax.vjp(jax.nn.gelu, hidden_pre)
    grad_pre = gelu_pull(contract(fed_low, dense_shr, 1, 1))[0].astype(BF)
    grad_normed = contract(grad_pre, dense_exp, 1, 1)
    scalar = jnp.sum(grad_normed * middle_value * gain_mid, axis=1)
    grad_normed, scalar = scatter_columns(lines, 8, grad_normed.astype(BF), scalar, "dense_back_mid")
    middle_own = own_columns(middle_value)
    grad_gain_mid = jnp.sum(grad_normed * middle_own * inv_mid, axis=0)
    grad_middle = (
        inv_mid * (grad_normed * own_columns(gain_mid))
        - middle_own * (inv_mid * inv_mid * inv_mid) * (scalar * (1.0 / width))[:, None]
        + own_columns(grad_after)
    )
    grad_attended = grad_middle.astype(BF)
    dense_grads = jnp.concatenate(
        [outer(normed_mid, grad_pre), outer(hidden, fed_low), vector_columns([grad_gain_mid])], axis=1
    )
    dense_shard = reduce_dp(dense_grads)
    grad_mixed = scatter_columns(
        lines, 9, contract(grad_attended, dense_out, 1, 1).astype(BF), None, "dense_back_mixed"
    ).astype(BF)
    dense_shard_out = reduce_dp(outer(mixed, grad_attended))
    (grad_heads,) = swap_blocks(
        lines, 10, "z", [pack(grad_mixed)], [((group, tokens // 2, lanes), BF)], [(0, columns(lanes), 0, slot)],
        "dense_grad_to_heads",
    )
    dq, dkv = dense_backward(
        place,
        queries,
        grad_heads.reshape(group, seqs, rows // 2, lanes),
        pairs,
        start,
        mixed_turned,
        lse,
    )
    dkv, dq, (routed_all, routed_all_in) = dense_from_heads(
        lines,
        11,
        dkv.reshape(ring, group, tokens, lanes),
        dq.reshape(group, tokens // 2, lanes),
        [routed_shard, routed_shard_in],
        "dense_from_heads",
    )
    grad_qkv = jnp.concatenate([dkv, unpack(dq)], axis=1)
    grad_normed = contract(grad_qkv, dense_qkv, 1, 1)
    scalar = jnp.sum(grad_normed * value * gain_pre, axis=1)
    value_own = own_columns(value)
    grad_normed, scalar, grad_gain_pre, dense_all_in, (dense_all, dense_all_out) = dense_finish(
        lines,
        12,
        grad_normed.astype(BF),
        scalar,
        value_own * inv_in,
        outer(normed, grad_qkv),
        [dense_shard, dense_shard_out],
        "dense_finish",
    )
    grad_in = (
        inv_in * (grad_normed * own_columns(gain_pre))
        - value_own * (inv_in * inv_in * inv_in) * (scalar * (1.0 / width))[:, None]
    )
    stream_grad = (grad_middle + grad_in).astype(BF).reshape(seqs, rows, part)

    share = hidden_size // dp
    local = width // dp
    middle_at = hidden_size + width
    r_exp, r_shr, r_mid, r_keys, r_values, r_query, r_out, r_pre = assemble(
        [
            ("hidden", routed_all, 0, hidden_size),
            ("stack", routed_all, hidden_size, width),
            ("sum", routed_all, middle_at, 128),
            ("pair", routed_all_in, 0, 2 * part),
            ("columns", routed_all_in, 2 * part, part),
            ("columns", routed_all_in, 3 * part, part),
            ("sum", routed_all_in, 4 * part, 128),
        ],
        share,
        "routed_places",
    )
    d_exp, d_shr, d_mid, d_keys, d_values, d_query, d_out = assemble(
        [
            ("hidden", dense_all, 0, hidden_size),
            ("stack", dense_all, hidden_size, width),
            ("sum", dense_all, middle_at, 128),
            ("pair", dense_all_in, 0, 2 * part),
            ("columns", dense_all_in, 2 * part, part),
            ("columns", dense_all_out, 0, part),
        ],
        share,
        "dense_places",
    )
    d_pre = lax.dynamic_slice_in_dim(grad_gain_pre, rank * local, local)
    d_shr = d_shr.reshape(sections * share, width)
    r_shr = r_shr.reshape(sections * share, width)
    return (
        (stream_out, stream_grad)
        + (d_pre, d_query, d_keys, d_values, d_out, d_mid[:, 0], d_exp, d_shr)
        + (r_pre[:, 0], r_query, r_keys, r_values, r_out, r_mid[:, 0], r_exp, r_shr)
        + (r_mid[:, 1],)
    )


def solution(mesh):
    streams, row, vector, copied = P(None, "dp", None), P("dp", None), P("dp"), P()
    layer = (vector, row, row, row, row, vector, row, row)
    outs = (P(None, "dp", "section"),) * 2 + layer + layer + (vector,)
    return jax.shard_map(
        on_device,
        mesh=mesh,
        in_specs=(streams, copied, copied, streams) + layer + layer + (vector,),
        out_specs=outs,
        check_vma=False,
    )
```

time: 700 us -> 614 us (0.88)
  waiting for transfers between devices: 96.1 us -> 22.3 us
  Pallas kernels: 406 us -> 386 us
  matrix products: 33.6 us -> 42.6 us
    reduce_scatter x2 -> x4, waiting for transfers between devices: 95.3 us -> 21.7 us  [reduce_dp(): return lax.psum_scatter(value, 'dp', scatter_dimension=0, tiled=True)]
    pallas_call x14, Pallas kernels: 384 us -> 357 us  [communicate(): pl.pallas_call(kernel, out_shape=[jax.ShapeDtypeStruct(s, d) for s, d in...]
    concatenate x4 -> x7, other arithmetic: 1.89 us -> 20.8 us  [the longest x1 11.2 us: on_device(): jnp.concatenate([outer(r_normed_mid, r_grad_pre), outer(r_hidden, r_fed_l...]
    unnamed x165 -> x219, local copies, waits for them, and re-layouts: 32 us -> 50.3 us
    convert_element_type x6 -> x0, local copies, waits for them, and re-layouts: 17 us -> none  [the longest x4 12.3 us: finish(): jnp.transpose(expand, (1, 2, 0, 3)).reshape(local, sections * hidden_size)]
    convert_element_type x9 -> x2, other arithmetic: 18 us -> 2.27 us  [the longest x1 2.26 us: on_device(): stream_grad = (grad_middle + grad_in).astype(BF).reshape(seqs, rows, part)]
    dot_general x12, matrix products: 26.7 us -> 35.7 us  [contract(): lax.dot_general(left, right, (((ldim,), (rdim,)), ((), ())), preferred_el...]
    reshape x4 -> x2, local copies, waits for them, and re-layouts: 7.06 us -> 0.01 us  [scalar_block(): jnp.pad(scalars, (0, count * 128 - scalars.shape[0])).reshape(count, 128)]
  transfers between devices with their start and end apart: 5 -> 7, of which waited for: 2 -> 1; matrix products, arithmetic and copies ran while one was open for 9% -> 16% of each run, Pallas kernels for 22% -> 46%
where the time goes in v3:
time: 614 us; the launch traced here: 605 us
  Pallas kernels  386 us (63%)
  local copies, waits for them, and re-layouts  101 us (16%)
  matrix products  42.6 us (7%)
  other arithmetic  36.3 us (6%)
  waiting for transfers between devices  22.3 us (4%)
  between operations  15.8 us (3%)
    pallas_call x14, Pallas kernels, communicate(): pl.pallas_call(kernel, out_shape=[jax.ShapeDtypeStruct(s, d) for s, d in...  357 us
    unnamed x219, local copies, waits for them, and re-layouts  50.3 us
    dot_general x12, matrix products, contract(): lax.dot_general(left, right, (((ldim,), (rdim,)), ((), ())), preferred_el...  35.7 us
    reduce_scatter x4, waiting for transfers between devices, reduce_dp(): return lax.psum_scatter(value, 'dp', scatter_dimension=0, tiled=True)  21.7 us
    pallas_call x1, Pallas kernels, dense_backward(): pl.pallas_call(dense_backward_kernel, grid_spec=grid, out_shape=[jax.Shap...  12.5 us
  transfers between devices with their start and end apart: 7, of which 1 were waited for; matrix products, arithmetic and copies ran while one was open for 16% of the time, Pallas kernels for 46%

profile of v3, /device:TPU:0, one launch (start us, length us, event | category | flops | bytes accessed | tf_op | source)
XLA Modules:
  0.0 605.1 jit_solution(17834349001500327644)
XLA Ops:
  7.3 1.9 reshape.385
  9.1 2.6 reshape.392
  11.7 5.0 dynamic-slice_reduce_fusion
  22.8 45.8 %first_weights.1 = (bf16[8,128,768]{2,1,0:T(8,128)(2,1)S(1)}, bf16[8,16,128]{2,1,0:T(8,128)(2,1)S(1)}) custom-call(bf16[128,768]{1,0:T(8,128)(2,1)S(1)} %pad_maximum_fusion.6.refs_0_, bf16[16,128]{1,0:T(8,128)(2,1)S(1)} %pad.22.refs_1_), custom_call_target="tpu_custom_call" | custom-call | tf_op jit(solution)/shard_map/first_weights/pallas_call | solution.py:99
  68.6 1.7 constant_dynamic-slice_fusion.4
  70.2 1.6 pad_maximum_fusion.7
  73.4 1.4 convolution_convert_fusion.7
  76.7 31.0 %dense_to_heads.1 = (bf16[2,4,768,128]{3,2,1,0:T(8,128)(2,1)S(1)}, bf16[4,384,128]{2,1,0:T(8,128)(2,1)S(1)}) custom-call(bf16[768,512]{1,0:T(8,128)(2,1)S(1)} %slice.186.p_ref, bf16[384,512]{1,0:T(8,128)(2,1)S(1)} %reshape.411.q_ref), custom_call_target="tpu_custom_call" | custom-call | tf_op jit(solution)/shard_map/dense_to_heads/pallas_call | solution.py:99
  108.7 1.7 pad_maximum_fusion.5
  111.8 9.2 %dense_attention.1 = (bf16[4,3,128,128]{3,2,1,0:T(8,128)(2,1)S(1)}, bf16[3,4,64,256]{3,2,1,0:T(8,128)(2,1)S(1)}, f32[3,4,1,256]{3,2,1,0:T(1,128)S(1)}) custom-call(s32[1]{0:T(128)} %bitcast.1.place_ref, bf16[4,3,128,128]{3,2,1,0:T(8,128)(2,1)S(1)} %bitcast.120, bf16[2,4,3,256,128]{4,3,2,1,0:T(8,128)(2,1)S(1)} %bitcast.117, ...), custom_call_target="tpu_custom_call" | custom-call | tf_op jit(solution)/shard_map/dense_attention/pallas_call | solution.py:719
  122.4 13.1 %dense_mixed.1 = bf16[384,512]{1,0:T(8,128)(2,1)S(1)} custom-call(bf16[4,384,128]{2,1,0:T(8,128)(2,1)S(1)} %bitcast.125), custom_call_target="tpu_custom_call" | custom-call | tf_op jit(solution)/shard_map/dense_mixed/pallas_call | solution.py:99
  138.7 16.1 %dense_mixed_columns.1 = bf16[768,1024]{1,0:T(8,128)(2,1)S(1)} custom-call(bf16[768,256]{1,0:T(8,128)(2,1)S(1)} %copy-done.16), custom_call_target="tpu_custom_call" | custom-call | tf_op jit(solution)/shard_map/dense_mixed_columns/pallas_call | solution.py:99
  154.7 1.3 broadcast_in_dim.135.row_ref
  157.3 1.5 select_select_fusion
  158.8 1.4 reshape.389
  160.2 1.3 constant_dynamic-slice_fusion.8
  162.8 1.6 copy.169.column_ref
  165.7 1.8 constant_dynamic-slice_fusion.9
  167.5 1.4 slice_bitcast_fusion.gains_ref
  168.8 1.7 convolution_convert_fusion.10.x_ref
  170.6 15.3 %dense_attended.1 = bf16[768,1024]{1,0:T(8,128)(2,1)S(1)} custom-call(bf16[768,256]{1,0:T(8,128)(2,1)S(1)} %convolution_convert_fusion.10.x_ref), custom_call_target="tpu_custom_call" | custom-call | tf_op jit(solution)/shard_map/dense_attended/pallas_call | solution.py:99
  188.2 1.7 copy-done.79
  189.9 1.8 fusion.15
  191.8 2.0 fusion.17.refs_0_
  193.8 14.4 %dense_fed.1 = f32[768,256]{1,0:T(8,128)S(1)} custom-call(bf16[768,1024]{1,0:T(8,128)(2,1)S(1)} %fusion.17.refs_0_), custom_call_target="tpu_custom_call" | custom-call | tf_op jit(solution)/shard_map/dense_fed/pallas_call | solution.py:99
  208.5 1.4 copy-done.2
  211.5 37.8 %routed_enter.1 = (bf16[96,1024]{1,0:T(8,128)(2,1)S(1)}, bf16[96,1024]{1,0:T(8,128)(2,1)S(1)}, bf16[96,1024]{1,0:T(8,128)(2,1)S(1)}, bf16[4,96,256]{2,1,0:T(8,12...) custom-call(bf16[3,256,512]{2,1,0:T(8,128)(2,1)S(1)} %bitcast.119, ...), custom_call_target="tpu_custom_call" | custom-call | tf_op jit(solution)/shard_map/routed_enter/pallas_call | solution.py:99
  254.6 2.3 copy-done.6
  260.5 16.5 %routed_feed.1 = (bf16[96,1024]{1,0:T(8,128)(2,1)S(1)}, bf16[96,1024]{1,0:T(8,128)(2,1)S(1)}, bf16[96,1024]{1,0:T(8,128)(2,1)S(1)}, bf16[96,1024]{1,0:T(8,128)(2...) custom-call(bf16[96,1024]{1,0:T(8,128)(2,1)S(1)} %copy-done.20, ...), custom_call_target="tpu_custom_call" | custom-call | tf_op jit(solution)/shard_map/routed_feed/pallas_call | solution.py:99
  281.9 11.2 %pad_maximum_fusion = bf16[1024,2176]{1,0:T(8,128)(2,1)} fusion(bf16[1024,128]{1,0:T(8,128)(2,1)S(1)} %pad_dynamic-update-slice_fusion.2, bf16[1024,1024]{1,0:T(8,128)(2,1)S(1)} %convolution_convert_fusion, bf16[1024,1024]{1,0:T(8,128)(2,1)S(1)} %convolution_convert_fusion.1), kind=kLoop, calls=%fused_computation.2 | loop fusion | flops 13369344 | bytes 8912896 | tf_op jit(solution)/shard_map/concatenate | solution.py:1453
  295.3 1.4 copy-done.3
  304.7 41.0 %routed_leave.1 = (bf16[3,256,1024]{2,1,0:T(8,128)(2,1)S(1)}, bf16[3,256,256]{2,1,0:T(8,128)(2,1)S(1)}, bf16[96,768]{1,0:T(8,128)(2,1)S(1)}, f32[8,256]{1,0:T(8,128)S(1)}) custom-call(bf16[96,256]{1,0:T(8,128)(2,1)S(1)} %copy-done.38, bf16[1024,256]{1,0:T(8,128)(2,1)S(1)} %slice.194.out_ref, bf16[1024,768]{1,0:T(8,128)(2,1)S(1)} %copy-done.3, ...), custom_call_target="tpu_custom_call" | custom-call | tf_op jit(solution)/shard_map/routed_leave/pallas_call | solution.py:99
  347.7 1.5 convolution_convert_fusion.4
  349.3 2.7 pad_maximum_fusion.2
  353.4 2.7 convert_add_fusion
  356.2 6.2 %fusion.6 = bf16[768,1024]{1,0:T(8,128)(2,1)S(1)} fusion(f32[768,1024]{1,0:T(8,128)S(1)} %copy-done.104, bf16[1024,2304]{1,0:T(8,128)(2,1)} %all-gather.4.cloned.1.call-done, f32[768,1024]{1,0:T(8,128)S(1)} %convert_add_fusion), kind=kOutput, calls=%fused_computation.10 | convolution fusion | flops 1627127808 | bytes 9961472 | tf_op jit(solution)/shard_map/dot_general | solution.py:27
  362.5 4.2 multiply_reduce_fusion.1
  366.7 17.1 %dense_back_mid.1 = (f32[768,256]{1,0:T(8,128)S(1)}, f32[8,128]{1,0:T(8,128)S(1)}) custom-call(bf16[768,1024]{1,0:T(8,128)(2,1)S(1)} %get-tuple-element.163.refs_0_, f32[8,128]{1,0:T(8,128)S(1)} %pad_bitcast_fusion.1.refs_1_), custom_call_target="tpu_custom_call" | custom-call | tf_op jit(solution)/shard_map/dense_back_mid/pallas_call | solution.py:99
  383.8 2.6 multiply_reduce_fusion.4
  386.6 3.1 convolution_convert_fusion.8
  389.7 5.7 convolution_convert_fusion.3
  395.7 5.5 convolution_convert_fusion.2
  401.1 2.3 pad_maximum_fusion.1
  406.9 1.5 copy-done.67
  408.3 1.6 convolution_convert_fusion.6.refs_0_
  410.0 15.4 %dense_back_mixed.1 = f32[768,256]{1,0:T(8,128)S(1)} custom-call(bf16[768,1024]{1,0:T(8,128)(2,1)S(1)} %convolution_convert_fusion.6.refs_0_), custom_call_target="tpu_custom_call" | custom-call | tf_op jit(solution)/shard_map/dense_back_mixed/pallas_call | solution.py:99
  428.2 3.1 copy.194
  431.3 2.7 reshape.413.refs_0_
  434.0 14.7 %dense_grad_to_heads.1 = bf16[4,384,128]{2,1,0:T(8,128)(2,1)S(1)} custom-call(bf16[384,512]{1,0:T(8,128)(2,1)S(1)} %reshape.413.refs_0_), custom_call_target="tpu_custom_call" | custom-call | tf_op jit(solution)/shard_map/dense_grad_to_heads/pallas_call | solution.py:99
  449.4 12.5 %dense_attention_grad.1 = (bf16[4,3,128,128]{3,2,1,0:T(8,128)(2,1)S(1)}, bf16[2,4,3,256,128]{4,3,2,1,0:T(8,128)(2,1)S(1)}) custom-call(s32[1]{0:T(128)} %bitcast.1.place_ref, bf16[4,3,128,128]{3,2,1,0:T(8,128)(2,1)S(1)} %bitcast.121, bf16[4,3,128,128]{3,2,1,0:T(8,128)(2,1)S(1)} %bitcast.122, bf16[2,4,3,256,128]{4,3,2,1,0:T(8,128)(2,1)S(1)} %bitcast.118, ...), custom_call_target="tpu_custom_call" | custom-call | tf_op jit(solution)/shard_map/dense_attention_grad/pallas_call | solution.py:791
  463.1 1.4 copy-done.13
  466.5 32.7 %dense_from_heads.1 = (bf16[768,512]{1,0:T(8,128)(2,1)S(1)}, bf16[384,512]{1,0:T(8,128)(2,1)S(1)}, bf16[128,8704]{1,0:T(8,128)(2,1)S(1)}, bf16[128,4608]{1,0:T(8,128)(2,1)S(1)}) custom-call(bf16[2,4,768,128]{3,2,1,0:T(8,128)(2,1)S(1)} %bitcast.123, bf16[4,384,128]{2,1,0:T(8,128)(2,1)S(1)} %bitcast.126, bf16[128,2176]{1,0:T(8,128)(2,1)S(1)} %copy-done.25, ...), custom_call_target="tpu_custom_call" | custom-call | tf_op jit(solution)/shard_map/dense_from_heads/pallas_call | solution.py:99
  499.2 1.3 copy-done.7
  502.7 1.7 copy.195
  505.7 1.7 copy-done.8
  507.4 3.5 routed_places.1
  511.6 2.6 multiply_reduce_fusion
  515.5 2.7 convolution_convert_fusion.5
  518.3 21.7 %reduce-scatter.9.cloned.1.call-done.refs_0_ = bf16[128,2176]{1,0:T(8,128)(2,1)} async-done(((bf16[1024,2176]{1,0:T(8,128)(2,1)}), bf16[128,2176]{1,0:T(8,128)(2,1)}) %reduce-scatter.9.cloned.1.call-update) | async-done | bytes 557072 | tf_op jit(solution)/shard_map/reduce_scatter | solution.py:1436
  540.0 1.4 copy-done.11
  541.4 1.4 copy-done.14
  544.7 46.6 %dense_finish.1 = (f32[768,256]{1,0:T(8,128)S(1)}, f32[8,128]{1,0:T(8,128)S(1)}, f32[8,1024]{1,0:T(8,128)S(1)}, bf16[128,3072]{1,0:T(8,128)(2,1)S(1)}, bf16[128,...) custom-call(bf16[768,1024]{1,0:T(8,128)(2,1)S(1)} %copy-done.11, f32[8,128]{1,0:T(8,128)S(1)} %pad_bitcast_fusion.e_ref, ...), custom_call_target="tpu_custom_call" | custom-call | tf_op jit(solution)/shard_map/dense_finish/pallas_call | solution.py:99
  591.3 3.0 dense_places.1
  595.5 2.3 add_convert_fusion
  (312 shorter events, 70.4 us)
Async XLA Ops:
  7.2 10.4 %copy-start = (bf16[512,1024]{1,0:T(8,128)(2,1)S(1)}, bf16[512,1024]{1,0:T(8,128)(2,1)}, u32[]{:S(2)}) copy-start(bf16[512,1024]{1,0:T(8,128)(2,1)} %param.32) | copy-start | bytes 3145732
  7.2 161.6 %all-gather.4.cloned.1.call-start = ((), (), s32[]{:S(2)}) async-start(), calls=%async_computation.4 | async-start | bytes 5308416 | tf_op jit(solution)/shard_map/all_gather | solution.py:1345
  16.7 6.0 copy-start.98
  16.7 6.0 copy-start.99
  16.7 6.0 copy-start.100
  16.7 6.0 copy-start.101
  16.7 6.0 copy-start.102
  17.6 54.3 %copy-start.62 = (bf16[3,256,1024]{2,1,0:T(8,128)(2,1)S(1)}, bf16[3,256,1024]{2,1,0:T(8,128)(2,1)}, u32[]{:S(2)}) copy-start(bf16[3,256,1024]{2,1,0:T(8,128)(2,1)} %param.21) | copy-start | bytes 4718596
  18.5 190.0 %all-gather.6.cloned.1.call-start = ((), (), s32[]{:S(2)}) async-start(), calls=%async_computation.5 | async-start | bytes 1769472 | tf_op jit(solution)/shard_map/all_gather | solution.py:1345
  68.5 6.3 %copy-start.60 = (bf16[8,128,768]{2,1,0:T(8,128)(2,1)}, bf16[8,128,768]{2,1,0:T(8,128)(2,1)S(1)}, u32[]{:S(2)}) copy-start(bf16[8,128,768]{2,1,0:T(8,128)(2,1)S(1)} %get-tuple-element.80) | copy-start | bytes 4718596
  71.9 182.8 %all-gather.8.cloned.1.call-start = ((), (), s32[]{:S(2)}) async-start(), calls=%async_computation.6 | async-start | bytes 5308416 | tf_op jit(solution)/shard_map/all_gather | solution.py:1345
  72.3 2.5 copy-start.80
  72.3 2.5 copy-start.78
  73.0 1.9 copy-start.82
  74.9 1.7 copy-start.76
  75.3 35.5 %copy-start.81 = (s32[3,2048]{1,0:T(4,128)S(1)}, s32[3,2048]{1,0:T(4,128)}, u32[]{:S(2)}) copy-start(s32[3,2048]{1,0:T(4,128)} %param.22) | copy-start | bytes 73732
  110.4 352.7 %reduce-scatter.7.cloned.1.call-start = ((), (), s32[]{:S(2)}) async-start(), calls=%async_computation.8 | async-start | bytes 2654208 | tf_op jit(solution)/shard_map/reduce_scatter | solution.py:1436
  154.7 31.1 %copy-start.9 = (bf16[768,1024]{1,0:T(8,128)(2,1)}, bf16[768,1024]{1,0:T(8,128)(2,1)S(1)}, u32[]{:S(2)}) copy-start(bf16[768,1024]{1,0:T(8,128)(2,1)S(1)} %dense_mixed_columns.1) | copy-start | bytes 4718596
  168.8 17.0 %copy-start.63 = (bf16[3,256,1024]{2,1,0:T(8,128)(2,1)S(1)}, bf16[3,256,1024]{2,1,0:T(8,128)(2,1)}, u32[]{:S(2)}) copy-start(bf16[3,256,1024]{2,1,0:T(8,128)(2,1)} %param.21) | copy-start | bytes 4718596
  185.9 4.0 copy-start.79
  185.9 4.0 copy-start.96
  187.0 21.2 %copy-start.69 = (f32[768,1024]{1,0:T(8,128)}, f32[768,1024]{1,0:T(8,128)S(1)}, u32[]{:S(2)}) copy-start(f32[768,1024]{1,0:T(8,128)S(1)} %get-tuple-element.165) | copy-start | bytes 9437188
  191.8 2.0 copy-start.103
  193.8 14.6 %copy-start.75 = (bf16[768,256]{1,0:T(8,128)(2,1)S(1)}, bf16[768,256]{1,0:T(8,128)(2,1)}, u32[]{:S(2)}) copy-start(bf16[768,256]{1,0:T(8,128)(2,1)} %constant_dynamic-slice_fusion.9) | copy-start | bytes 1179652
  208.5 1.4 copy-start.2
  254.6 2.3 copy-start.6
  280.3 1.5 copy-start.77
  281.8 11.2 %copy-start.24 = (bf16[96,1024]{1,0:T(8,128)(2,1)S(1)}, bf16[96,1024]{1,0:T(8,128)(2,1)}, u32[]{:S(2)}) copy-start(bf16[96,1024]{1,0:T(8,128)(2,1)} %copy-done.22) | copy-start | bytes 589828
  281.8 11.2 %copy-start.37 = (bf16[96,256]{1,0:T(8,128)(2,1)S(1)}, bf16[96,256]{1,0:T(8,128)(2,1)}, u32[]{:S(2)}) copy-start(bf16[96,256]{1,0:T(8,128)(2,1)} %copy-done.36) | copy-start | bytes 147460
  281.9 13.4 %copy-start.21 = (bf16[96,1024]{1,0:T(8,128)(2,1)S(1)}, bf16[96,1024]{1,0:T(8,128)(2,1)}, u32[]{:S(2)}) copy-start(bf16[96,1024]{1,0:T(8,128)(2,1)} %copy-done.19) | copy-start | bytes 589828
  281.9 13.4 %copy-start.54 = (s32[3,1,128]{2,1,0:T(1,128)S(1)}, s32[3,1,128]{2,1,0:T(1,128)}, u32[]{:S(2)}) copy-start(s32[3,1,128]{2,1,0:T(1,128)} %reshape.390.start_ref) | copy-start | bytes 4612
  293.1 54.7 %copy-start.31 = (bf16[96,1024]{1,0:T(8,128)(2,1)S(1)}, bf16[96,1024]{1,0:T(8,128)(2,1)}, u32[]{:S(2)}) copy-start(bf16[96,1024]{1,0:T(8,128)(2,1)} %copy-done.30) | copy-start | bytes 589828
  295.3 1.4 copy-start.3
  352.0 111.0 %reduce-scatter.5.cloned.1.call-start = ((), (), s32[]{:S(2)}) async-start(), calls=%async_computation.7 | async-start | bytes 5013504 | tf_op jit(solution)/shard_map/reduce_scatter | solution.py:1436
  352.6 165.6 %reduce-scatter.11.cloned.1.call-start = ((), (), s32[]{:S(2)}) async-start(), calls=%async_computation.10 | async-start | bytes 589824 | tf_op jit(solution)/shard_map/reduce_scatter | solution.py:1436
  353.4 2.8 copy-start.104
  356.2 27.6 %copy-start.72 = (f32[768,1024]{1,0:T(8,128)}, f32[768,1024]{1,0:T(8,128)S(1)}, u32[]{:S(2)}) copy-start(f32[768,1024]{1,0:T(8,128)S(1)} %convert_add_fusion) | copy-start | bytes 9437188
  356.2 6.2 %copy-start.5 = (bf16[768,1024]{1,0:T(8,128)(2,1)S(1)}, bf16[768,1024]{1,0:T(8,128)(2,1)}, u32[]{:S(2)}) copy-start(bf16[768,1024]{1,0:T(8,128)(2,1)} %copy-done.4) | copy-start | bytes 4718596
  356.2 6.2 %copy-start.64 = (bf16[3,256,1024]{2,1,0:T(8,128)(2,1)S(1)}, bf16[3,256,1024]{2,1,0:T(8,128)(2,1)}, u32[]{:S(2)}) copy-start(bf16[3,256,1024]{2,1,0:T(8,128)(2,1)} %param.21) | copy-start | bytes 4718596
  356.2 6.2 %copy-start.97 = (f32[1,8,128]{2,0,1:T(1,128)S(1)}, f32[1,8,128]{2,0,1:T(1,128)}, u32[]{:S(2)}) copy-start(f32[1,8,128]{2,0,1:T(1,128)} %get-tuple-element.170) | copy-start | bytes 12292
  362.5 4.2 copy-start.105
  362.5 21.3 %copy-start.86 = (f32[768]{0:T(1024)S(1)}, f32[768]{0:T(1024)}, u32[]{:S(2)}) copy-start(f32[768]{0:T(1024)} %copy-done.85) | copy-start | bytes 9220
  362.5 21.3 %copy-start.87 = (f32[768]{0:T(1024)S(1)}, f32[768]{0:T(1024)}, u32[]{:S(2)}) copy-start(f32[768]{0:T(1024)} %get-tuple-element.174) | copy-start | bytes 9220
  395.4 144.6 %reduce-scatter.9.cloned.1.call-start = ((), (), s32[]{:S(2)}) async-start(), calls=%async_computation.9 | async-start | bytes 5013504 | tf_op jit(solution)/shard_map/reduce_scatter | solution.py:1436
  395.7 5.5 copy-start.73
  403.5 2.7 copy-start.65
  406.2 2.2 copy-start.70
  406.7 1.7 copy-start.67
  425.4 23.3 %copy-start.28 = (bf16[3,4,64,256]{3,2,1,0:T(8,128)(2,1)S(1)}, bf16[3,4,64,256]{3,2,1,0:T(8,128)(2,1)}, u32[]{:S(2)}) copy-start(bf16[3,4,64,256]{3,2,1,0:T(8,128)(2,1)} %copy-done.27) | copy-start | bytes 1179652
  463.1 1.4 copy-start.13
  499.2 1.4 copy-start.7
  501.6 4.1 copy-start.18
  504.4 6.6 %copy-start.83 = (f32[1,8,128]{2,0,1:T(1,128)S(1)}, f32[1,8,128]{2,0,1:T(1,128)}, u32[]{:S(2)}) copy-start(f32[1,8,128]{2,0,1:T(1,128)} %copy-done.82) | copy-start | bytes 12292
  505.7 1.7 copy-start.8
  507.3 3.6 copy-start.74
  507.3 3.7 copy-start.61
  507.3 4.2 copy-start.66
  511.6 4.0 copy-start.68
  540.0 1.4 copy-start.11
  541.4 1.4 copy-start.14
  544.7 50.8 %copy-start.71 = (f32[768,256]{1,0:T(8,128)S(1)}, f32[768,256]{1,0:T(8,128)}, u32[]{:S(2)}) copy-start(f32[768,256]{1,0:T(8,128)} %get-tuple-element.158) | copy-start | bytes 2359300
  544.7 50.8 %copy-start.84 = (f32[768]{0:T(1024)S(1)}, f32[768]{0:T(1024)}, u32[]{:S(2)}) copy-start(f32[768]{0:T(1024)} %multiply_multiply_fusion.2) | copy-start | bytes 9220
  544.7 50.8 %copy-start.95 = (f32[1,256]{1,0:T(1,128)S(1)}, f32[1,256]{1,0:T(1,128)}, u32[]{:S(2)}) copy-start(f32[1,256]{1,0:T(1,128)} %constant_dynamic-slice_fusion.1) | copy-start | bytes 3076
  544.7 53.1 %copy-start.1 = (bf16[512,1024]{1,0:T(8,128)(2,1)S(1)}, bf16[512,1024]{1,0:T(8,128)(2,1)}, u32[]{:S(2)}) copy-start(bf16[512,1024]{1,0:T(8,128)(2,1)} %param.32) | copy-start | bytes 3145732
  (49 other events, 37.1 us)
Sparse Core Ops, SparseCore 0:
  18.7 82.9 all-gather.3
  103.9 31.1 all-gather.5
  137.3 48.9 all-gather.7
  352.2 37.6 reduce-scatter.6
  392.0 55.0 reduce-scatter.4
  449.8 34.4 reduce-scatter.10
  486.7 53.2 reduce-scatter.8

commit v4 on v3

v4 whole, which is shorter than its diff:
```python
import functools

import jax
import jax.numpy as jnp
from jax import lax
from jax.experimental import pallas as pl
from jax.experimental.pallas import tpu as pltpu
from jax.sharding import PartitionSpec as P

HEADS = 16
HDIM = 64
DOCS = 8
EPS = 1e-06
NEG = -1e30
SCALE = HDIM ** (-0.5)
VMEM = 32 * 2**20
MESH = pl.DeviceIdType.MESH
BF = jnp.bfloat16
F32 = jnp.float32


def matmul(left, right):
    return jnp.dot(left, right, preferred_element_type=F32)


def contract(left, right, ldim, rdim):
    return lax.dot_general(left, right, (((ldim,), (rdim,)), ((), ())), preferred_element_type=F32)


class Lines:
    def __init__(self, sections, dp, group):
        self.sizes = {"section": sections, "z": group, "core": dp // group}
        self.ring = dp // group

    def place(self, kind):
        if kind == "section":
            return lax.axis_index("section")
        index = lax.axis_index("dp")
        return index // self.ring if kind == "z" else lax.rem(index, self.ring)

    def device(self, kind, place):
        if kind == "section":
            return {"section": place}
        index = lax.axis_index("dp")
        if kind == "z":
            return {"dp": place * self.ring + lax.rem(index, self.ring)}
        return {"dp": (index // self.ring) * self.ring + place}

    def peers(self, kind):
        size = self.sizes[kind]
        me = self.place(kind)
        return [lax.rem(me + step, size) for step in range(1, size)]


class Copies:
    def __init__(self, lines, send, recv):
        self.lines, self.send, self.recv, self.used = lines, send, recv, 0

    def greet(self, kinds):
        barrier = pltpu.get_barrier_semaphore()
        count = 0
        for kind in kinds:
            for peer in self.lines.peers(kind):
                pl.semaphore_signal(
                    barrier, inc=1, device_id=self.lines.device(kind, peer), device_id_type=MESH
                )
                count += 1
        pl.semaphore_wait(barrier, count)

    def start(self, kind, peer, src, dst):
        assert self.used < self.send.shape[0]
        copy = pltpu.make_async_remote_copy(
            src_ref=src,
            dst_ref=dst,
            send_sem=self.send.at[self.used],
            recv_sem=self.recv.at[self.used],
            device_id=self.lines.device(kind, peer),
            device_id_type=MESH,
        )
        self.used += 1
        copy.start()
        return copy

    def swap(self, kind, src, dst):
        me = self.lines.place(kind)
        return [self.start(kind, peer, src(peer), dst(me)) for peer in self.lines.peers(kind)]


def wait(copies):
    for copy in copies:
        copy.wait()


def semaphores(count):
    return [pltpu.SemaphoreType.DMA((count,)), pltpu.SemaphoreType.DMA((count,))]


def communicate(kernel, ident, arrays, shapes, scratch, name, limit=24 * 2**20, far=()):
    vmem = pl.BlockSpec(memory_space=pltpu.VMEM)
    place = pl.BlockSpec(memory_space=pl.ANY)
    return pl.pallas_call(
        kernel,
        out_shape=[jax.ShapeDtypeStruct(s, d) for s, d in shapes],
        in_specs=[place if i in far else vmem for i in range(len(arrays))],
        out_specs=[vmem] * len(shapes),
        scratch_shapes=scratch,
        compiler_params=pltpu.CompilerParams(
            collective_id=ident, has_side_effects=True, vmem_limit_bytes=limit
        ),
        name=name,
    )(*arrays)


def span(place, width):
    return pl.ds(pl.multiple_of(place * width, width), width)


def square(lines):
    me = lines.place("section")
    low, high = lax.rem(me, 2), me // 2
    return high * 2 + 1 - low, (1 - high) * 2 + low, (1 - high) * 2 + 1 - low


def pieces_of(rows):
    half = rows // 2
    return (2, half // 2) if half % 32 == 0 else (1, half)


class SquareGather:
    @staticmethod
    def count(rows):
        return 6 * pieces_of(rows)[0]

    def __init__(self, copies, x_ref, o_ref):
        self.copies, self.x_ref, self.o_ref = copies, x_ref, o_ref
        self.width = x_ref.shape[1]
        self.me = copies.lines.place("section")
        near, far, _ = square(copies.lines)
        pieces, step = pieces_of(x_ref.shape[0])
        half = x_ref.shape[0] // 2
        self.parts = [
            (pl.ds(h * half + j * step, step), one, two)
            for j in range(pieces)
            for h, (one, two) in enumerate(((near, far), (far, near)))
        ]

    def send(self, at, to):
        dst = self.o_ref.at[at, span(self.me, self.width)]
        return self.copies.start("section", to, self.x_ref.at[at], dst)

    def start(self):
        self.first = [self.send(at, one) for at, one, _ in self.parts]
        self.rest = [self.send(at, two) for at, _, two in self.parts]
        self.o_ref[:, span(self.me, self.width)] = self.x_ref[...]

    def forward(self):
        for (at, one, two), copy in zip(self.parts, self.first):
            copy.wait_recv()
            place = self.o_ref.at[at, span(one, self.width)]
            self.rest.append(self.copies.start("section", two, place, place))

    def finish(self):
        for copy in self.first:
            copy.wait_send()
        wait(self.rest)


class SquareScatter:
    @staticmethod
    def count(rows):
        return 6 * pieces_of(rows)[0]

    @staticmethod
    def scratch(rows, width):
        return [pltpu.VMEM((2, rows, width), BF), pltpu.VMEM((rows, width), BF), pltpu.VMEM((rows, width), BF)]

    def __init__(self, copies, x_ref, got, turn, last, pieces=None):
        self.copies, self.x_ref, self.got, self.turn, self.last = copies, x_ref, got, turn, last
        self.width = turn.shape[1]
        self.me = copies.lines.place("section")
        near, far, self.across = square(copies.lines)
        half = x_ref.shape[0] // 2
        pieces, step = pieces_of(x_ref.shape[0]) if pieces is None else (pieces, half // pieces)
        self.parts = [
            (pl.ds(h * half + j * step, step), one, two)
            for j in range(pieces)
            for h, (one, two) in enumerate(((near, far), (far, near)))
        ]

    def read(self, at, place):
        return self.x_ref[at, span(place, self.width)].astype(F32)

    def start(self):
        self.passed, self.kept = [], []
        for at, one, _ in self.parts:
            for place, k, out in ((self.across, 0, self.passed), (one, 1, self.kept)):
                src = self.x_ref.at[at, span(place, self.width)]
                out.append(self.copies.start("section", one, src, self.got.at[k, at]))

    def forward(self):
        self.second = []
        for (at, _, two), copy in zip(self.parts, self.passed):
            copy.wait_recv()
            self.turn[at] = (self.read(at, two) + self.got[0, at].astype(F32)).astype(BF)
            self.second.append(self.copies.start("section", two, self.turn.at[at], self.last.at[at]))

    def finish(self, o_ref):
        for i, (at, _, _) in enumerate(self.parts):
            self.kept[i].wait_recv()
            self.second[i].wait_recv()
            o_ref[at] = self.read(at, self.me) + self.got[1, at].astype(F32) + self.last[at].astype(F32)
        for copy in self.passed + self.kept + self.second:
            copy.wait_send()


def gather_columns(lines, ident, part, name):
    rows, width = part.shape

    def kernel(x_ref, o_ref, send, recv):
        copies = Copies(lines, send, recv)
        copies.greet(["section"])
        gather = SquareGather(copies, x_ref, o_ref)
        gather.start()
        gather.forward()
        gather.finish()

    shape = ((rows, lines.sizes["section"] * width), part.dtype)
    (out,) = communicate(kernel, ident, [part], [shape], semaphores(SquareGather.count(rows)), name)
    return out


def scalar_block(scalars):
    count = -(-scalars.shape[0] // 128)
    count += -count % 8
    return jnp.pad(scalars, (0, count * 128 - scalars.shape[0])).reshape(count, 128)


def sum_places(ref):
    total = ref[0].astype(F32)
    for i in range(1, ref.shape[0]):
        total = total + ref[i].astype(F32)
    return total


def scatter_columns(lines, ident, part, scalars, name):
    rows, full = part.shape
    sections = lines.sizes["section"]
    width = full // sections
    extra = scalars is not None
    arrays = [part]
    shapes = [((rows, width), F32)]
    scratch = semaphores(SquareScatter.count(rows) + sections - 1) + SquareScatter.scratch(rows, width)
    if extra:
        arrays.append(scalar_block(scalars))
        shapes.append((arrays[1].shape, F32))
        scratch.append(pltpu.VMEM((sections,) + arrays[1].shape, F32))

    def kernel(*refs):
        x_ref, refs = refs[0], refs[1:]
        if extra:
            e_ref, o_ref, eo_ref, send, recv, got, turn, last, e_got = refs
        else:
            o_ref, send, recv, got, turn, last = refs
        copies = Copies(lines, send, recv)
        copies.greet(["section"])
        scatter = SquareScatter(copies, x_ref, got, turn, last)
        scatter.start()
        if extra:
            others = copies.swap("section", lambda peer: e_ref, lambda place: e_got.at[place])
            e_got[lines.place("section")] = e_ref[...]
        scatter.forward()
        scatter.finish(o_ref)
        if extra:
            wait(others)
            eo_ref[...] = sum_places(e_got)

    got = communicate(kernel, ident, arrays, shapes, scratch, name)
    if not extra:
        return got[0]
    return got[0], got[1].reshape(-1)[:rows]


def gather_rows(lines, ident, parts, name):
    group, ring = lines.sizes["z"], lines.sizes["core"]
    dp = group * ring
    many = len(parts)

    def kernel(*refs):
        ins, outs, (send, recv) = refs[:many], refs[many : 2 * many], refs[2 * many :]
        copies = Copies(lines, send, recv)
        rank = lax.axis_index("dp")
        zplace, place = lines.place("z"), lines.place("core")
        copies.greet(["z", "core"])
        along, handed = [], []
        for x_ref, o_ref in zip(ins, outs):
            along.append(copies.swap("z", lambda peer: x_ref, lambda _: o_ref.at[rank]))
        for x_ref, o_ref in zip(ins, outs):
            handed += copies.swap("core", lambda peer: x_ref, lambda _: o_ref.at[rank])
            o_ref[rank] = x_ref[...]
        for step in range(group - 1, 0, -1):
            source = lax.rem(zplace + step, group) * ring + place
            for arrived, o_ref in zip(along, outs):
                arrived[group - 1 - step].wait_recv()
                handed += copies.swap("core", lambda peer: o_ref.at[source], lambda _: o_ref.at[source])
        for arrived in along:
            for copy in arrived:
                copy.wait_send()
        wait(handed)

    return communicate(
        kernel,
        ident,
        parts,
        [((dp,) + part.shape, part.dtype) for part in parts],
        semaphores(many * (group - 1 + group * (ring - 1))),
        name,
    )


def swap_blocks(lines, ident, kind, arrays, shapes, plan, name):
    size = lines.sizes[kind]

    def kernel(*refs):
        ins, outs = refs[: len(arrays)], refs[len(arrays) : len(arrays) + len(shapes)]
        copies = Copies(lines, *refs[len(arrays) + len(shapes) :])
        me = lines.place(kind)
        copies.greet([kind])
        pending = []
        for i, src, o, dst in plan:
            pending += copies.swap(
                kind, lambda peer: src(ins[i], peer), lambda place: dst(outs[o], place)
            )
        for i, src, o, dst in plan:
            view = dst(outs[o], me)
            view[...] = src(ins[i], me)[...]
        wait(pending)

    return communicate(kernel, ident, arrays, shapes, semaphores((size - 1) * len(plan)), name)


def slot(ref, place):
    return ref.at[place]


def columns(width):
    def view(ref, place):
        return ref.at[:, span(place, width)]

    return view


def dense_to_heads(lines, ident, pairs, queries, name):
    group, ring = lines.sizes["z"], lines.sizes["core"]
    lanes = 2 * HDIM

    def kernel(p_ref, q_ref, po_ref, qo_ref, send, recv):
        copies = Copies(lines, send, recv)
        zplace, place = lines.place("z"), lines.place("core")
        copies.greet(["z", "core"])
        along, pending = [], []
        for peer in lines.peers("z"):
            along.append(copies.start("z", peer, p_ref.at[:, span(peer, lanes)], po_ref.at[place, zplace]))
        for peer in lines.peers("z"):
            pending.append(copies.start("z", peer, q_ref.at[:, span(peer, lanes)], qo_ref.at[zplace]))
        own = p_ref.at[:, span(zplace, lanes)]
        pending += copies.swap("core", lambda peer: own, lambda _: po_ref.at[place, zplace])
        po_ref[place, zplace] = own[...]
        qo_ref[zplace] = q_ref[:, span(zplace, lanes)]
        for step in range(group - 1, 0, -1):
            along[group - 1 - step].wait_recv()
            block = po_ref.at[place, lax.rem(zplace + step, group)]
            pending += copies.swap("core", lambda peer: block, lambda _: block)
        for copy in along:
            copy.wait_send()
        wait(pending)

    return communicate(
        kernel,
        ident,
        [pairs, queries],
        [((ring, group, pairs.shape[0], lanes), BF), ((group, queries.shape[0], lanes), BF)],
        semaphores(2 * (group - 1) + group * (ring - 1)),
        name,
    )


def dense_finish(lines, ident, vectors, weight, shards, name):
    group, ring, sections = (lines.sizes[k] for k in ("z", "core", "section"))
    dp = group * ring
    many = len(shards)
    local = weight.shape[0] // dp
    wide = weight.shape[1]
    weight = weight.reshape(dp, local, wide)
    width = vectors.shape[1]

    def kernel(x_ref, w_ref, *refs):
        s_refs, refs = refs[:many], refs[many:]
        v_ref, wo_ref, refs = refs[0], refs[1], refs[2:]
        so_refs, refs = refs[:many], refs[many:]
        send, recv, w_got, w_turn, w_all, w_own, v_z, v_core, v_all = refs
        copies = Copies(lines, send, recv)
        zplace, place, section = (lines.place(k) for k in ("z", "core", "section"))
        copies.greet(["z", "core", "section"])
        order = lines.peers("z") + [zplace]
        around = [
            copies.swap("core", lambda peer: w_ref.at[g * ring + peer], lambda me: w_got.at[me, g]) for g in order
        ]
        pending = copies.swap("z", lambda peer: x_ref, lambda me: v_z.at[me])
        v_z[zplace] = x_ref[...]
        gathers = [SquareGather(copies, x, o) for x, o in zip(s_refs, so_refs)]
        for gather in gathers:
            gather.start()
        along = []
        for i, (g, arrived) in enumerate(zip(order, around)):
            for copy in arrived:
                copy.wait_recv()
            total = w_ref[g * ring + place].astype(F32)
            for peer in lines.peers("core"):
                total = total + w_got[peer, g].astype(F32)
            w_turn[g] = total.astype(BF)
            if i < len(order) - 1:
                along.append(copies.start("z", g, w_turn.at[g], w_all.at[zplace]))
        wait(pending)
        v_core[place] = sum_places(v_z)
        wait(copies.swap("core", lambda peer: v_core.at[place], lambda me: v_core.at[me]))
        v_all[section] = sum_places(v_core)
        pending = copies.swap("section", lambda peer: v_all.at[section], lambda me: v_all.at[me])
        for gather in gathers:
            gather.forward()
        wait(along)
        w_all[zplace] = w_turn[zplace]
        w_own[...] = sum_places(w_all).astype(BF)
        last_gather = SquareGather(copies, w_own, wo_ref)
        last_gather.start()
        wait(pending)
        for i in range(sections):
            v_ref[:, i * width : (i + 1) * width] = v_all[i]
        last_gather.forward()
        for arrived in around:
            for copy in arrived:
                copy.wait_send()
        for gather in gathers:
            gather.finish()
        last_gather.finish()

    z, c, s = group - 1, ring - 1, sections - 1
    result = communicate(
        kernel,
        ident,
        [vectors, weight] + shards,
        [((8, sections * width), F32), ((local, sections * wide), BF)]
        + [((x.shape[0], sections * x.shape[1]), x.dtype) for x in shards],
        semaphores(
            group * c
            + z
            + sum(SquareGather.count(x.shape[0]) for x in shards)
            + SquareGather.count(local)
            + z
            + c
            + s
        )
        + [
            pltpu.VMEM((ring, group, local, wide), BF),
            pltpu.VMEM((group, local, wide), BF),
            pltpu.VMEM((group, local, wide), BF),
            pltpu.VMEM((local, wide), BF),
            pltpu.VMEM((group, 8, width), F32),
            pltpu.VMEM((ring, 8, width), F32),
            pltpu.VMEM((sections, 8, width), F32),
        ],
        name,
        limit=32 * 2**20,
    )
    return result[0], result[1], result[2:]


def assemble(pieces, share, name):
    arrays = []
    for _, array, _, _ in pieces:
        if not any(array is other for other in arrays):
            arrays.append(array)
    where = [next(i for i, other in enumerate(arrays) if other is array) for _, array, _, _ in pieces]
    local = arrays[0].shape[0]
    steps = local // 32 if local % 32 == 0 else 1
    rows = local // steps
    sections = lax.axis_size("section")
    shapes, specs = [], []
    for kind, _, _, width in pieces:
        many = 2 if kind == "pair" else 1
        for _ in range(many):
            if kind == "stack":
                shapes.append(jax.ShapeDtypeStruct((sections, local, width), F32))
                specs.append(pl.BlockSpec((sections, rows, width), lambda i: (0, i, 0)))
            else:
                total = width if kind == "sum" else sections * width // many
                shapes.append(jax.ShapeDtypeStruct((local, total), F32))
                specs.append(pl.BlockSpec((rows, total), lambda i: (i, 0)))

    def kernel(*refs):
        ins, outs = refs[: len(arrays)], list(refs[len(arrays) :])
        for (kind, array, first, width), i in zip(pieces, where):
            wide = array.shape[1] // sections
            blocks = [ins[i][:, s * wide + first : s * wide + first + width].astype(F32) for s in range(sections)]
            out = outs.pop(0)
            if kind == "columns":
                for s, item in enumerate(blocks):
                    out[:, s * width : (s + 1) * width] = item
            elif kind == "stack":
                for s, item in enumerate(blocks):
                    out[s] = item
            elif kind == "sum":
                total = blocks[0]
                for item in blocks[1:]:
                    total = total + item
                out[...] = total
            elif kind == "hidden":
                for d in range(width // share):
                    out[:, d * share * sections : (d + 1) * share * sections] = jnp.concatenate(
                        [item[:, d * share : (d + 1) * share] for item in blocks], axis=1
                    )
            else:
                other = outs.pop(0)
                half = width // 2
                for s, item in enumerate(blocks):
                    for side, dst in ((0, out), (1, other)):
                        heads = [
                            item[:, (2 * g + side) * HDIM : (2 * g + side + 1) * HDIM]
                            for g in range(width // (2 * HDIM))
                        ]
                        dst[:, s * half : (s + 1) * half] = jnp.concatenate(heads, axis=1)

    return pl.pallas_call(
        kernel,
        grid=(steps,),
        in_specs=[pl.BlockSpec((rows, a.shape[1]), lambda i: (i, 0)) for a in arrays],
        out_specs=specs,
        out_shape=shapes,
        compiler_params=pltpu.CompilerParams(vmem_limit_bytes=24 * 2**20),
        name=name,
    )(*arrays)


def column_to_rows(column):
    return jnp.broadcast_to(column, (column.shape[0], 128)).T[:8]


def row_to_column(row):
    return jnp.broadcast_to(row, (128, row.shape[1])).T[:, :1]


def outer_product(left_ref, right_ref, out_ref, first):
    step = 256
    wide = right_ref.shape[1]
    for i in range(left_ref.shape[1] // step):
        block = contract(left_ref[:, i * step : (i + 1) * step], right_ref[...], 0, 0)
        out_ref[i * step : (i + 1) * step, first : first + wide] = block.astype(BF)


def unpack_low(packed):
    lane = lax.broadcasted_iota(jnp.int32, packed.shape, 1)
    zero = jnp.zeros_like(packed)
    low = jnp.where(lane < HDIM, packed, zero)
    turned = jnp.concatenate([packed[:, HDIM:], packed[:, :HDIM]], axis=1)
    high = jnp.where(lane < HDIM, turned, zero)
    return jnp.concatenate([low, high], axis=0)


def unpack_high(packed):
    lane = lax.broadcasted_iota(jnp.int32, packed.shape, 1)
    zero = jnp.zeros_like(packed)
    turned = jnp.concatenate([packed[:, HDIM:], packed[:, :HDIM]], axis=1)
    low = jnp.where(lane >= HDIM, turned, zero)
    high = jnp.where(lane >= HDIM, packed, zero)
    return jnp.concatenate([low, high], axis=0)


def pack_turned(turned):
    half = turned.shape[1] // 2
    return jnp.concatenate([turned[:, :half], turned[:, half:]], axis=0).T


def forward_block(query, pieces, qpos, start, causal):
    scores = []
    peak = None
    for index, (pair, _, first) in enumerate(pieces):
        item = contract(pair, query, 1, 1)
        kpos = first + lax.broadcasted_iota(jnp.int32, item.shape, 0)
        allowed = kpos >= start
        if causal[index]:
            allowed = allowed & (kpos <= qpos)
        item = jnp.where(allowed, item, NEG)
        top = jnp.max(item, axis=0, keepdims=True)
        peak = top if peak is None else jnp.maximum(peak, top)
        scores.append(item)
    total = jnp.zeros_like(peak)
    mixed = None
    for item, (_, turned, _) in zip(scores, pieces):
        weight = jnp.exp(item - peak)
        total = total + jnp.sum(weight, axis=0, keepdims=True)
        part = matmul(turned[HDIM:], weight.astype(BF))
        mixed = part if mixed is None else mixed + part
    return mixed / total, peak + jnp.log(total)


def backward_block(query, grad, grad_turned, mixed_turned, lse, pieces, qpos, start, causal):
    row_sum = jnp.sum(grad_turned.astype(F32) * mixed_turned.astype(F32), axis=0, keepdims=True)
    grad_query = None
    grads = []
    for index, (pair, turned, first) in enumerate(pieces):
        scores = contract(pair, query, 1, 1)
        kpos = first + lax.broadcasted_iota(jnp.int32, scores.shape, 0)
        allowed = kpos >= start
        if causal[index]:
            allowed = allowed & (kpos <= qpos)
        probs = jnp.where(allowed, jnp.exp(scores - lse), 0.0)
        grad_probs = contract(pair, grad, 1, 1)
        grad_scores = (probs * (grad_probs - row_sum)).astype(BF)
        grads.append(matmul(grad_scores, query) + matmul(probs.astype(BF), grad))
        part = matmul(turned[:HDIM], grad_scores)
        grad_query = part if grad_query is None else grad_query + part
    return grad_query * SCALE, grads


def dense_forward_kernel(place_ref, q_ref, kv_ref, start_ref, out_ref, turned_ref, lse_ref):
    group, _, half, _ = q_ref.shape
    ring, _, _, block, _ = kv_ref.shape
    place = place_ref[0]
    span = ring * block
    pieces = []
    for g in range(group):
        pair = kv_ref[:, g, 0].reshape(span, 2 * HDIM)
        pieces.append((pair, pair.T, g * span))
    for g in range(group):
        query = unpack_low(q_ref[g, 0]) * jnp.asarray(SCALE, BF)
        qpos = g * span + place * block + lax.broadcasted_iota(jnp.int32, (1, block), 1)
        mixed, lse = forward_block(
            query, pieces[: g + 1], qpos, start_ref[0, g], [i == g for i in range(g + 1)]
        )
        turned_ref[0, g] = mixed.astype(BF)
        lse_ref[0, g] = lse
        out_ref[g, 0] = pack_turned(mixed).astype(BF)


def dense_forward(place, q, kv, start):
    group, seqs, half, lanes = q.shape
    ring, _, _, block, _ = kv.shape
    grid = pltpu.PrefetchScalarGridSpec(
        num_scalar_prefetch=1,
        grid=(seqs,),
        in_specs=[
            pl.BlockSpec((group, 1, half, lanes), lambda s, _: (0, s, 0, 0)),
            pl.BlockSpec((ring, group, 1, block, lanes), lambda s, _: (0, 0, s, 0, 0)),
            pl.BlockSpec((1, group, 1, block), lambda s, _: (s, 0, 0, 0)),
        ],
        out_specs=[
            pl.BlockSpec((group, 1, half, lanes), lambda s, _: (0, s, 0, 0)),
            pl.BlockSpec((1, group, HDIM, block), lambda s, _: (s, 0, 0, 0)),
            pl.BlockSpec((1, group, 1, block), lambda s, _: (s, 0, 0, 0)),
        ],
    )
    return pl.pallas_call(
        dense_forward_kernel,
        grid_spec=grid,
        out_shape=[
            jax.ShapeDtypeStruct(q.shape, BF),
            jax.ShapeDtypeStruct((seqs, group, HDIM, block), BF),
            jax.ShapeDtypeStruct((seqs, group, 1, block), F32),
        ],
        compiler_params=pltpu.CompilerParams(vmem_limit_bytes=VMEM),
        name="dense_attention",
    )(place, q, kv, start)


def dense_return(lines, ident, arrays, shape, name):
    seqs, rows, width, hidden_size = shape
    sections, group, ring = (lines.sizes[k] for k in ("section", "z", "core"))
    part = width // sections
    half = rows // 2
    lanes = 2 * HDIM
    block = ring * rows

    def kernel(
        fed_ref,
        own_ref,
        value_ref,
        attended_ref,
        slope_ref,
        hidden_ref,
        mixed_ref,
        rest_ref,
        qkv_w,
        q_ref,
        kv_ref,
        start_ref,
        turned_ref,
        lse_ref,
        gains_ref,
        grads_ref,
        dqkv_w_ref,
        stream_ref,
        vectors_ref,
        send,
        recv,
        normed,
        dpre,
        dattended,
        dqkv,
        wide,
        got,
        turn,
        last,
        scalar,
        scalar_got,
        middle,
        total,
        heads,
        heads_got,
        acc,
        pairs,
        pairs_got,
        queries,
        queries_got,
        sums,
        sums_got,
        kv,
        local,
    ):
        copies = Copies(lines, send, recv)
        section, zplace, place = (lines.place(k) for k in ("section", "z", "core"))
        own = span(section, part)
        copies.greet(["section", "z", "core"])
        out_w = rest_ref.at[:, :part]
        expand_w = rest_ref.at[:, part : part + hidden_size]
        shrink_w = rest_ref.at[:, part + hidden_size :]
        scatters = {}

        def begin(stage, q, value, scalars):
            wide[stage, q] = value.astype(BF)
            item = SquareScatter(
                copies, wide.at[stage, q], got.at[stage, q], turn.at[stage, q], last.at[stage, q], 1
            )
            item.start()
            others = []
            if scalars is not None:
                side = min(stage, 1)
                scalar[side, q] = column_to_rows(scalars)
                others = copies.swap(
                    "section", lambda peer: scalar.at[side, q], lambda me: scalar_got.at[side, q, me]
                )
                scalar_got[side, q, section] = scalar[side, q]
            scatters[stage, q] = (item, others)

        def forward(stage, q):
            scatters[stage, q][0].forward()

        def finish(stage, q):
            item, others = scatters[stage, q]
            item.finish(total)
            if not others:
                return total[...], None
            wait(others)
            return total[...], row_to_column(sum_places(scalar_got.at[min(stage, 1), q])[:1])

        def middle_of(q):
            at = pl.ds(q * rows, rows)
            return value_ref[at].astype(F32) + attended_ref[at].astype(F32)

        def feed(q):
            at = pl.ds(q * rows, rows)
            grad_pre = (contract(fed_ref[at], shrink_w[...], 1, 1) * slope_ref[at].astype(F32)).astype(BF)
            dpre[at] = grad_pre
            grad_normed = contract(grad_pre, expand_w[...], 1, 1)
            weighted = middle_of(q) * gains_ref[1:2]
            begin(0, q, grad_normed, jnp.sum(grad_normed * weighted, axis=1, keepdims=True))

        def project(q):
            at = pl.ds(q * rows, rows)
            grad_normed, scalars = finish(0, q)
            mid = middle_of(q)
            inv = inverse_rms(mid)
            normed[at] = (mid * inv * gains_ref[1:2]).astype(BF)
            mid = value_ref[at, own].astype(F32) + attended_ref[at, own].astype(F32)
            vectors_ref[0:1] += jnp.sum(grad_normed * mid * inv, axis=0, keepdims=True)
            grad = (
                inv * (grad_normed * gains_ref[1:2, own])
                - mid * (inv * inv * inv) * (scalars * (1.0 / width))
                + own_ref[at]
            )
            middle[q] = grad
            low = grad.astype(BF)
            dattended[at] = low
            begin(1, q, contract(low, out_w[...], 1, 1), None)

        def to_heads(q):
            grad, _ = finish(1, q)
            grad = grad.astype(BF)
            for g in range(group):
                columns = slice(g * HDIM, (g + 1) * HDIM)
                heads[g, q] = side_by_side([grad[:half, columns], grad[half:, columns]])
            heads_got[zplace, q] = heads[zplace, q]
            return copies.swap("z", lambda peer: heads.at[peer, q], lambda me: heads_got.at[me, q])

        def fetch(q):
            return pltpu.make_async_copy(kv_ref.at[:, :, q], kv, local.at[q])

        def load(src, index):
            copy = pltpu.make_async_copy(src, dpre, local.at[index])
            copy.start()
            copy.wait()

        def attend(q):
            fetch(q).wait()
            pieces = []
            for g in range(group):
                pair = kv[:, g].reshape(block, lanes)
                pieces.append((pair, pair.T, g * block))
            for g in reversed(range(group)):
                query = unpack_low(q_ref[g, q]) * jnp.asarray(SCALE, BF)
                packed = heads_got[g, q]
                flat = packed.T
                qpos = g * block + place * rows + lax.broadcasted_iota(jnp.int32, (1, rows), 1)
                grad_query, grads = backward_block(
                    query,
                    unpack_high(packed),
                    side_by_side([flat[:HDIM], flat[HDIM:]]),
                    turned_ref[q, g],
                    lse_ref[q, g],
                    pieces[: g + 1],
                    qpos,
                    start_ref[q, g],
                    [i == g for i in range(g + 1)],
                )
                queries[g, q] = pack_turned(grad_query).astype(BF)
                for i, item in enumerate(grads):
                    if g == group - 1:
                        acc[i] = item
                    else:
                        acc[i] += item
            for g in range(group):
                for r in range(ring):
                    pairs[r, g] = acc[g, r * rows : (r + 1) * rows].astype(BF)
            if q + 1 < seqs:
                fetch(q + 1).start()
            queries_got[zplace, q] = queries[zplace, q]
            around = copies.swap("core", lambda peer: pairs.at[peer], lambda me: pairs_got.at[me, :, q])
            along = copies.swap("z", lambda peer: queries.at[peer, q], lambda me: queries_got.at[me, q])
            return around, along

        def to_tokens(q, around):
            wait(around)
            for g in range(group):
                item = pairs[place, g].astype(F32)
                for peer in lines.peers("core"):
                    item = item + pairs_got[peer, g, q].astype(F32)
                sums[g, q] = item.astype(BF)
            sums_got[zplace, q] = sums[zplace, q]
            return copies.swap("z", lambda peer: sums.at[peer, q], lambda me: sums_got.at[me, q])

        def enter(q, pending):
            wait(pending)
            at = pl.ds(q * rows, rows)
            packed = [queries_got[g, q] for g in range(group)]
            upright = [jnp.concatenate([p[:, :HDIM], p[:, HDIM:]], axis=0) for p in packed]
            grad = side_by_side([sums_got[g, q] for g in range(group)] + upright)
            dqkv[at] = grad
            grad_normed = contract(grad, qkv_w[...], 1, 1)
            value = value_ref[at].astype(F32)
            normed[at] = (value * inverse_rms(value) * gains_ref[0:1]).astype(BF)
            begin(2, q, grad_normed, jnp.sum(grad_normed * value * gains_ref[0:1], axis=1, keepdims=True))

        def leave(q):
            at = pl.ds(q * rows, rows)
            grad_normed, scalars = finish(2, q)
            inv = inverse_rms(value_ref[at].astype(F32))
            value = value_ref[at, own].astype(F32)
            vectors_ref[1:2] += jnp.sum(grad_normed * value * inv, axis=0, keepdims=True)
            grad = (
                inv * (grad_normed * gains_ref[0:1, own])
                - value * (inv * inv * inv) * (scalars * (1.0 / width))
                + middle[q]
            )
            stream_ref[at] = grad.astype(BF)

        vectors_ref[...] = jnp.zeros_like(vectors_ref)
        arriving, around, along, leaving = {}, {}, {}, {}
        fetch(0).start()

        def turn_back(q):
            wait(arriving[q])
            around[q], along[q] = attend(q)

        def hand_back(q):
            leaving[q] = to_tokens(q, around[q]) + along[q]

        def step(name, q):
            if q < 0 or q >= seqs:
                return
            if name == "heads":
                arriving[q] = to_heads(q)
            elif name == "enter":
                enter(q, leaving[q])
            elif name in ("mid", "out", "in"):
                forward(("mid", "out", "in").index(name), q)
            else:
                {"feed": feed, "project": project, "attend": turn_back, "back": hand_back, "leave": leave}[name](q)

        last_of = seqs - 1
        for q in range(seqs):
            step("feed", q)
            step("mid", q - 1)
            step("project", q - 2)
        step("mid", last_of)
        step("project", last_of - 1)
        step("out", 0)
        step("heads", 0)
        step("project", last_of)
        for q in range(1, seqs):
            step("out", q)
            step("heads", q)
            step("attend", q - 1)
            step("back", q - 1)
        outer_product(normed, dpre, grads_ref, 0)
        step("attend", last_of)
        step("back", last_of)
        load(hidden_ref, seqs)
        outer_product(dpre, fed_ref, grads_ref, hidden_size)
        load(mixed_ref, seqs + 1)
        outer_product(dpre, dattended, grads_ref, hidden_size + width)
        for q in range(seqs):
            step("enter", q)
            step("in", q - 1)
            step("leave", q - 2)
        outer_product(normed, dqkv, dqkv_w_ref, 0)
        step("in", last_of)
        step("leave", last_of - 1)
        step("leave", last_of)

    tokens = seqs * rows
    z, c, s = group - 1, ring - 1, sections - 1
    vmem = pltpu.VMEM
    return communicate(
        kernel,
        ident,
        arrays,
        [
            ((width, hidden_size + width + part), BF),
            ((width, 3 * part), BF),
            ((tokens, part), BF),
            ((8, part), F32),
        ],
        semaphores(seqs * (3 * 6 + 2 * s + 3 * z + c))
        + [
            vmem((tokens, width), BF),
            vmem((tokens, hidden_size), BF),
            vmem((tokens, part), BF),
            vmem((tokens, 3 * part), BF),
            vmem((3, seqs, rows, width), BF),
            vmem((3, seqs, 2, rows, part), BF),
            vmem((3, seqs, rows, part), BF),
            vmem((3, seqs, rows, part), BF),
            vmem((2, seqs, 8, rows), F32),
            vmem((2, seqs, sections, 8, rows), F32),
            vmem((seqs, rows, part), F32),
            vmem((rows, part), F32),
            vmem((group, seqs, half, lanes), BF),
            vmem((group, seqs, half, lanes), BF),
            vmem((group, block, lanes), F32),
            vmem((ring, group, rows, lanes), BF),
            vmem((ring, group, seqs, rows, lanes), BF),
            vmem((group, seqs, half, lanes), BF),
            vmem((group, seqs, half, lanes), BF),
            vmem((group, seqs, rows, lanes), BF),
            vmem((group, seqs, rows, lanes), BF),
            vmem((ring, group, rows, lanes), BF),
            pltpu.SemaphoreType.DMA((seqs + 2,)),
        ],
        name,
        limit=62 * 2**20,
        far=(5, 6, 10),
    )


def inverse_rms(value):
    return lax.rsqrt(jnp.mean(value * value, axis=-1, keepdims=True) + EPS)


def gelu_terms(value):
    scale = 0.7978845608028654
    square = value * value
    bend = jnp.tanh(scale * (value + 0.044715 * square * value))
    half = 0.5 * (1.0 + bend)
    slope = half + 0.5 * value * (1.0 - bend * bend) * scale * (1.0 + 0.134145 * square)
    return value * half, slope


def side_by_side(blocks):
    return jnp.concatenate(blocks, axis=1)


class ColumnSum:
    @staticmethod
    def count(sections, scalars):
        return (sections - 1) * (2 if scalars else 1)

    @staticmethod
    def scratch(sections, rows, width, scalars):
        buffers = [pltpu.VMEM((rows, sections * width), BF), pltpu.VMEM((sections, rows, width), BF)]
        if scalars:
            wide = rows + -rows % 128
            buffers += [pltpu.VMEM((8, wide), F32), pltpu.VMEM((sections, 8, wide), F32)]
        return buffers

    def __init__(self, copies, buffers):
        self.copies, self.buffers = copies, buffers

    def start(self, value, scalars=None):
        buf, got = self.buffers[:2]
        width = got.shape[2]
        section = self.copies.lines.place("section")
        buf[...] = value.astype(BF)
        self.pending = self.copies.swap(
            "section", lambda peer: buf.at[:, span(peer, width)], lambda me: got.at[me]
        )
        got[section] = buf[:, span(section, width)]
        if scalars is not None:
            sbuf, sgot = self.buffers[2:]
            sbuf[...] = jnp.zeros_like(sbuf)
            sbuf[:, : scalars.shape[0]] = column_to_rows(scalars)
            self.pending += self.copies.swap("section", lambda peer: sbuf, lambda me: sgot.at[me])
            sgot[section] = sbuf[...]

    def finish(self):
        wait(self.pending)
        total = sum_places(self.buffers[1])
        if len(self.buffers) == 2:
            return total
        rows = total.shape[0]
        return total, row_to_column(sum_places(self.buffers[3])[:1, :rows])


def routed_layer(lines, ident, arrays, shape, name):
    seqs, sel, rows, width, part = shape
    sections, group, ring = (lines.sizes[k] for k in ("section", "z", "core"))
    dp = group * ring
    slots = seqs * sel
    lanes = 2 * HDIM
    rest_w = arrays[-1]
    hidden_size = rest_w.shape[1] - part - width
    qkv_at = hidden_size + width
    vector_at = qkv_at + 4 * part

    def kernel(
        source_ref,
        top_ref,
        column_ref,
        row_ref,
        start_ref,
        gains_ref,
        qkv_w,
        rest_ref,
        fed_out,
        own_out,
        added_ref,
        grads_ref,
        send,
        recv,
        value_core,
        value_core_got,
        value_z,
        value_z_got,
        value_all,
        grad_core,
        grad_core_got,
        grad_z,
        grad_z_got,
        grad_all,
        heads_buf,
        heads_got,
        pairs_all,
        out_buf,
        out_got,
        mixed_all,
        attended_all,
        grad_buf,
        grad_got,
        turn_buf,
        turn_got,
        back_buf,
        back_got,
        keep,
        normed_keep,
        mixed_keep,
        mid_keep,
        dpre_keep,
        hidden_keep,
        fed_keep,
        attended_keep,
        dqkv_keep,
        sent_buf,
        sent_got,
        sent_all,
        final_buf,
        final_got,
        final_all,
        *buffers,
    ):
        copies = Copies(lines, send, recv)
        section, zplace, place = (lines.place(k) for k in ("section", "z", "core"))
        rank = lax.axis_index("dp")
        copies.greet(["section", "z", "core"])
        own = span(section, part)
        gain_pre, gain_mid, router = (gains_ref[i : i + 1, :] for i in range(3))
        own_pre, own_mid, own_router = (gains_ref[i : i + 1, own] for i in range(3))
        out_w = rest_ref.at[:, :part]
        expand_w = rest_ref.at[:, part : part + hidden_size]
        shrink_w = rest_ref.at[:, part + hidden_size :]
        sums = [ColumnSum(copies, buffers[4 * i : 4 * i + 4]) for i in range(3)]
        sums.append(ColumnSum(copies, buffers[12:14]))

        def ring_swap(buf, got):
            return copies.swap("core", lambda peer: buf.at[peer], lambda me: got.at[me])

        def ring_sum(buf, got):
            total = buf[place].astype(F32)
            for peer in lines.peers("core"):
                total = total + got[peer].astype(F32)
            return total.astype(BF)

        def z_swap(buf, got):
            pending = copies.swap("z", lambda peer: buf.at[peer], lambda me: got.at[me])
            got[zplace] = buf[zplace]
            return pending

        def share(kind, all_ref):
            me = lines.place(kind)
            return copies.swap(kind, lambda peer: all_ref.at[me], lambda _: all_ref.at[me])

        def together(all_ref):
            return side_by_side([all_ref[i] for i in range(sections)])

        position = rank * rows + lax.broadcasted_iota(jnp.int32, (1, rows), 1)
        for q in range(seqs):
            table = (column_ref[q] == position).astype(F32).astype(BF)
            found = matmul(table, source_ref[q]).astype(BF)
            for d in range(dp):
                at = slice(q * sel, (q + 1) * sel)
                value_core[d % ring, d // ring, at] = found[d * sel : (d + 1) * sel, :part]
                grad_core[d % ring, d // ring, at] = found[d * sel : (d + 1) * sel, part:]
        pending = ring_swap(value_core, value_core_got)
        grad_pending = ring_swap(grad_core, grad_core_got)
        wait(pending)
        value_z[...] = ring_sum(value_core, value_core_got)
        pending = z_swap(value_z, value_z_got)
        wait(grad_pending)
        grad_z[...] = ring_sum(grad_core, grad_core_got)
        wait(pending)
        value_all[section] = sum_places(value_z_got).astype(BF)
        pending = share("section", value_all)
        grad_pending = z_swap(grad_z, grad_z_got)
        wait(pending)
        picked = together(value_all).astype(F32)

        inv_in = inverse_rms(picked)
        normed = (picked * inv_in * gain_pre).astype(BF)
        normed_keep[...] = normed
        qkv = matmul(normed, qkv_w[...]).astype(BF)
        blank = jnp.zeros((slots, HDIM), BF)
        for g in range(group):
            query = qkv[:, 2 * part + g * HDIM : 2 * part + (g + 1) * HDIM]
            heads_buf[g, :, :lanes] = side_by_side([query, blank])
            heads_buf[g, :, lanes:] = qkv[:, g * lanes : (g + 1) * lanes]
        pending = z_swap(heads_buf, heads_got)
        wait(grad_pending)
        grad_all[section] = sum_places(grad_z_got).astype(BF)
        grad_pending = share("section", grad_all)
        wait(pending)
        pairs_all[place] = heads_got[:, :, lanes:]
        wait(share("core", pairs_all))

        index = lax.broadcasted_iota(jnp.int32, (1, group * sel), 1)
        place_of = (index // sel) * (ring * sel) + place * sel + lax.rem(index, sel)

        def sequence(q):
            at = slice(q * sel, (q + 1) * sel)
            query = jnp.concatenate([heads_got[g, at, :lanes] for g in range(group)], axis=0)
            pair = jnp.concatenate([pairs_all[r, g, at] for g in range(group) for r in range(ring)], axis=0)
            return query * jnp.asarray(SCALE, BF), pair

        kept = []
        for q in range(seqs):
            query, pair = sequence(q)
            turned, lse = forward_block(query, [(pair, pair.T, 0)], place_of, start_ref[q], [True])
            kept.append((turned.astype(BF), lse))
            upright = jnp.concatenate([turned, jnp.zeros_like(turned)], axis=0).T.astype(BF)
            for g in range(group):
                out_buf[g, q * sel : (q + 1) * sel] = upright[g * sel : (g + 1) * sel]
        wait(z_swap(out_buf, out_got))
        mixed_all[section] = side_by_side([out_got[g, :, :HDIM] for g in range(group)])
        wait(share("section", mixed_all))
        mixed_keep[...] = together(mixed_all)
        attended_own = matmul(mixed_keep[...], out_w[...]).astype(BF)
        attended_all[section] = attended_own
        pending = share("section", attended_all)
        wait(grad_pending)
        grad_sent = together(grad_all).astype(F32)
        gate = jax.nn.sigmoid(jnp.sum(picked * router, axis=1, keepdims=True))
        grad_delta = gate * grad_sent
        fed_low = grad_delta.astype(BF)
        fed_keep[...] = fed_low
        grad_hidden = contract(fed_low, shrink_w[...], 1, 1)
        wait(pending)

        middle = picked + together(attended_all).astype(F32)
        inv_mid = inverse_rms(middle)
        normed_mid = (middle * inv_mid * gain_mid).astype(BF)
        hidden, slope = gelu_terms(matmul(normed_mid, expand_w[...]))
        hidden = hidden.astype(BF)
        grad_pre = (grad_hidden * slope).astype(BF)
        grad_normed = contract(grad_pre, expand_w[...], 1, 1)
        sums[0].start(grad_normed, jnp.sum(grad_normed * middle * gain_mid, axis=1, keepdims=True))
        mid_keep[...] = normed_mid
        hidden_keep[...] = hidden
        dpre_keep[...] = grad_pre
        fed_part = matmul(hidden, shrink_w[...])
        keep[0] = middle
        keep[1] = grad_delta
        keep[2] = grad_sent
        own_attended = attended_own.astype(F32)
        gate_part = jnp.sum(grad_sent * fed_part, axis=1, keepdims=True) + jnp.sum(
            keep[2, :, own] * own_attended, axis=1, keepdims=True
        )
        middle_own, grad_delta_own = keep[0, :, own], keep[1, :, own]
        picked_own = value_all[section].astype(F32)
        grad_normed, scalar = sums[0].finish()
        vector_mid = jnp.sum(grad_normed * middle_own * inv_mid, axis=0, keepdims=True)
        grad_middle = inv_mid * (grad_normed * own_mid) - middle_own * (inv_mid * inv_mid * inv_mid) * (
            scalar * (1.0 / width)
        )
        grad_attended = (grad_middle + grad_delta_own).astype(BF)
        attended_keep[...] = grad_attended

        sums[3].start(contract(grad_attended, out_w[...], 1, 1))
        sums[1].start(fed_part, gate_part)
        outer_product(mid_keep, dpre_keep, grads_ref, 0)
        grad_mixed = sums[3].finish().astype(BF)
        for g in range(group):
            grad_buf[g] = side_by_side([blank, grad_mixed[:, g * HDIM : (g + 1) * HDIM]])
        pending = z_swap(grad_buf, grad_got)
        fed, grad_gate = sums[1].finish()
        sent_buf[...] = (gate * (own_attended + fed)).astype(BF)
        grad_logit = grad_gate * gate * (1.0 - gate)
        vector_router = jnp.sum(grad_logit * picked_own, axis=0, keepdims=True)
        wait(pending)
        sent_pending = copies.swap("z", lambda peer: sent_buf, lambda me: sent_got.at[me])
        sent_got[zplace] = sent_buf[...]
        for q in range(seqs):
            at = slice(q * sel, (q + 1) * sel)
            query, pair = sequence(q)
            grad = jnp.concatenate([grad_got[g, at] for g in range(group)], axis=0)
            turned, lse = kept[q]
            grad_query, grad_pairs = backward_block(
                query, grad, grad.T[HDIM:], turned, lse, [(pair, pair.T, 0)], place_of, start_ref[q], [True]
            )
            upright = jnp.concatenate([grad_query, jnp.zeros_like(grad_query)], axis=0).T.astype(BF)
            low = grad_pairs[0].astype(BF)
            for g in range(group):
                back_buf[g, at, :lanes] = upright[g * sel : (g + 1) * sel]
                for r in range(ring):
                    first = (g * ring + r) * sel
                    turn_buf[r, g, at] = low[first : first + sel]
        wait(ring_swap(turn_buf, turn_got))
        back_buf[:, :, lanes:] = ring_sum(turn_buf, turn_got)
        pending = z_swap(back_buf, back_got)
        wait(sent_pending)
        sent_all[place] = sent_got[...]
        sent_pending = share("core", sent_all)
        outer_product(hidden_keep, fed_keep, grads_ref, hidden_size)
        wait(pending)
        dqkv_keep[...] = side_by_side(
            [back_got[g, :, lanes:] for g in range(group)] + [back_got[g, :, :HDIM] for g in range(group)]
        )
        grad_normed = contract(dqkv_keep[...], qkv_w[...], 1, 1)
        sums[2].start(grad_normed, jnp.sum(grad_normed * picked * gain_pre, axis=1, keepdims=True))
        outer_product(normed_keep, dqkv_keep, grads_ref, qkv_at)
        grad_normed, scalar = sums[2].finish()
        vector_pre = jnp.sum(grad_normed * picked_own * inv_in, axis=0, keepdims=True)
        grad_in = inv_in * (grad_normed * own_pre) - picked_own * (inv_in * inv_in * inv_in) * (
            scalar * (1.0 / width)
        )
        final_buf[...] = (grad_middle + grad_in + grad_logit * own_router).astype(BF)

        along = copies.swap("z", lambda peer: final_buf, lambda me: final_got.at[me])
        final_got[zplace] = final_buf[...]

        def hand_on(i):
            dst = final_all.at[place, i, :, own]
            dst[...] = final_got[i]
            return copies.swap("section", lambda peer: final_got.at[i], lambda me: dst)

        spread = hand_on(zplace)
        outer_product(mixed_keep, attended_keep, grads_ref, qkv_at + 3 * part)
        lane = lax.broadcasted_iota(jnp.int32, (part, 128), 1)
        vectors = jnp.zeros((part, 128), F32)
        for i, vector in enumerate((vector_pre, vector_mid, vector_router)):
            vectors = jnp.where(lane == i, row_to_column(vector), vectors)
        grads_ref[:, vector_at:] = jnp.zeros((width, 128), BF)
        grads_ref[pl.ds(pl.multiple_of(section * part, part), part), vector_at:] = vectors.astype(BF)
        wait(sent_pending)
        slot_of = rank * rows + lax.broadcasted_iota(jnp.int32, (rows, 1), 0)
        tables = [(row_ref[q] == slot_of).astype(F32).astype(BF) for q in range(seqs)]

        def at_positions(q, all_ref):
            at = slice(q * sel, (q + 1) * sel)
            found = jnp.concatenate([all_ref[r, g, at] for g in range(group) for r in range(ring)], axis=0)
            return matmul(tables[q], found)

        for q in range(seqs):
            added_ref[q] = at_positions(q, sent_all).astype(BF)
        for step in range(group - 1, 0, -1):
            along[group - 1 - step].wait_recv()
            spread += hand_on(lax.rem(zplace + step, group))
        for copy in along:
            copy.wait_send()
        wait(spread)
        wait(share("core", final_all))
        for q in range(seqs):
            grad = top_ref[q].astype(F32) + at_positions(q, final_all)
            fed_out[q] = grad.astype(BF)
            returned = jnp.concatenate(
                [final_all[r, g, q * sel : (q + 1) * sel, own] for g in range(group) for r in range(ring)], axis=0
            )
            own_out[q] = top_ref[q, :, own].astype(F32) + matmul(tables[q], returned)

    vmem = pltpu.VMEM
    z, s, c = group - 1, sections - 1, ring - 1
    short = ((group, slots, part), BF)
    lane_block = ((group, slots, lanes), BF)
    ring_block = ((ring, group, slots, lanes), BF)
    row = ((slots, width), BF)
    scratch = [
        ((ring,) + short[0], BF),
        ((ring,) + short[0], BF),
        short,
        short,
        ((sections, slots, part), BF),
        ((ring,) + short[0], BF),
        ((ring,) + short[0], BF),
        short,
        short,
        ((sections, slots, part), BF),
        ((group, slots, 2 * lanes), BF),
        ((group, slots, 2 * lanes), BF),
        ring_block,
        lane_block,
        lane_block,
        ((sections, slots, part), BF),
        ((sections, slots, part), BF),
        lane_block,
        lane_block,
        ring_block,
        ring_block,
        ((group, slots, 2 * lanes), BF),
        ((group, slots, 2 * lanes), BF),
        ((3, slots, width), F32),
        row,
        row,
        row,
        ((slots, hidden_size), BF),
        ((slots, hidden_size), BF),
        row,
        ((slots, part), BF),
        ((slots, 3 * part), BF),
        ((slots, part), BF),
        short,
        ((ring,) + short[0], BF),
        ((slots, part), BF),
        short,
        ((ring, group, slots, width), BF),
    ]
    return communicate(
        kernel,
        ident,
        arrays,
        [
            ((seqs, rows, width), BF),
            ((seqs, rows, part), F32),
            ((seqs, rows, part), BF),
            ((width, vector_at + 128), BF),
        ],
        semaphores(
            6 * c
            + 8 * z
            + 4 * s
            + 3 * ColumnSum.count(sections, True)
            + ColumnSum.count(sections, False)
            + group * s
        )
        + [vmem(a, b) for a, b in scratch]
        + 3 * ColumnSum.scratch(sections, slots, part, True)
        + ColumnSum.scratch(sections, slots, part, False),
        name,
        limit=56 * 2**20,
    )


def on_device(
    stream_in,
    segment_ids,
    chosen_rows,
    cotangent,
    dense_prenorm,
    dense_query,
    dense_keys,
    dense_values,
    dense_output,
    dense_midnorm,
    dense_expand,
    dense_shrink,
    routed_prenorm,
    routed_query,
    routed_keys,
    routed_values,
    routed_output,
    routed_midnorm,
    routed_expand,
    routed_shrink,
    router_weight,
):
    sections, dp = lax.axis_size("section"), lax.axis_size("dp")
    section, rank = lax.axis_index("section"), lax.axis_index("dp")
    seqs, rows, width = stream_in.shape
    tokens = seqs * rows
    part = width // sections
    group = HEADS // sections
    ring = dp // group
    total_sel = chosen_rows.shape[1]
    sel = total_sel // dp
    place = lax.rem(rank, ring).astype(jnp.int32).reshape(1)
    lines = Lines(sections, dp, group)
    lanes = 2 * HDIM

    def own_columns(value):
        return lax.dynamic_slice_in_dim(value, section * part, part, value.ndim - 1)

    def own_hidden(expand, shrink):
        inner = expand.shape[1] // dp
        share = inner // sections
        cut = expand.reshape(expand.shape[0], dp, sections, share)
        cut = lax.dynamic_index_in_dim(cut, section, 2, keepdims=False).reshape(expand.shape[0], dp * share)
        return cut, lax.dynamic_slice_in_dim(shrink, section * share, share, 0)

    def own_attention(query, keys, values):
        local = query.shape[0]
        pair = jnp.stack(
            [own_columns(keys).reshape(local, group, HDIM), own_columns(values).reshape(local, group, HDIM)],
            axis=2,
        ).reshape(local, 2 * part)
        return jnp.concatenate([pair, own_columns(query)], axis=1)

    gains = jnp.stack([dense_prenorm, dense_midnorm, routed_prenorm, routed_midnorm, router_weight])
    gains = jnp.pad(gains, ((0, 16 - gains.shape[0]), (0, 0)))
    first = own_attention(dense_query, dense_keys, dense_values)
    dense_qkv, gains = gather_rows(lines, 1, [first, gains], "first_weights")
    dense_qkv = dense_qkv.reshape(width, 3 * part)
    gains = jnp.transpose(gains, (1, 0, 2)).reshape(16, width).astype(F32)
    gain_pre, gain_mid = gains[0], gains[1]

    def gather(value):
        return lax.all_gather(value, "dp", axis=0, tiled=True)

    def after(value, other):
        return lax.optimization_barrier((value, other))[0]

    expand_cut, shrink_cut = own_hidden(dense_expand, dense_shrink)
    hidden_size = expand_cut.shape[1]
    rest = gather(jnp.concatenate([own_columns(dense_output), expand_cut, shrink_cut], axis=1))
    dense_out, dense_exp, dense_shr = (
        rest[:, :part],
        rest[:, part : part + hidden_size],
        rest[:, part + hidden_size :],
    )
    routed_qkv = gather(after(own_attention(routed_query, routed_keys, routed_values), dense_qkv))
    expand_cut, shrink_cut = own_hidden(routed_expand, routed_shrink)
    routed_rest = jnp.concatenate([own_columns(routed_output), expand_cut, shrink_cut], axis=1)

    first_of = jnp.sum(
        (segment_ids[:, None, :] < jnp.arange(DOCS, dtype=jnp.int32)[None, :, None]).astype(jnp.int32), axis=2
    )

    def document(positions):
        shape = (seqs,) + (1,) * (positions.ndim - 1)
        found = jnp.zeros(positions.shape, jnp.int32)
        for c in range(1, DOCS):
            found = found + (positions >= first_of[:, c].reshape(shape)).astype(jnp.int32)
        return found

    def pick(table, index):
        shape = (seqs,) + (1,) * (index.ndim - 1)
        out = jnp.zeros(index.shape, jnp.int32)
        for c in range(DOCS):
            out = jnp.where(index == c, table[:, c].reshape(shape), out)
        return out

    blocks = jnp.arange(group, dtype=jnp.int32) * ring + place[0]
    attended_pos = blocks[:, None] * rows + jnp.arange(rows, dtype=jnp.int32)[None, :]
    attended_pos = jnp.broadcast_to(attended_pos[None], (seqs, group, rows))
    start = pick(first_of, document(attended_pos))[:, :, None, :]
    chosen_doc = document(chosen_rows)
    first_slot = jnp.sum(
        (chosen_doc[:, None, :] < jnp.arange(DOCS, dtype=jnp.int32)[None, :, None]).astype(jnp.int32), axis=2
    )
    chosen_start = pick(first_slot, chosen_doc).reshape(seqs, group, ring, sel)
    routed_start = lax.dynamic_index_in_dim(chosen_start, place[0], 2, keepdims=False)
    routed_start = routed_start.reshape(seqs, 1, group * sel)

    def pack(value):
        value = value.reshape(seqs, 2, rows // 2, group, HDIM)
        return jnp.transpose(value, (0, 2, 3, 1, 4)).reshape(tokens // 2, 2 * part)

    def unpack(value):
        value = value.reshape(seqs, rows // 2, group, 2, HDIM)
        return jnp.transpose(value, (0, 3, 1, 2, 4)).reshape(tokens, part)

    value = stream_in.reshape(tokens, width).astype(F32)
    grad_top = cotangent.reshape(tokens, width)
    inv_in = inverse_rms(value)
    normed = (value * inv_in * gain_pre).astype(BF)
    qkv = matmul(normed, dense_qkv).astype(BF)
    pairs, queries = dense_to_heads(
        lines, 2, qkv[:, : 2 * part], pack(qkv[:, 2 * part :]), "dense_to_heads"
    )
    routed_rest = gather(after(routed_rest, queries))
    queries = queries.reshape(group, seqs, rows // 2, lanes)
    pairs = pairs.reshape(ring, group, seqs, rows, lanes)
    mixed, mixed_turned, lse = dense_forward(place, queries, pairs, start)
    packed = (tokens // 2, group * lanes)
    (mixed,) = swap_blocks(
        lines, 3, "z", [mixed.reshape(group, tokens // 2, lanes)], [(packed, BF)], [(0, slot, 0, columns(lanes))],
        "dense_mixed",
    )
    mixed = gather_columns(lines, 4, unpack(mixed), "dense_mixed_columns")
    attended = gather_columns(lines, 5, matmul(mixed, dense_out).astype(BF), "dense_attended")
    middle_value = value + attended.astype(F32)
    inv_mid = inverse_rms(middle_value)
    normed_mid = (middle_value * inv_mid * gain_mid).astype(BF)
    hidden_pre = matmul(normed_mid, dense_exp)
    hidden, slope = gelu_terms(hidden_pre)
    hidden, slope = hidden.astype(BF), slope.astype(BF)
    fed = scatter_columns(lines, 6, matmul(hidden, dense_shr).astype(BF), None, "dense_fed")
    after_dense = own_columns(middle_value) + fed

    def reduce_dp(value):
        return lax.psum_scatter(value, "dp", scatter_dimension=0, tiled=True)

    source = jnp.concatenate([after_dense.astype(BF), own_columns(grad_top)], axis=1)
    fed_low, grad_own, added, routed_grads = routed_layer(
        lines,
        7,
        [
            source.reshape(seqs, rows, 2 * part),
            cotangent,
            chosen_rows[:, :, None],
            chosen_rows[:, None, :],
            routed_start,
            gains[2:5],
            routed_qkv,
            routed_rest,
        ],
        (seqs, sel, rows, width, part),
        "routed_layer",
    )
    stream_out = (after_dense + added.reshape(tokens, part).astype(F32)).astype(BF).reshape(seqs, rows, part)
    routed_shard = reduce_dp(routed_grads)

    dense_grads, dense_qkv_grad, stream_grad, d_vectors = dense_return(
        lines,
        8,
        [
            fed_low.reshape(tokens, width),
            grad_own.reshape(tokens, part),
            stream_in.reshape(tokens, width),
            attended,
            slope,
            hidden,
            mixed,
            rest,
            dense_qkv,
            queries,
            pairs,
            start,
            mixed_turned,
            lse,
            gains[:2],
        ],
        (seqs, rows, width, hidden_size),
        "dense_return",
    )
    stream_grad = stream_grad.reshape(seqs, rows, part)
    dense_shard = reduce_dp(dense_grads)
    vectors, dense_all_in, (routed_all,) = dense_finish(
        lines, 9, d_vectors, dense_qkv_grad, [routed_shard], "dense_finish"
    )
    dense_all = gather_columns(lines, 10, after(dense_shard, dense_all_in), "dense_shards")

    share = hidden_size // dp
    local = width // dp
    inner_at = hidden_size + width
    r_exp, r_shr, r_keys, r_values, r_query, r_out, r_vector = assemble(
        [
            ("hidden", routed_all, 0, hidden_size),
            ("stack", routed_all, hidden_size, width),
            ("pair", routed_all, inner_at, 2 * part),
            ("columns", routed_all, inner_at + 2 * part, part),
            ("columns", routed_all, inner_at + 3 * part, part),
            ("sum", routed_all, inner_at + 4 * part, 128),
        ],
        share,
        "routed_places",
    )
    d_exp, d_shr, d_out, d_keys, d_values, d_query = assemble(
        [
            ("hidden", dense_all, 0, hidden_size),
            ("stack", dense_all, hidden_size, width),
            ("columns", dense_all, hidden_size + width, part),
            ("pair", dense_all_in, 0, 2 * part),
            ("columns", dense_all_in, 2 * part, part),
        ],
        share,
        "dense_places",
    )
    vectors = lax.dynamic_slice_in_dim(vectors, rank * local, local, 1)
    d_shr = d_shr.reshape(sections * share, width)
    r_shr = r_shr.reshape(sections * share, width)
    return (
        (stream_out, stream_grad)
        + (vectors[1], d_query, d_keys, d_values, d_out, vectors[0], d_exp, d_shr)
        + (r_vector[:, 0], r_query, r_keys, r_values, r_out, r_vector[:, 1], r_exp, r_shr)
        + (r_vector[:, 2],)
    )


def solution(mesh):
    streams, row, vector, copied = P(None, "dp", None), P("dp", None), P("dp"), P()
    layer = (vector, row, row, row, row, vector, row, row)
    outs = (P(None, "dp", "section"),) * 2 + layer + layer + (vector,)
    return jax.shard_map(
        on_device,
        mesh=mesh,
        in_specs=(streams, copied, copied, streams) + layer + layer + (vector,),
        out_specs=outs,
        check_vma=False,
    )
```

time: 614 us -> 508 us (0.83)
  local copies, waits for them, and re-layouts: 101 us -> 39.9 us
  matrix products: 42.6 us -> 9.79 us
  other arithmetic: 36.3 us -> 8.77 us
  Pallas kernels: 386 us -> 404 us
    unnamed x219 -> x71, local copies, waits for them, and re-layouts: 50.3 us -> 12.4 us
    dot_general x12 -> x0, matrix products: 35.7 us -> none  [contract(): lax.dot_general(left, right, (((ldim,), (rdim,)), ((), ())), preferred_el...]
    pallas_call x14 -> x10, Pallas kernels: 357 us -> 389 us  [communicate(): pl.pallas_call(kernel, out_shape=[jax.ShapeDtypeStruct(s, d) for s, d in...]
    concatenate x4 -> x0, other arithmetic: 17.5 us -> none  [the longest x1 11.2 us: on_device(): jnp.concatenate([outer(r_normed_mid, r_grad_pre), outer(r_hidden, r_fed_l...]
    pallas_call x1 -> x0, Pallas kernels: 12.5 us -> none  [dense_backward(): pl.pallas_call(dense_backward_kernel, grid_spec=grid, out_shape=[jax.Shap...]
    reduce_scatter x4 -> x2, waiting for transfers between devices: 21.7 us -> 22.2 us  [reduce_dp(): return lax.psum_scatter(value, 'dp', scatter_dimension=0, tiled=True)]
  transfers between devices with their start and end apart: 7 -> 5, of which waited for: 1 -> 1; matrix products, arithmetic and copies ran while one was open for 16% -> 7% of each run, Pallas kernels for 46% -> 58%
where the time goes in v4:
time: 508 us; the launch traced here: 501 us
  Pallas kernels  404 us (80%)
  local copies, waits for them, and re-layouts  39.9 us (8%)
  waiting for transfers between devices  22.3 us (4%)
  between operations  14.9 us (3%)
  matrix products  9.79 us (2%)
  other arithmetic  8.77 us (2%)
    pallas_call x10, Pallas kernels, communicate(): pl.pallas_call(kernel, out_shape=[jax.ShapeDtypeStruct(s, d) for s, d in...  389 us
    reduce_scatter x2, waiting for transfers between devices, reduce_dp(): return lax.psum_scatter(value, 'dp', scatter_dimension=0, tiled=True)  22.2 us
    unnamed x71, local copies, waits for them, and re-layouts  12.4 us
  transfers between devices with their start and end apart: 5, of which 1 were waited for; matrix products, arithmetic and copies ran while one was open for 7% of the time, Pallas kernels for 58%

profile of v4, /device:TPU:0, one launch (start us, length us, event | category | flops | bytes accessed | tf_op | source)
XLA Modules:
  0.0 500.7 jit_solution(12095005753168442034)
XLA Ops:
  7.3 1.9 reshape.319
  9.1 2.6 reshape.326
  11.7 4.3 dynamic-slice_reduce_fusion
  16.1 0.9 constant_dynamic-slice_fusion.9
  17.0 0.9 pad_maximum_fusion.1
  18.0 1.0 constant_dynamic-slice_fusion.12
  19.0 0.9 constant_dynamic-slice_fusion.10
  20.2 0.9 constant_dynamic-slice_fusion.4
  21.4 0.8 copy.96
  22.2 45.8 %first_weights.1 = (bf16[8,128,768]{2,1,0:T(8,128)(2,1)S(1)}, bf16[8,16,128]{2,1,0:T(8,128)(2,1)S(1)}) custom-call(bf16[128,768]{1,0:T(8,128)(2,1)S(1)} %pad_maximum_fusion.3.refs_0_, bf16[16,128]{1,0:T(8,128)(2,1)S(1)} %pad.4.refs_1_), custom_call_target="tpu_custom_call" | custom-call | tf_op jit(solution)/shard_map/first_weights/pallas_call | solution.py:101
  68.0 1.1 constant_dynamic-slice_fusion.2
  69.1 1.6 pad_maximum_fusion.4
  70.8 0.4 fusion
  71.2 0.6 fusion.23
  71.8 0.4 fusion.2
  72.2 1.4 convolution_convert_fusion
  74.1 0.9 copy.99
  75.0 0.5 reshape.336.q_ref
  75.4 31.7 %dense_to_heads.1 = (bf16[2,4,768,128]{3,2,1,0:T(8,128)(2,1)S(1)}, bf16[4,384,128]{2,1,0:T(8,128)(2,1)S(1)}) custom-call(bf16[768,512]{1,0:T(8,128)(2,1)S(1)} %slice.145.p_ref, bf16[384,512]{1,0:T(8,128)(2,1)S(1)} %reshape.336.q_ref), custom_call_target="tpu_custom_call" | custom-call | tf_op jit(solution)/shard_map/dense_to_heads/pallas_call | solution.py:101
  107.2 1.2 constant_dynamic-slice_fusion.1
  108.3 0.9 pad_maximum_fusion.2
  109.3 0.3 reduce-scatter.3.cloned.1.call-start
  109.5 0.6 broadcast_in_dim.115.row_ref
  110.3 0.3 slice_reduce_fusion.18
  110.8 0.3 slice_reduce_fusion.10
  111.3 0.7 reshape.324.start_ref
  112.0 0.9 copy.98.column_ref
  113.2 9.2 %dense_attention.1 = (bf16[4,3,128,128]{3,2,1,0:T(8,128)(2,1)S(1)}, bf16[3,4,64,256]{3,2,1,0:T(8,128)(2,1)S(1)}, f32[3,4,1,256]{3,2,1,0:T(1,128)S(1)}) custom-call(s32[1]{0:T(128)} %bitcast.1.place_ref, bf16[4,3,128,128]{3,2,1,0:T(8,128)(2,1)S(1)} %bitcast.72, bf16[2,4,3,256,128]{4,3,2,1,0:T(8,128)(2,1)S(1)} %bitcast.67, ...), custom_call_target="tpu_custom_call" | custom-call | tf_op jit(solution)/shard_map/dense_attention/pallas_call | solution.py:661
  122.5 0.7 copy-done.12
  123.2 0.6 copy-done.14
  123.8 11.9 %dense_mixed.1 = bf16[384,512]{1,0:T(8,128)(2,1)S(1)} custom-call(bf16[4,384,128]{2,1,0:T(8,128)(2,1)S(1)} %bitcast.74), custom_call_target="tpu_custom_call" | custom-call | tf_op jit(solution)/shard_map/dense_mixed/pallas_call | solution.py:101
  135.7 0.2 copy.88
  136.1 0.7 copy.100
  136.7 0.5 reshape.337.x_ref
  137.2 16.5 %dense_mixed_columns.1.mixed_ref = bf16[768,1024]{1,0:T(8,128)(2,1)S(1)} custom-call(bf16[768,256]{1,0:T(8,128)(2,1)S(1)} %reshape.337.x_ref), custom_call_target="tpu_custom_call" | custom-call | tf_op jit(solution)/shard_map/dense_mixed_columns/pallas_call | solution.py:101
  153.7 1.3 constant_dynamic-slice_fusion.7
  155.1 1.4 slice_bitcast_fusion.gains_ref
  156.4 1.7 convolution_convert_fusion.1.x_ref
  158.2 15.7 %dense_attended.1.attended_ref = bf16[768,1024]{1,0:T(8,128)(2,1)S(1)} custom-call(bf16[768,256]{1,0:T(8,128)(2,1)S(1)} %convolution_convert_fusion.1.x_ref), custom_call_target="tpu_custom_call" | custom-call | tf_op jit(solution)/shard_map/dense_attended/pallas_call | solution.py:101
  174.0 0.6 multiply_reduce_fusion
  174.6 0.5 copy-done.2
  175.1 2.9 copy-done.19
  178.0 4.9 add_convert_fusion
  182.9 1.8 fusion.9.refs_0_
  184.7 14.4 %dense_fed.1 = f32[768,256]{1,0:T(8,128)S(1)} custom-call(bf16[768,1024]{1,0:T(8,128)(2,1)S(1)} %fusion.9.refs_0_), custom_call_target="tpu_custom_call" | custom-call | tf_op jit(solution)/shard_map/dense_fed/pallas_call | solution.py:101
  199.3 1.0 pad_maximum_fusion
  200.3 86.1 %routed_layer.1 = (bf16[3,256,1024]{2,1,0:T(8,128)(2,1)}, f32[3,256,256]{2,1,0:T(8,128)}, bf16[3,256,256]{2,1,0:T(8,128)(2,1)}, bf16[1024,3200]{1,0:T(8,128)(2,1)}) custom-call(bf16[3,256,512]{2,1,0:T(8,128)(2,1)} %bitcast.76, bf16[3,256,1024]{2,1,0:T(8,128)(2,1)} %top_ref.1, s32[3,256,1]{2,1,0:T(8,128)} %copy.98.column_ref, ...), custom_call_target="tpu_custom_call" | custom-call | tf_op jit(solution)/shard_map/routed_layer/pallas_call | solution.py:101
  286.5 0.2 reduce-scatter.5.cloned.1.call-start
  286.7 1.4 slice_bitcast_fusion.1.gains_ref
  288.0 104.0 %dense_return.1 = (bf16[1024,2304]{1,0:T(8,128)(2,1)}, bf16[1024,768]{1,0:T(8,128)(2,1)}, bf16[768,256]{1,0:T(8,128)(2,1)}, f32[8,256]{1,0:T(8,128)}) custom-call(bf16[768,1024]{1,0:T(8,128)(2,1)} %bitcast.79, f32[768,256]{1,0:T(8,128)} %bitcast.86, bf16[768,1024]{1,0:T(8,128)(2,1)} %bitcast.75, bf16[768,1024]{1,0:T(8,128)(2,1)} %copy-done.2, ...), custom_call_target="tpu_custom_call" | custom-call | tf_op jit(solution)/shard_map/dense_return/pallas_call | solution.py:101
  392.1 0.9 copy-done.21
  393.1 2.0 fusion.14
  395.1 1.4 copy-done.8
  396.5 1.1 copy-done.10
  397.7 40.5 %dense_finish.1 = (f32[8,1024]{1,0:T(8,128)S(1)}, bf16[128,3072]{1,0:T(8,128)(2,1)S(1)}, bf16[128,12800]{1,0:T(8,128)(2,1)S(1)}) custom-call(f32[8,256]{1,0:T(8,128)S(1)} %copy-done.15, bf16[8,128,768]{2,1,0:T(8,128)(2,1)S(1)} %bitcast.71, bf16[128,3200]{1,0:T(8,128)(2,1)S(1)} %copy-done.10), custom_call_target="tpu_custom_call" | custom-call | tf_op jit(solution)/shard_map/dense_finish/pallas_call | solution.py:101
  438.2 1.7 copy-done.5
  439.9 0.5 slice_bitcast_fusion.2
  440.4 22.2 %reduce-scatter.5.cloned.1.call-done.x_ref = bf16[128,2304]{1,0:T(8,128)(2,1)} async-done(((bf16[1024,2304]{1,0:T(8,128)(2,1)}), bf16[128,2304]{1,0:T(8,128)(2,1)}) %reduce-scatter.5.cloned.1.call-update) | async-done | bytes 589840 | tf_op jit(solution)/shard_map/reduce_scatter | solution.py:1553
  462.6 1.1 copy-done.11
  463.7 22.6 %dense_shards.1.refs_0_ = bf16[128,9216]{1,0:T(8,128)(2,1)S(1)} custom-call(bf16[128,2304]{1,0:T(8,128)(2,1)S(1)} %copy-done.11), custom_call_target="tpu_custom_call" | custom-call | tf_op jit(solution)/shard_map/dense_shards/pallas_call | solution.py:101
  486.2 3.0 dense_places.1
  489.3 3.0 routed_places.1
  492.3 0.7 slice_reduce_fusion
  493.0 0.7 copy.117
  (101 shorter events, 2.6 us)
Async XLA Ops:
  7.2 9.7 %copy-start = (bf16[512,1024]{1,0:T(8,128)(2,1)S(1)}, bf16[512,1024]{1,0:T(8,128)(2,1)}, u32[]{:S(2)}) copy-start(bf16[512,1024]{1,0:T(8,128)(2,1)} %param.32) | copy-start | bytes 3145732
  7.2 149.2 %all-gather.4.cloned.1.call-start = ((), (), s32[]{:S(2)}) async-start(), calls=%async_computation.2 | async-start | bytes 5308416 | tf_op jit(solution)/shard_map/all_gather | solution.py:1469
  17.0 5.2 %copy-start.27 = (bf16[128]{0:T(256)(128)(2,1)S(1)}, bf16[128]{0:T(256)(128)(2,1)}, u32[]{:S(2)}) copy-start(bf16[128]{0:T(256)(128)(2,1)} %param.25) | copy-start | bytes 772
  17.0 5.2 %copy-start.28 = (bf16[128]{0:T(256)(128)(2,1)S(1)}, bf16[128]{0:T(256)(128)(2,1)}, u32[]{:S(2)}) copy-start(bf16[128]{0:T(256)(128)(2,1)} %param.30) | copy-start | bytes 772
  17.0 5.2 %copy-start.29 = (bf16[128]{0:T(256)(128)(2,1)S(1)}, bf16[128]{0:T(256)(128)(2,1)}, u32[]{:S(2)}) copy-start(bf16[128]{0:T(256)(128)(2,1)} %param.33) | copy-start | bytes 772
  17.0 5.2 %copy-start.30 = (bf16[128]{0:T(256)(128)(2,1)S(1)}, bf16[128]{0:T(256)(128)(2,1)}, u32[]{:S(2)}) copy-start(bf16[128]{0:T(256)(128)(2,1)} %param.38) | copy-start | bytes 772
  17.0 5.2 %copy-start.31 = (bf16[128]{0:T(256)(128)(2,1)S(1)}, bf16[128]{0:T(256)(128)(2,1)}, u32[]{:S(2)}) copy-start(bf16[128]{0:T(256)(128)(2,1)} %param.41) | copy-start | bytes 772
  17.9 52.9 %copy-start.16 = (bf16[3,256,1024]{2,1,0:T(8,128)(2,1)S(1)}, bf16[3,256,1024]{2,1,0:T(8,128)(2,1)}, u32[]{:S(2)}) copy-start(bf16[3,256,1024]{2,1,0:T(8,128)(2,1)} %param.21) | copy-start | bytes 4718596
  17.9 182.4 %all-gather.6.cloned.1.call-start = ((), (), s32[]{:S(2)}) async-start(), calls=%async_computation.3 | async-start | bytes 1769472 | tf_op jit(solution)/shard_map/all_gather | solution.py:1469
  68.0 4.2 copy-start.7
  70.7 129.6 %all-gather.8.cloned.1.call-start = ((), (), s32[]{:S(2)}) async-start(), calls=%async_computation.4 | async-start | bytes 5308416 | tf_op jit(solution)/shard_map/all_gather | solution.py:1469
  71.2 0.6 copy-start.23
  75.0 34.6 %copy-start.24 = (s32[3,256]{1,0:T(4,128)S(1)}, s32[3,256]{1,0:T(4,128)}, u32[]{:S(2)}) copy-start(s32[3,256]{1,0:T(4,128)} %param.23) | copy-start | bytes 9220
  75.0 35.2 %copy-start.25 = (s32[3,2048]{1,0:T(4,128)S(1)}, s32[3,2048]{1,0:T(4,128)}, u32[]{:S(2)}) copy-start(s32[3,2048]{1,0:T(4,128)} %param.22) | copy-start | bytes 73732
  107.1 15.3 %copy-start.3 = (bf16[2,4,768,128]{3,2,1,0:T(8,128)(2,1)}, bf16[2,4,768,128]{3,2,1,0:T(8,128)(2,1)S(1)}, u32[]{:S(2)}) copy-start(bf16[2,4,768,128]{3,2,1,0:T(8,128)(2,1)S(1)} %get-tuple-element.56) | copy-start | bytes 4718596
  107.1 15.3 %copy-start.9 = (bf16[4,384,128]{2,1,0:T(8,128)(2,1)}, bf16[4,384,128]{2,1,0:T(8,128)(2,1)S(1)}, u32[]{:S(2)}) copy-start(bf16[4,384,128]{2,1,0:T(8,128)(2,1)S(1)} %get-tuple-element.55) | copy-start | bytes 1179652
  109.3 285.8 %reduce-scatter.3.cloned.1.call-start = ((), (), s32[]{:S(2)}) async-start(), calls=%async_computation.5 | async-start | bytes 7372800 | tf_op jit(solution)/shard_map/reduce_scatter | solution.py:1553
  113.2 22.8 %copy-start.13 = (s32[3,4,1,256]{3,2,1,0:T(1,128)}, s32[3,4,1,256]{3,2,1,0:T(1,128)S(1)}, u32[]{:S(2)}) copy-start(s32[3,4,1,256]{3,2,1,0:T(1,128)S(1)} %compare_select_fusion.7.start_ref) | copy-start | bytes 36868
  122.5 0.7 copy-start.12
  123.2 0.6 copy-start.14
  153.7 2.7 copy-start.4
  156.4 17.5 %copy-start.17 = (bf16[3,256,1024]{2,1,0:T(8,128)(2,1)S(1)}, bf16[3,256,1024]{2,1,0:T(8,128)(2,1)}, u32[]{:S(2)}) copy-start(bf16[3,256,1024]{2,1,0:T(8,128)(2,1)} %param.21) | copy-start | bytes 4718596
  173.9 1.1 copy-start.2
  173.9 4.0 copy-start.19
  174.0 4.0 copy-start.26
  175.1 24.0 %copy-start.18 = (f32[768,1024]{1,0:T(8,128)}, f32[768,1024]{1,0:T(8,128)S(1)}, u32[]{:S(2)}) copy-start(f32[768,1024]{1,0:T(8,128)S(1)} %get-tuple-element.109) | copy-start | bytes 9437188
  182.9 1.8 copy-start.20
  286.5 176.1 %reduce-scatter.5.cloned.1.call-start = ((), (), s32[]{:S(2)}) async-start(), calls=%async_computation.6 | async-start | bytes 5308416 | tf_op jit(solution)/shard_map/reduce_scatter | solution.py:1553
  392.1 1.0 copy-start.21
  392.1 3.0 copy-start.15
  395.1 1.4 copy-start.8
  396.5 1.1 copy-start.10
  438.2 1.7 copy-start.5
  462.6 1.1 copy-start.11
  463.7 25.6 %copy-start.6 = (bf16[128,12800]{1,0:T(8,128)(2,1)S(1)}, bf16[128,12800]{1,0:T(8,128)(2,1)}, u32[]{:S(2)}) copy-start(bf16[128,12800]{1,0:T(8,128)(2,1)} %copy-done.5) | copy-start | bytes 9830404
  489.3 3.8 copy-start.22
  489.3 4.5 copy-start.1
Sparse Core Ops, SparseCore 0:
  18.0 83.7 all-gather.3
  104.0 25.7 all-gather.5
  131.4 51.1 all-gather.7
  286.6 96.9 reduce-scatter.2
  392.2 70.3 reduce-scatter.4
